TPU v7x, 256 devices: a whole 4x4x8 slice. The times are simulated.
256 devices in a mesh: px: 16 (over y, x), py: 16 (over z, core).
Axes of the slice: x: 4, y: 4, z: 8, core: 2. Of those that a mesh axis runs over, the one named last changes fastest.
Arguments:
- body_force: float32 [16, 16, 3, 4096], P('px', 'py'), may hold values from -6 to 6
- fault_slip: float32 [16, 16, 3, 512], P('px', 'py'), may hold values from -6 to 6
- elem_nodes: int32 [16, 16, 27, 512], P('px', 'py'), may hold values from 0 to 5119
- moduli: float32 [16, 16, 2, 512], P('px', 'py'), may hold values from 0.5 to 5
- stiff_ref: float32 [2, 81, 81], replicated
- block_inv: float32 [16, 16, 9, 4096], P('px', 'py')
- send_nodes: int32 [16, 16, 4, 256], P('px', 'py'), may hold values from 0 to 4095
- fault_nodes: int32 [16, 16, 2, 512], P('px', 'py'), may hold values from 0 to 4095
Outputs:
- displacement: float32 [16, 16, 3, 4096], P('px', 'py')
- multiplier: float32 [16, 16, 3, 512], P('px', 'py')
Inputs may be any that keep to these rules, and one draw needn't show every extreme that they name: `elem_nodes`: slots below 4096 are owned nodes; slot 4096 + k * 256 + i is entry i of ghost block k (k = 0 .. 3 from px-1, px+1, py-1, py+1). `send_nodes`: owned node numbers; entries may repeat. `fault_nodes`: owned node numbers; entries may repeat.
All inputs are finite; a program needn't handle non-finite values.
Results may differ from a plain program's by a relative error of at most 0.00018.
Values sent between devices are 32-bit elements; how exact they have to be, the bound alone decides.
No kernel may reach another device: no remote copies, remote signals or barrier semaphores. Data moves between devices by JAX's collectives and lax.ppermute only.
A program may use at most 64 MiB of HBM per device.

v0:
```python
import jax
import jax.numpy as jnp
from jax import lax
from jax.sharding import PartitionSpec as P

ITERS = 3


highest = lax.Precision.HIGHEST


def extended_2(block, sides, width):
    for axis, dim in sides:
        count = lax.axis_size(axis)
        forward = [(i, i + 1) for i in range(count - 1)]
        backward = [(target, source) for source, target in forward]
        low = lax.ppermute(
            lax.slice_in_dim(block, block.shape[dim] - width, None, axis=dim), axis, forward
        )
        high = lax.ppermute(lax.slice_in_dim(block, 0, width, axis=dim), axis, backward)
        block = jnp.concatenate([low, block, high], axis=dim)
    return block


def partner(shard, axis, apart):
    return lax.ppermute(shard, axis, [(i, i ^ 1 << apart) for i in range(lax.axis_size(axis))])


def precondition(block_inv, field):
    blocks = block_inv.reshape((3, 3, block_inv.shape[-1]))
    return jnp.sum(blocks * field[None, :, :], axis=1)


def across_strike(payload):
    widened = extended_2(payload, (("px", 0),), 1)
    return (widened[0], widened[3])


def across_dip(payload):
    widened = extended_2(payload, (("py", 0),), 1)
    return (widened[0], widened[3])


def element_apply(extended, nodes, moduli, stiff_ref):
    count = nodes.shape[1]
    local = extended[:, nodes].reshape(81, count)
    first = jnp.dot(stiff_ref[0], local, precision=highest)
    second = jnp.dot(stiff_ref[1], local, precision=highest)
    result = moduli[0] * first + moduli[1] * second
    return jnp.zeros(extended.shape, jnp.float32).at[:, nodes].add(result.reshape(3, 27, count))


def operator(disp, mult, elem_nodes, moduli, stiff_ref, send_nodes, fault_nodes):
    owned_count = disp.shape[-1]
    width = send_nodes.shape[-1]
    boundary = disp[:, send_nodes]
    own_ids = fault_nodes[0]
    peer_ids = fault_nodes[1]
    peer_disp = disp[:, peer_ids]
    lower_x, upper_x = across_strike(jnp.stack([boundary[:, 0], boundary[:, 1]]))
    swapped = partner(jnp.stack([peer_disp, mult]), "px", 0)
    facing_disp = swapped[0]
    facing_mult = swapped[1]
    lower_y, upper_y = across_dip(jnp.stack([boundary[:, 2], boundary[:, 3]]))
    extended = jnp.concatenate([disp, lower_x, upper_x, lower_y, upper_y], axis=-1)
    applied = element_apply(extended, elem_nodes, moduli, stiff_ref)
    owned = applied[:, :owned_count]
    ghost_blocks = [
        applied[:, owned_count + side * width : owned_count + (side + 1) * width]
        for side in range(4)
    ]
    back_low_x, back_up_x = across_strike(jnp.stack([ghost_blocks[0], ghost_blocks[1]]))
    back_low_y, back_up_y = across_dip(jnp.stack([ghost_blocks[2], ghost_blocks[3]]))
    owned = owned.at[:, send_nodes[0]].add(back_low_x)
    owned = owned.at[:, send_nodes[1]].add(back_up_x)
    owned = owned.at[:, send_nodes[2]].add(back_low_y)
    owned = owned.at[:, send_nodes[3]].add(back_up_y)
    owned = owned.at[:, own_ids].add(mult)
    owned = owned.at[:, peer_ids].add(-facing_mult)
    jump = disp[:, own_ids] - facing_disp
    return (owned, jump)


def local_inner(first, second):
    return jnp.sum(first[0] * second[0]) + jnp.sum(first[1] * second[1])


def least_squares(columns, beta):
    cosines, sines, upper = ([], [], [])
    target = [beta] + [jnp.zeros_like(beta) for later in columns]
    for position, column in enumerate(columns):
        column = list(column)
        for earlier in range(position):
            top = cosines[earlier] * column[earlier] + sines[earlier] * column[earlier + 1]
            below = -sines[earlier] * column[earlier] + cosines[earlier] * column[earlier + 1]
            column[earlier] = top
            column[earlier + 1] = below
        pivot = column[position]
        under = column[position + 1]
        radius = jnp.sqrt(pivot * pivot + under * under)
        cosine = pivot / radius
        sine = under / radius
        column[position] = radius
        cosines.append(cosine)
        sines.append(sine)
        target[position + 1] = -sine * target[position]
        target[position] = cosine * target[position]
        upper.append(column)
    count = len(columns)
    coeffs = [None] * count
    for row_index in reversed(range(count)):
        total = target[row_index]
        for later in range(row_index + 1, count):
            total = total - upper[later][row_index] * coeffs[later]
        coeffs[row_index] = total / upper[row_index][row_index]
    return coeffs


def body(body_force, fault_slip, elem_nodes, moduli, stiff_ref, block_inv, send_nodes, fault_nodes):
    load = body_force[0, 0]
    slip = fault_slip[0, 0]
    nodes = elem_nodes[0, 0]
    lame = moduli[0, 0]
    inverse = block_inv[0, 0]
    sends = send_nodes[0, 0]
    faults = fault_nodes[0, 0]
    rhs = (load, slip)
    beta = jnp.sqrt(lax.psum(local_inner(rhs, rhs), ("px", "py")))
    basis = [(load / beta, slip / beta)]
    columns = []
    for position in range(ITERS):
        current = basis[-1]
        image = operator(
            precondition(inverse, current[0]), current[1], nodes, lame, stiff_ref, sends, faults
        )
        column = []
        for vector in basis:
            entry = lax.psum(local_inner(image, vector), ("px", "py"))
            image = (image[0] - entry * vector[0], image[1] - entry * vector[1])
            column.append(entry)
        norm = jnp.sqrt(lax.psum(local_inner(image, image), ("px", "py")))
        column.append(norm)
        columns.append(column)
        basis.append((image[0] / norm, image[1] / norm))
    coeffs = least_squares(columns, beta)
    combo_disp = sum((coeffs[index_pos] * basis[index_pos][0] for index_pos in range(ITERS)))
    combo_mult = sum((coeffs[index_pos] * basis[index_pos][1] for index_pos in range(ITERS)))
    displacement = precondition(inverse, combo_disp)
    return (displacement[None, None], combo_mult[None, None])


def solution(mesh):
    in_specs = (
        P("px", "py", None, None),
        P("px", "py", None, None),
        P("px", "py", None, None),
        P("px", "py", None, None),
        P(),
        P("px", "py", None, None),
        P("px", "py", None, None),
        P("px", "py", None, None),
    )
    out_specs = (P("px", "py", None, None), P("px", "py", None, None))
    return jax.shard_map(body, mesh=mesh, in_specs=in_specs, out_specs=out_specs, check_vma=False)
```

profile of v0, /device:TPU:1, one launch (start us, length us, event | category | flops | bytes accessed | tf_op | source)
XLA Modules:
  0.0 1366.6 jit_solution(5779158047997547238)
XLA Ops:
  4.7 81.4 %psum.70 = f32[]{:T(128)} all-reduce(f32[]{:T(128)S(6)} %add.257), channel_id=1, replica_groups=mesh['px'=16,'py'=16] {'px','py'}, use_global_device_ids=true, to_apply=%region_2.0 | all-reduce | flops 1 | bytes 8 | tf_op jit(solution)/shard_map/psum | solution.py:128
  100.4 4.0 collective-permute-start
  107.1 26.1 %gather_fusion.1 = f32[13824,3]{1,0:T(8,128)} fusion(f32[3,5120]{0,1:T(8,128)S(1)} %copy.107, s32[14336]{0:T(1024)S(1)} %pad_clamp_fusion), kind=kCustom, calls=%fused_computation.1 | custom fusion | bytes 387072 | tf_op jit(solution)/shard_map/gather | solution.py:46
  133.2 5.0 copy.108
  138.9 4.1 copy.111
  143.0 74.7 %scatter_custom_fusion = f32[3,5120]{0,1:T(8,128)S(1)} fusion(s32[13824]{0:T(1024)S(1)} %reshape.456, f32[13824,3]{1,0:T(8,128)} %bitcast.369, f32[]{:T(128)} %constant.4.clone.1), kind=kCustom, calls=%fused_computation.37 | custom fusion | flops 41472 | bytes 61952 | tf_op jit(solution)/shard_map/scatter-add | solution.py:50
  225.4 4.6 collective-permute-start.4
  236.1 5.1 scatter_custom_fusion.1
  241.2 5.1 scatter_custom_fusion.2
  246.2 5.2 scatter_custom_fusion.3
  251.5 4.7 scatter_custom_fusion.4
  256.2 5.9 scatter_fusion
  262.3 5.9 scatter_fusion.1
  273.0 77.9 %psum.71 = f32[]{:T(128)} all-reduce(f32[]{:T(128)S(6)} %add.267), channel_id=1, replica_groups=mesh['px'=16,'py'=16] {'px','py'}, use_global_device_ids=true, to_apply=%region_13.0 | all-reduce | flops 1 | bytes 8 | tf_op jit(solution)/shard_map/psum | solution.py:138
  354.7 73.2 %psum.72 = f32[]{:T(128)} all-reduce(f32[]{:T(128)S(6)} %add.268), channel_id=1, replica_groups=mesh['px'=16,'py'=16] {'px','py'}, use_global_device_ids=true, to_apply=%region_16.0 | all-reduce | flops 1 | bytes 8 | tf_op jit(solution)/shard_map/psum | solution.py:141
  436.9 3.6 collective-permute-start.11
  441.8 4.0 collective-permute-start.9
  448.3 26.1 %gather_fusion.5 = f32[13824,3]{1,0:T(8,128)} fusion(f32[3,5120]{0,1:T(8,128)S(1)} %copy.123, s32[14336]{0:T(1024)S(1)} %pad_clamp_fusion), kind=kCustom, calls=%fused_computation.5 | custom fusion | bytes 387072 | tf_op jit(solution)/shard_map/gather | solution.py:46
  474.4 5.0 copy.124
  480.2 4.1 copy.125
  484.3 74.7 %scatter_custom_fusion.7 = f32[3,5120]{0,1:T(8,128)S(1)} fusion(s32[13824]{0:T(1024)} %copy-done.5, f32[13824,3]{1,0:T(8,128)} %bitcast.370, f32[]{:T(128)} %constant.4.clone.1), kind=kCustom, calls=%fused_computation.35 | custom fusion | flops 41472 | bytes 61952 | tf_op jit(solution)/shard_map/scatter-add | solution.py:50
  561.8 3.6 collective-permute-start.15
  566.7 4.6 collective-permute-start.13
  579.3 5.1 scatter_custom_fusion.8
  584.4 5.1 scatter_custom_fusion.9
  589.5 5.1 scatter_custom_fusion.10
  594.5 5.1 scatter_custom_fusion.11
  599.6 6.3 scatter_fusion.2
  606.1 5.9 scatter_fusion.3
  616.9 78.4 %psum.73 = f32[]{:T(128)} all-reduce(f32[]{:T(128)S(6)} %add.272), channel_id=1, replica_groups=mesh['px'=16,'py'=16] {'px','py'}, use_global_device_ids=true, to_apply=%region_27.0 | all-reduce | flops 1 | bytes 8 | tf_op jit(solution)/shard_map/psum | solution.py:138
  699.2 73.5 %psum.74 = f32[]{:T(128)} all-reduce(f32[]{:T(128)S(6)} %add.273), channel_id=1, replica_groups=mesh['px'=16,'py'=16] {'px','py'}, use_global_device_ids=true, to_apply=%region_30.0 | all-reduce | flops 1 | bytes 8 | tf_op jit(solution)/shard_map/psum | solution.py:138
  777.2 74.2 %psum.75 = f32[]{:T(128)} all-reduce(f32[]{:T(128)S(6)} %add.276), channel_id=1, replica_groups=mesh['px'=16,'py'=16] {'px','py'}, use_global_device_ids=true, to_apply=%region_33.0 | all-reduce | flops 1 | bytes 8 | tf_op jit(solution)/shard_map/psum | solution.py:141
  865.1 4.0 collective-permute-start.18
  874.5 26.1 %gather_fusion.9 = f32[13824,3]{1,0:T(8,128)} fusion(f32[3,5120]{0,1:T(8,128)S(1)} %copy.136, s32[14336]{0:T(1024)S(1)} %pad_clamp_fusion), kind=kCustom, calls=%fused_computation.9 | custom fusion | bytes 387072 | tf_op jit(solution)/shard_map/gather | solution.py:46
  900.6 5.0 copy.137
  906.3 4.1 copy.138
  910.4 74.7 %scatter_custom_fusion.14 = f32[3,5120]{0,1:T(8,128)S(1)} fusion(s32[13824]{0:T(1024)} %copy-done.5, f32[13824,3]{1,0:T(8,128)} %bitcast.368, f32[]{:T(128)} %constant.4.clone.1), kind=kCustom, calls=%fused_computation.33 | custom fusion | flops 41472 | bytes 61952 | tf_op jit(solution)/shard_map/scatter-add | solution.py:50
  992.8 4.8 collective-permute-start.22
  1007.0 5.1 scatter_custom_fusion.15
  1012.1 5.1 scatter_custom_fusion.16
  1017.2 5.1 scatter_custom_fusion.17
  1022.2 4.8 scatter_custom_fusion.18
  1027.1 5.9 scatter_fusion.4
  1033.9 5.9 scatter_fusion.5
  1045.3 78.1 %psum.76 = f32[]{:T(128)} all-reduce(f32[]{:T(128)S(6)} %add.280), channel_id=1, replica_groups=mesh['px'=16,'py'=16] {'px','py'}, use_global_device_ids=true, to_apply=%region_44.0 | all-reduce | flops 1 | bytes 8 | tf_op jit(solution)/shard_map/psum | solution.py:138
  1129.2 73.5 %psum.77 = f32[]{:T(128)} all-reduce(f32[]{:T(128)S(6)} %add.281), channel_id=1, replica_groups=mesh['px'=16,'py'=16] {'px','py'}, use_global_device_ids=true, to_apply=%region_47.0 | all-reduce | flops 1 | bytes 8 | tf_op jit(solution)/shard_map/psum | solution.py:138
  1208.6 74.2 %psum.78 = f32[]{:T(128)} all-reduce(f32[]{:T(128)S(6)} %add.283), channel_id=1, replica_groups=mesh['px'=16,'py'=16] {'px','py'}, use_global_device_ids=true, to_apply=%region_50.0 | all-reduce | flops 1 | bytes 8 | tf_op jit(solution)/shard_map/psum | solution.py:138
  1288.7 73.3 %psum.79 = f32[]{:T(128)} all-reduce(f32[]{:T(128)S(6)} %add.286), channel_id=1, replica_groups=mesh['px'=16,'py'=16] {'px','py'}, use_global_device_ids=true, to_apply=%region_53.0 | all-reduce | flops 1 | bytes 8 | tf_op jit(solution)/shard_map/psum | solution.py:141
  (242 shorter events, 123.0 us)
Async XLA Ops:
  87.5 16.9 %copy-start.4 = (f32[1,1,3,512]{3,1,2,0:T(1,128)S(1)}, f32[1,1,3,512]{3,1,2,0:T(1,128)}, u32[]{:S(2)}) copy-start(f32[1,1,3,512]{3,1,2,0:T(1,128)} %param.9) | copy-start | bytes 18436
  87.5 343.6 %copy-start.10 = (s32[1024]{0:T(1024)}, s32[1024]{0:T(1024)S(1)}, u32[]{:S(2)}) copy-start(s32[1024]{0:T(1024)S(1)} %broadcast_clamp_fusion) | copy-start | bytes 12292
  87.5 16.9 %copy-start.30 = (s32[1,1,2,512]{3,2,1,0:T(2,128)S(1)}, s32[1,1,2,512]{3,2,1,0:T(2,128)}, u32[]{:S(2)}) copy-start(s32[1,1,2,512]{3,2,1,0:T(2,128)} %param.15) | copy-start | bytes 12292
  93.6 12.7 collective-permute-start.3
  96.4 9.8 collective-permute-start.2
  99.1 7.1 collective-permute-start.1
  100.4 5.8 collective-permute-start
  104.5 151.7 %copy-start.15 = (s32[512,1]{0,1:T(1,128)}, s32[512,1]{0,1:T(1,128)S(1)}, u32[]{:S(2)}) copy-start(s32[512,1]{0,1:T(1,128)S(1)} %get-tuple-element.51) | copy-start | bytes 6148
  104.5 157.8 %copy-start.12 = (s32[512,1]{0,1:T(1,128)}, s32[512,1]{0,1:T(1,128)S(1)}, u32[]{:S(2)}) copy-start(s32[512,1]{0,1:T(1,128)S(1)} %get-tuple-element.50) | copy-start | bytes 6148
  104.5 125.8 %copy-start.24 = (s32[1024]{0:T(1024)}, s32[1024]{0:T(1024)S(1)}, u32[]{:S(2)}) copy-start(s32[1024]{0:T(1024)S(1)} %get-tuple-element.58) | copy-start | bytes 12292
  104.5 325.6 %copy-start.27 = (s32[1024]{0:T(1024)}, s32[1024]{0:T(1024)S(1)}, u32[]{:S(2)}) copy-start(s32[1024]{0:T(1024)S(1)} %get-tuple-element.59) | copy-start | bytes 12292
  105.7 156.4 %collective-permute-start.8 = (f32[2,3,512]{2,1,0:T(4,128)S(1)}, f32[2,3,512]{2,1,0:T(4,128)S(1)}, u32[]{:S(2)}, u32[]{:S(2)}) collective-permute-start(f32[2,3,512]{2,1,0:T(4,128)S(1)} %pad_maximum_fusion), channel_id=1, source_target_pairs={{0,16},{16,0},{32,48},{48,32},{64,80},{80,64},{96,112},{112,96},{1... | collective-permute-start | bytes 36872 | tf_op jit(solution)/shard_map/ppermute | solution.py:26
  106.0 37.0 %copy-start.5 = (s32[13824]{0:T(1024)}, s32[13824]{0:T(1024)S(1)}, u32[]{:S(2)}) copy-start(s32[13824]{0:T(1024)S(1)} %reshape.456) | copy-start | bytes 165892
  106.2 32.0 %copy-start.21 = (f32[1,1,1,512]{3,2,1,0:T(1,128)}, f32[1,1,1,512]{3,2,1,0:T(1,128)S(1)}, u32[]{:S(2)}) copy-start(f32[1,1,1,512]{3,2,1,0:T(1,128)S(1)} %get-tuple-element.57) | copy-start | bytes 6148
  106.2 32.3 %copy-start.18 = (f32[1,1,1,512]{3,2,1,0:T(1,128)}, f32[1,1,1,512]{3,2,1,0:T(1,128)S(1)}, u32[]{:S(2)}) copy-start(f32[1,1,1,512]{3,2,1,0:T(1,128)S(1)} %get-tuple-element.56) | copy-start | bytes 6148
  143.0 87.1 %copy-start.29 = (s32[1,1,4,256]{3,2,1,0:T(4,128)S(1)}, s32[1,1,4,256]{3,2,1,0:T(4,128)}, u32[]{:S(2)}) copy-start(s32[1,1,4,256]{3,2,1,0:T(4,128)} %param.14) | copy-start | bytes 12292
  218.6 32.9 %collective-permute-start.7 = (f32[1,3,256]{1,2,0:T(8,128)}, f32[1,3,256]{1,2,0:T(8,128)S(1)}, u32[]{:S(2)}, u32[]{:S(2)}) collective-permute-start(f32[1,3,256]{1,2,0:T(8,128)} %get-tuple-element.30), channel_id=1, source_target_pairs={{1,0},{2,1},{3,2},{4,3},{5,4},{6,5},{7,6},{8,7},{9,8},{10,9},{11,1... | collective-permute-start | bytes 9224 | tf_op jit(solution)/shard_map/ppermute | solution.py:20
  220.7 25.5 %collective-permute-start.6 = (f32[1,3,256]{1,2,0:T(8,128)}, f32[1,3,256]{1,2,0:T(8,128)}, u32[]{:S(2)}, u32[]{:S(2)}) collective-permute-start(f32[1,3,256]{1,2,0:T(8,128)} %get-tuple-element.31), channel_id=1, source_target_pairs={{0,1},{1,2},{2,3},{3,4},{4,5},{5,6},{6,7},{7,8},{8,9},{9,10},{10,1... | collective-permute-start | bytes 9224 | tf_op jit(solution)/shard_map/ppermute | solution.py:17
  224.1 17.0 %collective-permute-start.5 = (f32[1,3,256]{1,2,0:T(8,128)}, f32[1,3,256]{1,2,0:T(8,128)}, u32[]{:S(2)}, u32[]{:S(2)}) collective-permute-start(f32[1,3,256]{1,2,0:T(8,128)} %get-tuple-element.32), channel_id=1, source_target_pairs={{16,0},{32,16},{48,32},{64,48},{80,64},{96,80},{112,96},{128,112},... | collective-permute-start | bytes 9224 | tf_op jit(solution)/shard_map/ppermute | solution.py:20
  225.4 10.6 collective-permute-start.4
  230.1 21.4 %copy-start.32 = (s32[256,1]{0,1:T(1,128)}, s32[256,1]{0,1:T(1,128)S(1)}, u32[]{:S(2)}) copy-start(s32[256,1]{0,1:T(1,128)S(1)} %get-tuple-element.52) | copy-start | bytes 3076
  251.5 19.0 %copy-start = (f32[1,1,3,4096]{3,1,2,0:T(1,128)S(1)}, f32[1,1,3,4096]{3,1,2,0:T(1,128)}, u32[]{:S(2)}) copy-start(f32[1,1,3,4096]{3,1,2,0:T(1,128)} %param.8) | copy-start | bytes 147460
  430.1 17.5 %copy-start.3 = (f32[3,4096]{0,1:T(8,128)}, f32[3,4096]{0,1:T(8,128)S(1)}, u32[]{:S(2)}) copy-start(f32[3,4096]{0,1:T(8,128)S(1)} %copy.121) | copy-start | bytes 147460
  434.3 13.2 collective-permute-start.12
  436.9 10.6 collective-permute-start.11
  440.5 7.0 collective-permute-start.10
  441.8 5.7 collective-permute-start.9
  446.4 28.0 %copy-start.9 = (f32[1,3,512]{2,1,0:T(4,128)}, f32[1,3,512]{2,1,0:T(4,128)S(1)}, u32[]{:S(2)}) copy-start(f32[1,3,512]{2,1,0:T(4,128)S(1)} %fusion.51) | copy-start | bytes 18436
  446.4 159.5 %collective-permute-start.17 = (f32[2,3,512]{2,1,0:T(4,128)S(1)}, f32[2,3,512]{2,1,0:T(4,128)S(1)}, u32[]{:S(2)}, u32[]{:S(2)}) collective-permute-start(f32[2,3,512]{2,1,0:T(4,128)S(1)} %pad_maximum_fusion.1), channel_id=1, source_target_pairs={{0,16},{16,0},{32,48},{48,32},{64,80},{80,64},{96,112},{112,96},{1... | collective-permute-start | bytes 36872 | tf_op jit(solution)/shard_map/ppermute | solution.py:26
  484.3 89.0 %copy-start.25 = (s32[1024]{0:T(1024)S(1)}, s32[1024]{0:T(1024)}, u32[]{:S(2)}) copy-start(s32[1024]{0:T(1024)} %copy-done.24) | copy-start | bytes 12292
  559.8 34.7 %collective-permute-start.16 = (f32[1,3,256]{1,2,0:T(8,128)}, f32[1,3,256]{1,2,0:T(8,128)}, u32[]{:S(2)}, u32[]{:S(2)}) collective-permute-start(f32[1,3,256]{1,2,0:T(8,128)} %get-tuple-element.26), channel_id=1, source_target_pairs={{1,0},{2,1},{3,2},{4,3},{5,4},{6,5},{7,6},{8,7},{9,8},{10,9},{11,1... | collective-permute-start | bytes 9224 | tf_op jit(solution)/shard_map/ppermute | solution.py:20
  561.8 27.7 %collective-permute-start.15 = (f32[1,3,256]{1,2,0:T(8,128)}, f32[1,3,256]{1,2,0:T(8,128)}, u32[]{:S(2)}, u32[]{:S(2)}) collective-permute-start(f32[1,3,256]{1,2,0:T(8,128)} %get-tuple-element.27), channel_id=1, source_target_pairs={{0,1},{1,2},{2,3},{3,4},{4,5},{5,6},{6,7},{7,8},{8,9},{9,10},{10,1... | collective-permute-start | bytes 9224 | tf_op jit(solution)/shard_map/ppermute | solution.py:17
  565.4 19.0 %collective-permute-start.14 = (f32[1,3,256]{1,2,0:T(8,128)}, f32[1,3,256]{1,2,0:T(8,128)}, u32[]{:S(2)}, u32[]{:S(2)}) collective-permute-start(f32[1,3,256]{1,2,0:T(8,128)} %get-tuple-element.28), channel_id=1, source_target_pairs={{16,0},{32,16},{48,32},{64,48},{80,64},{96,80},{112,96},{128,112},... | collective-permute-start | bytes 9224 | tf_op jit(solution)/shard_map/ppermute | solution.py:20
  566.7 12.6 collective-permute-start.13
  614.2 238.7 %copy-start.28 = (s32[1024]{0:T(1024)S(1)}, s32[1024]{0:T(1024)}, u32[]{:S(2)}) copy-start(s32[1024]{0:T(1024)} %copy-done.27) | copy-start | bytes 12292
  697.9 154.4 %copy-start.7 = (f32[3,512]{1,0:T(4,128)}, f32[3,512]{1,0:T(4,128)S(1)}, u32[]{:S(2)}) copy-start(f32[3,512]{1,0:T(4,128)S(1)} %get-tuple-element.19) | copy-start | bytes 18436
  853.0 20.7 %copy-start.2 = (f32[3,4096]{0,1:T(8,128)}, f32[3,4096]{0,1:T(8,128)S(1)}, u32[]{:S(2)}) copy-start(f32[3,4096]{0,1:T(8,128)S(1)} %copy.134) | copy-start | bytes 147460
  858.3 15.4 %collective-permute-start.21 = (f32[1,3,256]{2,1,0:T(4,128)S(1)}, f32[1,3,256]{2,1,0:T(4,128)S(1)}, u32[]{:S(2)}, u32[]{:S(2)}) collective-permute-start(f32[1,3,256]{2,1,0:T(4,128)S(1)} %get-tuple-element.36), channel_id=1, source_target_pairs={{1,0},{2,1},{3,2},{4,3},{5,4},{6,5},{7,6},{8,7},{9,8},{10,9},{11,1... | collective-permute-start | bytes 9224 | tf_op jit(solution)/shard_map/ppermute | solution.py:20
  860.8 12.8 collective-permute-start.20
  863.8 9.8 collective-permute-start.19
  865.1 8.5 collective-permute-start.18
  872.5 160.6 %collective-permute-start.26 = (f32[2,3,512]{2,1,0:T(4,128)}, f32[2,3,512]{2,1,0:T(4,128)}, u32[]{:S(2)}, u32[]{:S(2)}) collective-permute-start(f32[2,3,512]{2,1,0:T(4,128)} %pad_maximum_fusion.2), channel_id=1, source_target_pairs={{0,16},{16,0},{32,48},{48,32},{64,80},{80,64},{96,112},{112,96},{1... | collective-permute-start | bytes 36872 | tf_op jit(solution)/shard_map/ppermute | solution.py:26
  910.4 87.2 %copy-start.8 = (f32[3,512]{1,0:T(4,128)S(1)}, f32[3,512]{1,0:T(4,128)}, u32[]{:S(2)}) copy-start(f32[3,512]{1,0:T(4,128)} %copy-done.7) | copy-start | bytes 18436
  910.4 90.6 %copy-start.26 = (s32[1024]{0:T(1024)S(1)}, s32[1024]{0:T(1024)}, u32[]{:S(2)}) copy-start(s32[1024]{0:T(1024)} %copy-done.24) | copy-start | bytes 12292
  985.9 36.3 %collective-permute-start.25 = (f32[1,3,256]{1,2,0:T(8,128)}, f32[1,3,256]{1,2,0:T(8,128)S(1)}, u32[]{:S(2)}, u32[]{:S(2)}) collective-permute-start(f32[1,3,256]{1,2,0:T(8,128)} %get-tuple-element.22), channel_id=1, source_target_pairs={{1,0},{2,1},{3,2},{4,3},{5,4},{6,5},{7,6},{8,7},{9,8},{10,9},{11,1... | collective-permute-start | bytes 9224 | tf_op jit(solution)/shard_map/ppermute | solution.py:20
  988.1 29.0 %collective-permute-start.24 = (f32[1,3,256]{1,2,0:T(8,128)}, f32[1,3,256]{1,2,0:T(8,128)}, u32[]{:S(2)}, u32[]{:S(2)}) collective-permute-start(f32[1,3,256]{1,2,0:T(8,128)} %get-tuple-element.23), channel_id=1, source_target_pairs={{0,1},{1,2},{2,3},{3,4},{4,5},{5,6},{6,7},{7,8},{8,9},{9,10},{10,1... | collective-permute-start | bytes 9224 | tf_op jit(solution)/shard_map/ppermute | solution.py:17
  991.5 20.6 %collective-permute-start.23 = (f32[1,3,256]{1,2,0:T(8,128)}, f32[1,3,256]{1,2,0:T(8,128)}, u32[]{:S(2)}, u32[]{:S(2)}) collective-permute-start(f32[1,3,256]{1,2,0:T(8,128)} %get-tuple-element.24), channel_id=1, source_target_pairs={{16,0},{32,16},{48,32},{64,48},{80,64},{96,80},{112,96},{128,112},... | collective-permute-start | bytes 9224 | tf_op jit(solution)/shard_map/ppermute | solution.py:20
  992.8 14.2 %collective-permute-start.22 = (f32[1,3,256]{1,2,0:T(8,128)}, f32[1,3,256]{1,2,0:T(8,128)}, u32[]{:S(2)}, u32[]{:S(2)}) collective-permute-start(f32[1,3,256]{1,2,0:T(8,128)} %get-tuple-element.25), channel_id=1, source_target_pairs={{0,16},{16,32},{32,48},{48,64},{64,80},{80,96},{96,112},{112,128},... | collective-permute-start | bytes 9224 | tf_op jit(solution)/shard_map/ppermute | solution.py:17
  (15 other events, 172.1 us)
where the time goes:
time: 1380 us; the launch traced here: 1370 us
  blocking collectives  758 us (55%)
  other arithmetic  358 us (26%)
  local copies, waits for them, and re-layouts  153 us (11%)
  starting transfers between devices  70 us (5%)
  between operations  26.6 us (2%)
    psum x6, blocking collectives, body(): entry = lax.psum(local_inner(image, vector), ('px', 'py'))  456 us
    scatter-add x3, other arithmetic, element_apply(): jnp.zeros(extended.shape, jnp.float32).at[:, nodes]  224 us
    psum x3, blocking collectives, body(): norm = jnp.sqrt(lax.psum(local_inner(image, image), ('px', 'py')))  221 us
    gather x6, local copies, waits for them, and re-layouts, element_apply(): local = extended[:, nodes].reshape(81, count)  93.2 us
    psum x1, blocking collectives, body(): beta = jnp.sqrt(lax.psum(local_inner(rhs, rhs), ('px', 'py')))  81.4 us
    ppermute x12, starting transfers between devices, extended_2(): lax.ppermute(lax.slice_in_dim(block, block.shape[dim] - width, None, axis...  45.7 us
  transfers between devices with their start and end apart: 27, of which 0 were waited for; matrix products, arithmetic and copies ran while one was open for 32% of the time, Pallas kernels for 0%

commit v1 on v0

v1 whole, which is shorter than its diff:
```python
import jax
import jax.numpy as jnp
from jax import lax
from jax.experimental import pallas as pl
from jax.experimental.pallas import tpu as pltpu
from jax.sharding import PartitionSpec as P

ITERS = 3
LANES = 128
ROWS = 32
PIVOT_MIN = 0.01
f32, bf16, i32 = jnp.float32, jnp.bfloat16, jnp.int32
highest = lax.Precision.HIGHEST

VMEM = pl.BlockSpec(memory_space=pltpu.VMEM)
SMEM = pl.BlockSpec(memory_space=pltpu.SMEM)


def shape(*dims):
    return jax.ShapeDtypeStruct(dims, f32)


def call(kernel, outs, args, scratch=(), smem_first=False, flops=2_000_000):
    specs = [VMEM] * len(args)
    if smem_first:
        specs[0] = SMEM
    return pl.pallas_call(
        kernel,
        out_shape=outs,
        in_specs=specs,
        out_specs=[VMEM] * len(outs),
        scratch_shapes=list(scratch),
        compiler_params=pltpu.CompilerParams(vmem_limit_bytes=32 * 1024 * 1024),
        cost_estimate=pl.CostEstimate(flops=flops, bytes_accessed=1_000_000, transcendentals=0),
    )(*args)


def take_lanes(row, lanes):
    return jnp.take_along_axis(
        jnp.broadcast_to(row, lanes.shape), lanes, axis=1, mode="promise_in_bounds"
    )


def gather_rows(table, first, count, high, low, start):
    acc = [list(per) for per in start]
    for r in range(count):
        rows = [table(c, r) for c in range(3)]
        for n in range(len(high)):
            here = high[n] == r + first
            for c in range(3):
                acc[n][c] = jnp.where(here, take_lanes(rows[c], low[n]), acc[n][c])
    return acc


def one_hot_low(low_row):
    width = low_row.shape[1]
    rows = lax.broadcasted_iota(i32, (256, width), 0)
    return jnp.where(rows == low_row, 1.0, 0.0).astype(bf16)


def spread_owned(high_row, values):
    width = high_row.shape[1]
    rows = lax.broadcasted_iota(i32, (16, width), 0)
    here = rows == high_row
    upper, lower = [], []
    for value in values:
        top = value.astype(bf16).astype(f32)
        upper.append(jnp.where(here, top, 0.0))
        lower.append(jnp.where(here, value - top, 0.0))
    return jnp.concatenate(upper + lower, axis=0).astype(bf16)


def spread_ghost(high_row, values):
    width = high_row.shape[1]
    rows = lax.broadcasted_iota(i32, (16, width), 0)
    here = (rows < 12) & ((rows & 3) + 16 == high_row)
    tops = [value.astype(bf16).astype(f32) for value in values]
    rests = [value - top for value, top in zip(values, tops)]
    parts = []
    for v in (tops, rests):
        whole = jnp.where(rows < 4, v[0], jnp.where(rows < 8, v[1], v[2]))
        parts.append(jnp.where(here, whole, 0.0))
    return jnp.concatenate(parts, axis=0).astype(bf16)


def times_one_hot(spread, one_hot):
    return lax.dot_general(
        spread, one_hot, (((1,), (1,)), ((), ())), preferred_element_type=f32
    )


def send_payloads(par, u_ref, m_rows, sf, pay_e, pay_o, pay_f, pay_b, uown):
    high = [sf[8 * n : 8 * n + 8, :] >> 7 for n in range(2)]
    low = [sf[8 * n : 8 * n + 8, :] & 127 for n in range(2)]
    zero = jnp.zeros((8, LANES), f32)
    got = gather_rows(
        lambda c, r: u_ref[c, r : r + 1, :], 0, ROWS, high, low, [[zero] * 3, [zero] * 3]
    )
    pad = jnp.zeros((2, LANES), f32)
    sides = [
        jnp.concatenate([got[0][c][2 * s : 2 * s + 2, :] for c in range(3)] + [pad], axis=0)
        for s in range(4)
    ]
    odd = par == 1
    pay_e[0:8, :] = jnp.where(odd, sides[0], sides[1])
    pay_o[...] = jnp.where(odd, sides[1], sides[0])
    pay_b[...] = sides[2]
    pay_f[...] = sides[3]
    for c in range(3):
        pay_e[8 + 4 * c : 12 + 4 * c, :] = got[1][c][0:4, :]
        uown[4 * c : 4 * c + 4, :] = got[1][c][4:8, :]
    pay_e[20:32, :] = m_rows


def apply_blocks(inv_ref, w_ref, u_ref):
    w = [w_ref[c] for c in range(3)]
    for i in range(3):
        u_ref[i] = inv_ref[3 * i] * w[0] + inv_ref[3 * i + 1] * w[1] + inv_ref[3 * i + 2] * w[2]


def from_sides(flags, e, o, f, b):
    odd = flags[0] == 1
    zero = jnp.zeros((8, LANES), f32)
    e, o = e[0:8, :], o[...]
    return [
        jnp.where(flags[1] == 1, jnp.where(odd, e, o), zero),
        jnp.where(flags[2] == 1, jnp.where(odd, o, e), zero),
        jnp.where(flags[3] == 1, f[...], zero),
        jnp.where(flags[4] == 1, b[...], zero),
    ]


def first_kernel(flags, load, slip, inv, send, fault, w, m, inv_out, u, sf, pay_e, pay_o, pay_f, pay_b, uown):
    for r in range(ROWS):
        lanes = slice(LANES * r, LANES * r + LANES)
        for c in range(3):
            w[c, r : r + 1, :] = load[c : c + 1, lanes]
        for k in range(9):
            inv_out[k, r : r + 1, :] = inv[k : k + 1, lanes]
    for c in range(3):
        for t in range(4):
            m[4 * c + t : 4 * c + t + 1, :] = slip[c : c + 1, LANES * t : LANES * t + LANES]
    for s in range(4):
        for h in range(2):
            sf[2 * s + h : 2 * s + h + 1, :] = send[s : s + 1, LANES * h : LANES * h + LANES]
    for t in range(4):
        lanes = slice(LANES * t, LANES * t + LANES)
        sf[8 + t : 9 + t, :] = fault[1:2, lanes]
        sf[12 + t : 13 + t, :] = fault[0:1, lanes]
    apply_blocks(inv_out, w, u)
    send_payloads(flags[0], u, m[...], sf, pay_e, pay_o, pay_f, pay_b, uown)


def prepare_kernel(nodes, stiff, nodes_out, stiff_out):
    nodes_out[27:32, :] = jnp.zeros((5, 512), i32)
    nodes_out[0:27, :] = nodes[...]
    rows = lax.broadcasted_iota(i32, (96, 81), 0)
    cols = lax.broadcasted_iota(i32, (96, 81), 1)
    a = rows & 31
    widen = jnp.where(((rows >> 5) * 27 + a == cols) & (a < 27), 1.0, 0.0)
    for k in range(2):
        part = jnp.dot(widen, stiff[k], precision=highest, preferred_element_type=f32)
        stiff_out[:, 96 * k : 96 * k + 96] = lax.dot_general(
            part, widen, (((1,), (1,)), ((), ())), precision=highest, preferred_element_type=f32
        )


def local_kernel(u, nodes, got):
    zero = jnp.zeros((8, LANES), f32)

    def block(i, carry):
        first = pl.multiple_of(8 * i, 8)
        index = [nodes[pl.ds(first, 8), LANES * t : LANES * t + LANES] for t in range(4)]
        high = [x >> 7 for x in index]
        low = [x & 127 for x in index]
        acc = gather_rows(
            lambda c, r: u[c, r : r + 1, :], 0, ROWS, high, low, [[zero] * 3 for t in range(4)]
        )
        for t in range(4):
            for c in range(3):
                got[c, pl.ds(first, 8), LANES * t : LANES * t + LANES] = acc[t][c]
        return carry

    lax.fori_loop(0, 4, block, 0)


def element_kernel(flags, got, nodes, moduli, stiff, uown, e, o, f, b, r_out, m_next, facing,
                   pay_e, pay_o, pay_f, pay_b, ghost, wide, out):
    sides = from_sides(flags, e, o, f, b)
    for k in range(4):
        for c in range(3):
            ghost[c, 2 * k : 2 * k + 2, :] = sides[k][2 * c : 2 * c + 2, :]
    m_next[...] = uown[...] - e[8:20, :]
    facing[...] = e[20:32, :]

    def block(i, carry):
        first = pl.multiple_of(8 * i, 8)
        lanes = [slice(LANES * t, LANES * t + LANES) for t in range(4)]
        index = [nodes[pl.ds(first, 8), lane] for lane in lanes]
        high = [x >> 7 for x in index]
        low = [x & 127 for x in index]
        acc = gather_rows(
            lambda c, r: ghost[c, r : r + 1, :], ROWS, 8, high, low,
            [[got[c, pl.ds(first, 8), lane] for c in range(3)] for lane in lanes],
        )
        for t in range(4):
            for c in range(3):
                for k in range(2):
                    row = pl.multiple_of(96 * k + 32 * c + 8 * i, 8)
                    wide[pl.ds(row, 8), lanes[t]] = acc[t][c] * moduli[k : k + 1, lanes[t]]
        return carry

    lax.fori_loop(0, 4, block, 0)
    r_out[...] = jnp.dot(stiff[...], wide[...], precision=highest, preferred_element_type=f32)

    def scatter(i, total):
        spreads, hots = [], []
        for n in range(3):
            a = 3 * i + n
            index = nodes[pl.ds(a, 1), :]
            values = [r_out[pl.ds(32 * c + a, 1), :] for c in range(3)]
            spreads.append(spread_ghost(index >> 8, values))
            hots.append(one_hot_low(index & 255))
        return total + times_one_hot(
            jnp.concatenate(spreads, axis=1), jnp.concatenate(hots, axis=1)
        )

    total = lax.fori_loop(0, 9, scatter, jnp.zeros((32, 256), f32))
    both = total[0:16] + total[16:32]
    out[...] = both
    odd = flags[0] == 1
    for dst in (pay_e, pay_o, pay_f, pay_b):
        dst[6:8, :] = jnp.zeros((2, LANES), f32)
    for c in range(3):
        for h in range(2):
            lane = slice(LANES * h, LANES * h + LANES)
            blocks = [out[4 * c + k : 4 * c + k + 1, lane] for k in range(4)]
            row = slice(2 * c + h, 2 * c + h + 1)
            pay_e[row, :] = jnp.where(odd, blocks[0], blocks[1])
            pay_o[row, :] = jnp.where(odd, blocks[1], blocks[0])
            pay_b[row, :] = blocks[2]
            pay_f[row, :] = blocks[3]


def owned_kernel(r, nodes, sf, m, facing, part):
    def scatter(i, total):
        spreads, hots = [], []
        for n in range(3):
            a = 3 * i + n
            index = nodes[pl.ds(a, 1), :]
            values = [r[pl.ds(32 * c + a, 1), :] for c in range(3)]
            spreads.append(spread_owned(index >> 8, values))
            hots.append(one_hot_low(index & 255))
        return total + times_one_hot(
            jnp.concatenate(spreads, axis=1), jnp.concatenate(hots, axis=1)
        )

    total = lax.fori_loop(0, 9, scatter, jnp.zeros((96, 256), f32))
    spreads, hots = [], []
    for t in range(8):
        index = sf[8 + t : 9 + t, :]
        if t < 4:
            values = [-facing[4 * c + t : 4 * c + t + 1, :] for c in range(3)]
        else:
            values = [m[4 * c + t - 4 : 4 * c + t - 3, :] for c in range(3)]
        spreads.append(spread_owned(index >> 8, values))
        hots.append(one_hot_low(index & 255))
    total += times_one_hot(jnp.concatenate(spreads, axis=1), jnp.concatenate(hots, axis=1))
    part[...] = total[0:48] + total[48:96]


def assemble(flags, part, sf, e, o, f, b, w):
    sides = from_sides(flags, e, o, f, b)
    spreads, hots = [], []
    for s in range(4):
        for h in range(2):
            index = sf[2 * s + h : 2 * s + h + 1, :]
            values = [sides[s][2 * c + h : 2 * c + h + 1, :] for c in range(3)]
            spreads.append(spread_owned(index >> 8, values))
            hots.append(one_hot_low(index & 255))
    total = times_one_hot(jnp.concatenate(spreads, axis=1), jnp.concatenate(hots, axis=1))
    total = part[...] + total[0:48] + total[48:96]
    for c in range(3):
        for h in range(2):
            w[c, pl.ds(h, 16, stride=2), :] = total[
                16 * c : 16 * c + 16, LANES * h : LANES * h + LANES
            ]


def next_kernel(flags, part, sf, m_next, inv, e, o, f, b, w, u, pay_e, pay_o, pay_f, pay_b, uown):
    assemble(flags, part, sf, e, o, f, b, w)
    apply_blocks(inv, w, u)
    send_payloads(flags[0], u, m_next[...], sf, pay_e, pay_o, pay_f, pay_b, uown)


def last_kernel(flags, part, sf, e, o, f, b, w0, w1, w2, m0, m1, m2, m3, w3, sums):
    assemble(flags, part, sf, e, o, f, b, w3)
    fields, mults = [w0, w1, w2, w3], [m0, m1, m2, m3]
    lane = lax.broadcasted_iota(i32, (1, LANES), 1)
    row = jnp.zeros((1, LANES), f32)
    place = 0
    for i in range(4):
        for j in range(i, 4):
            prod = fields[i][...] * fields[j][...]
            prod = jnp.sum(prod, axis=0)
            total = jnp.sum(prod, axis=0, keepdims=True) + jnp.sum(
                mults[i][...] * mults[j][...], axis=0, keepdims=True
            )
            row = jnp.where(lane == place, jnp.sum(total, axis=1, keepdims=True), row)
            place += 1
    sums[...] = jnp.broadcast_to(row[None], sums.shape)


def finish_kernel(sums, u0, u1, u2, m0, m1, m2, disp, mult, good):
    whole = jnp.sum(sums[:, 0, :], axis=0, keepdims=True)
    gram = {}
    place = 0
    for i in range(4):
        for j in range(i, 4):
            gram[i, j] = whole[0:1, place : place + 1]
            place += 1
    scale = [lax.rsqrt(gram[i, i]) for i in range(4)]
    scale = [s * (1.5 - 0.5 * ((gram[i, i] * s) * s)) for i, s in enumerate(scale)]
    norm = {(i, j): (gram[i, j] * scale[i]) * scale[j] for i, j in gram}
    d1 = norm[1, 1]
    l21 = norm[1, 2] / d1
    l31 = norm[1, 3] / d1
    d2 = norm[2, 2] - l21 * norm[1, 2]
    t32 = norm[2, 3] - l21 * norm[1, 3]
    l32 = t32 / d2
    d3 = norm[3, 3] - l31 * norm[1, 3] - l32 * t32
    z1 = norm[0, 1]
    z2 = norm[0, 2] - l21 * z1
    z3 = norm[0, 3] - l31 * z1 - l32 * z2
    y3 = z3 / d3
    y2 = z2 / d2 - l32 * y3
    y1 = z1 / d1 - l21 * y2 - l31 * y3
    root = gram[0, 0] * scale[0]
    coef = [y1 * (root * scale[1]), y2 * (root * scale[2]), y3 * (root * scale[3])]
    ok = (d2 > PIVOT_MIN) & (d3 > PIVOT_MIN)
    for i in range(4):
        ok = ok & (gram[i, i] > 1e-25) & (gram[i, i] < 1e37)
    good[...] = jnp.where(ok, 1, 0)
    fields, mults = [u0, u1, u2], [m0, m1, m2]
    for c in range(3):
        sol = coef[0] * u0[c] + coef[1] * u1[c] + coef[2] * u2[c]
        for r in range(ROWS):
            disp[c : c + 1, LANES * r : LANES * r + LANES] = sol[r : r + 1, :]
    sol = coef[0] * m0[...] + coef[1] * m1[...] + coef[2] * m2[...]
    for c in range(3):
        for t in range(4):
            mult[c : c + 1, LANES * t : LANES * t + LANES] = sol[4 * c + t : 4 * c + t + 1, :]


def exchange(pay_e, pay_o, pay_f, pay_b):
    count_x, count_y = lax.axis_size("px"), lax.axis_size("py")
    pairs = [(i, i ^ 1) for i in range(count_x)]
    others = [(i, (((i + 1) ^ 1) - 1) % count_x) for i in range(count_x)]
    forward = [(i, (i + 1) % count_y) for i in range(count_y)]
    backward = [(i, (i - 1) % count_y) for i in range(count_y)]
    return (
        lax.ppermute(pay_e, "px", pairs),
        lax.ppermute(pay_o, "px", others),
        lax.ppermute(pay_f, "py", forward),
        lax.ppermute(pay_b, "py", backward),
    )


def half_operator(flags, u, m, uown, pays, nodes, moduli, stiff, sf):
    came = exchange(*pays)
    (got,) = call(local_kernel, [shape(3, 32, 512)], [u, nodes], flops=20_000_000)
    r, m_next, facing, *pays = call(
        element_kernel,
        [shape(96, 512), shape(12, LANES), shape(12, LANES)] + [shape(8, LANES)] * 4,
        [flags, got, nodes, moduli, stiff, uown, *came],
        scratch=[
            pltpu.VMEM((3, 8, LANES), f32),
            pltpu.VMEM((192, 512), f32),
            pltpu.VMEM((16, 256), f32),
        ],
        smem_first=True,
    )
    back = exchange(*pays)
    (part,) = call(owned_kernel, [shape(48, 256)], [r, nodes, sf, m, facing], flops=20_000_000)
    return part, back, m_next


PAYLOADS = [shape(32, LANES), shape(8, LANES), shape(8, LANES), shape(8, LANES), shape(12, LANES)]


def least_squares(columns, beta):
    cosines, sines, upper = ([], [], [])
    target = [beta] + [jnp.zeros_like(beta) for later in columns]
    for position, column in enumerate(columns):
        column = list(column)
        for earlier in range(position):
            top = cosines[earlier] * column[earlier] + sines[earlier] * column[earlier + 1]
            below = -sines[earlier] * column[earlier] + cosines[earlier] * column[earlier + 1]
            column[earlier] = top
            column[earlier + 1] = below
        pivot = column[position]
        under = column[position + 1]
        radius = jnp.sqrt(pivot * pivot + under * under)
        cosine = pivot / radius
        sine = under / radius
        column[position] = radius
        cosines.append(cosine)
        sines.append(sine)
        target[position + 1] = -sine * target[position]
        target[position] = cosine * target[position]
        upper.append(column)
    count = len(columns)
    coeffs = [None] * count
    for row_index in reversed(range(count)):
        total = target[row_index]
        for later in range(row_index + 1, count):
            total = total - upper[later][row_index] * coeffs[later]
        coeffs[row_index] = total / upper[row_index][row_index]
    return coeffs


def inner(first, second):
    total = jnp.sum(first[0] * second[0]) + jnp.sum(first[1] * second[1])
    return lax.psum(total, ("px", "py"))


def apply_kernel(flags, w, m, inv, sf, u, pay_e, pay_o, pay_f, pay_b, uown):
    apply_blocks(inv, w, u)
    send_payloads(flags[0], u, m[...], sf, pay_e, pay_o, pay_f, pay_b, uown)


def step_by_step(flags, w0, m0, inv, nodes, moduli, stiff, sf):
    beta = jnp.sqrt(inner((w0, m0), (w0, m0)))
    basis_w = jnp.zeros((ITERS + 1,) + w0.shape, f32).at[0].set(w0 / beta)
    basis_m = jnp.zeros((ITERS + 1,) + m0.shape, f32).at[0].set(m0 / beta)
    solves = jnp.zeros((ITERS,) + w0.shape, f32)
    entries = jnp.zeros((ITERS, ITERS + 1), f32)

    def step(j, state):
        basis_w, basis_m, solves, entries = state
        m = basis_m[j]
        u, *pays, uown = call(
            apply_kernel, [shape(3, ROWS, LANES)] + PAYLOADS,
            [flags, basis_w[j], m, inv, sf], smem_first=True,
        )
        part, back, m_next = half_operator(flags, u, m, uown, pays, nodes, moduli, stiff, sf)
        w = call(
            next_kernel, [shape(3, ROWS, LANES)] * 2 + PAYLOADS,
            [flags, part, sf, m_next, inv, *back], smem_first=True,
        )[0]
        column = []
        for i in range(ITERS):
            entry = jnp.where(i <= j, inner((w, m_next), (basis_w[i], basis_m[i])), 0.0)
            w, m_next = w - entry * basis_w[i], m_next - entry * basis_m[i]
            column.append(entry)
        norm = jnp.sqrt(inner((w, m_next), (w, m_next)))
        column = jnp.stack(column + [jnp.zeros_like(norm)])
        column = jnp.where(jnp.arange(ITERS + 1) == j + 1, norm, column)
        return (
            basis_w.at[j + 1].set(w / norm),
            basis_m.at[j + 1].set(m_next / norm),
            solves.at[j].set(u),
            entries.at[j].set(column),
        )

    basis_w, basis_m, solves, entries = lax.fori_loop(
        0, ITERS, step, (basis_w, basis_m, solves, entries)
    )
    columns = [[entries[j, i] for i in range(j + 2)] for j in range(ITERS)]
    coeffs = least_squares(columns, beta)
    disp = sum(coeffs[j] * solves[j] for j in range(ITERS))
    mult = sum(coeffs[j] * basis_m[j] for j in range(ITERS))
    return disp.reshape(3, ROWS * LANES), mult.reshape(3, 4 * LANES)


def body(body_force, fault_slip, elem_nodes, moduli, stiff_ref, block_inv, send_nodes, fault_nodes):
    lame = moduli[0, 0]
    at_x, at_y = lax.axis_index("px"), lax.axis_index("py")
    count_x, count_y = lax.axis_size("px"), lax.axis_size("py")
    flags = jnp.stack(
        [at_x % 2, at_x > 0, at_x < count_x - 1, at_y > 0, at_y < count_y - 1]
    ).astype(i32)
    w0, m0, inv, u, sf, *pays, uown = call(
        first_kernel,
        [
            shape(3, ROWS, LANES), shape(12, LANES), shape(9, ROWS, LANES), shape(3, ROWS, LANES),
            jax.ShapeDtypeStruct((16, LANES), i32),
        ] + PAYLOADS,
        [flags, body_force[0, 0], fault_slip[0, 0], block_inv[0, 0], send_nodes[0, 0], fault_nodes[0, 0]],
        smem_first=True,
    )
    nodes, stiff = call(
        prepare_kernel,
        [jax.ShapeDtypeStruct((32, 512), i32), shape(96, 192)],
        [elem_nodes[0, 0], stiff_ref],
    )
    fields, mults, solves = [w0], [m0], []
    for j in range(ITERS):
        solves.append(u)
        part, back, m = half_operator(flags, u, mults[-1], uown, pays, nodes, lame, stiff, sf)
        mults.append(m)
        if j < ITERS - 1:
            w, u, *pays, uown = call(
                next_kernel, [shape(3, ROWS, LANES)] * 2 + PAYLOADS,
                [flags, part, sf, m, inv, *back], smem_first=True,
            )
            fields.append(w)
    count = count_x * count_y
    w, sums = call(
        last_kernel, [shape(3, ROWS, LANES), shape(count, 1, LANES)],
        [flags, part, sf, *back, *fields, *mults], smem_first=True,
    )
    sums = lax.all_to_all(sums, ("px", "py"), 0, 0)
    disp, mult, good = call(
        finish_kernel,
        [shape(3, ROWS * LANES), shape(3, 4 * LANES), jax.ShapeDtypeStruct((1, 1), i32)],
        [sums, *solves, *mults[:ITERS]],
    )
    disp, mult = lax.cond(
        good[0, 0] == 1,
        lambda: (disp, mult),
        lambda: step_by_step(flags, w0, m0, inv, nodes, lame, stiff, sf),
    )
    return (disp[None, None], mult[None, None])


def solution(mesh):
    split = P("px", "py", None, None)
    in_specs = (split, split, split, split, P(), split, split, split)
    return jax.shard_map(
        body, mesh=mesh, in_specs=in_specs, out_specs=(split, split), check_vma=False
    )
```

time: 1380 us -> 115 us (0.08)
  blocking collectives: 758 us -> 0 us
  other arithmetic: 358 us -> 0 us
  local copies, waits for them, and re-layouts: 153 us -> 4.37 us
  Pallas kernels: 0 us -> 44.6 us
  between operations: 26.6 us -> 1.71 us
  starting transfers between devices: 70 us -> 51 us
    psum x10 -> x0, blocking collectives: 758 us -> none  [the longest x6 456 us: body(): entry = lax.psum(local_inner(image, vector), ('px', 'py'))]
    scatter-add x21 -> x0, other arithmetic: 320 us -> none  [the longest x3 224 us: element_apply(): jnp.zeros(extended.shape, jnp.float32).at[:, nodes]]
    gather x24 -> x0, local copies, waits for them, and re-layouts: 120 us -> none  [the longest x6 93.2 us: element_apply(): local = extended[:, nodes].reshape(81, count)]
    pallas_call x0 -> x15, Pallas kernels: none -> 44.6 us  [call(): pl.pallas_call(kernel, out_shape=outs, in_specs=specs, out_specs=[VMEM] *...]
    ppermute x27 -> x24, starting transfers between devices: 70 us -> 37.8 us  [the longest x6 15.2 us: exchange(): lax.ppermute(pay_o, 'px', others)]
    reduce_sum x24 -> x0, other arithmetic: 26.2 us -> none  [the longest x20 25.6 us: local_inner(): return jnp.sum(first[0] * second[0]) + jnp.sum(first[1] * second[1])]
  transfers between devices with their start and end apart: 27 -> 25, of which waited for: 0 -> 1; matrix products, arithmetic and copies ran while one was open for 32% -> 0% of each run, Pallas kernels for 0% -> 20%
where the time goes in v1:
time: 115 us
  starting transfers between devices  51 us (44%)
  Pallas kernels  44.6 us (39%)
  waiting for transfers between devices  12.9 us (11%)
  local copies, waits for them, and re-layouts  4.37 us (4%)
  between operations  1.71 us (1%)
    pallas_call x15, Pallas kernels, call(): pl.pallas_call(kernel, out_shape=outs, in_specs=specs, out_specs=[VMEM] *...  44.6 us
    ppermute x6, starting transfers between devices, exchange(): lax.ppermute(pay_o, 'px', others)  15.2 us
    ppermute x6, starting transfers between devices, exchange(): lax.ppermute(pay_b, 'py', backward)  14.1 us
    all_to_all x1, starting transfers between devices, body(): sums = lax.all_to_all(sums, ('px', 'py'), 0, 0)  13.2 us
    all_to_all x1, waiting for transfers between devices, body(): sums = lax.all_to_all(sums, ('px', 'py'), 0, 0)  12.8 us
    ppermute x6, starting transfers between devices, exchange(): lax.ppermute(pay_f, 'py', forward)  5.63 us
    unnamed x17, local copies, waits for them, and re-layouts  3.03 us
    ppermute x6, starting transfers between devices, exchange(): lax.ppermute(pay_e, 'px', pairs)  2.85 us
  transfers between devices with their start and end apart: 25, of which 1 were waited for; matrix products, arithmetic and copies ran while one was open for 0% of the time, Pallas kernels for 20%

profile of v1, /device:TPU:1, one launch (start us, length us, event | category | flops | bytes accessed | tf_op | source)
XLA Modules:
  0.0 114.6 jit_solution(14377099356583217267)
XLA Ops:
  0.7 0.7 copy.35
  1.4 0.8 copy.34
  2.2 0.1 copy.32
  2.3 0.1 stack.71.flags
  2.4 0.7 copy-done.1
  3.1 0.0 copy-done
  3.1 1.1 shard_map.99
  4.2 2.1 %collective-permute-start.8 = (f32[32,128]{1,0:T(8,128)S(1)}, f32[32,128]{1,0:T(8,128)S(1)}, u32[]{:S(2)}, u32[]{:S(2)}) collective-permute-start(f32[32,128]{1,0:T(8,128)S(1)} %get-tuple-element.471), channel_id=1, source_target_pairs={{0,16},{16,0},{32,48},{48,32},{64,80},{80,64},{96,112},{112,96},{1... | collective-permute-start | bytes 49160 | tf_op jit(solution)/shard_map/ppermute | solution.py:362
  6.3 4.3 %collective-permute-start.9 = (f32[8,128]{1,0:T(8,128)S(1)}, f32[8,128]{1,0:T(8,128)S(1)}, u32[]{:S(2)}, u32[]{:S(2)}) collective-permute-start(f32[8,128]{1,0:T(8,128)S(1)} %get-tuple-element.472), channel_id=1, source_target_pairs={{0,240},{16,32},{32,16},{48,64},{64,48},{80,96},{96,80},{112,128},... | collective-permute-start | bytes 12296 | tf_op jit(solution)/shard_map/ppermute | solution.py:363
  10.6 2.8 %collective-permute-start.10 = (f32[8,128]{1,0:T(8,128)S(1)}, f32[8,128]{1,0:T(8,128)S(1)}, u32[]{:S(2)}, u32[]{:S(2)}) collective-permute-start(f32[8,128]{1,0:T(8,128)S(1)} %get-tuple-element.473), channel_id=1, source_target_pairs={{0,1},{1,2},{2,3},{3,4},{4,5},{5,6},{6,7},{7,8},{8,9},{9,10},{10,1... | collective-permute-start | bytes 12296 | tf_op jit(solution)/shard_map/ppermute | solution.py:364
  13.4 0.6 shard_map.100
  14.0 3.5 %shard_map.101.got = f32[3,32,512]{2,1,0:T(8,128)S(1)} custom-call(f32[3,32,128]{2,1,0:T(8,128)S(1)} %get-tuple-element.467.u.u0, s32[32,512]{1,0:T(8,128)S(1)} %get-tuple-element.468.nodes), custom_call_target="tpu_custom_call" | custom-call | flops 20000000 | bytes 1000000 | tf_op jit(solution)/shard_map/pallas_call | solution.py:27
  17.5 0.0 copy-start.2
  17.6 0.6 copy-done.2
  18.2 5.1 %shard_map.102 = (f32[96,512]{1,0:T(8,128)S(1)}, f32[12,128]{1,0:T(8,128)S(1)}, f32[12,128]{1,0:T(8,128)S(1)}, f32[8,128]{1,0:T(8,128)S(1)}, f32[8,128]{1,0:T(8,...) custom-call(s32[5]{0:T(128)S(1)} %stack.71.flags, f32[3,32,512]{2,1,0:T(8,128)S(1)} %shard_map.101.got, ...), custom_call_target="tpu_custom_call" | custom-call | flops 2000000 | bytes 1000000 | tf_op jit(solution)/shard_map/pallas_call | solution.py:27
  23.4 0.1 collective-permute-start.12
  23.5 0.6 collective-permute-start.13
  24.1 2.3 %collective-permute-start.14 = (f32[8,128]{1,0:T(8,128)S(1)}, f32[8,128]{1,0:T(8,128)S(1)}, u32[]{:S(2)}, u32[]{:S(2)}) collective-permute-start(f32[8,128]{1,0:T(8,128)S(1)} %get-tuple-element.483), channel_id=1, source_target_pairs={{0,1},{1,2},{2,3},{3,4},{4,5},{5,6},{6,7},{7,8},{8,9},{9,10},{10,1... | collective-permute-start | bytes 12296 | tf_op jit(solution)/shard_map/ppermute | solution.py:364
  26.4 1.8 %collective-permute-start.15 = (f32[8,128]{1,0:T(8,128)S(1)}, f32[8,128]{1,0:T(8,128)S(1)}, u32[]{:S(2)}, u32[]{:S(2)}) collective-permute-start(f32[8,128]{1,0:T(8,128)S(1)} %get-tuple-element.484), channel_id=1, source_target_pairs={{0,15},{1,0},{2,1},{3,2},{4,3},{5,4},{6,5},{7,6},{8,7},{9,8},{10,9... | collective-permute-start | bytes 12296 | tf_op jit(solution)/shard_map/ppermute | solution.py:365
  28.1 3.8 %shard_map.103.part = f32[48,256]{1,0:T(8,128)S(1)} custom-call(f32[96,512]{1,0:T(8,128)S(1)} %get-tuple-element.475.r, s32[32,512]{1,0:T(8,128)S(1)} %get-tuple-element.468.nodes, s32[16,128]{1,0:T(8,128)S(1)} %get-tuple-element.476.sf, f32[12,128]{1,0:T(8,128)S(1)} %get-tuple-element.477.m.m0, f32[12,128]{1,0:T(8,128)S(1)} %get-tuple-element.478.facing), custom_call_target="tpu_custom_call" | custom-call | flops 20000000 | bytes 1000000 | tf_op jit(solution)/shard_map/pallas_call | solution.py:27
  32.0 1.3 %shard_map.104 = (f32[3,32,128]{2,1,0:T(8,128)S(1)}, f32[3,32,128]{2,1,0:T(8,128)S(1)}, f32[32,128]{1,0:T(8,128)S(1)}, f32[8,128]{1,0:T(8,128)S(1)}, f32[8,128]{...) custom-call(s32[5]{0:T(128)S(1)} %stack.71.flags, f32[48,256]{1,0:T(8,128)S(1)} %shard_map.103.part, ...), custom_call_target="tpu_custom_call" | custom-call | flops 2000000 | bytes 1000000 | tf_op jit(solution)/shard_map/pallas_call | solution.py:27
  33.3 0.4 collective-permute-start.16
  33.7 3.5 %collective-permute-start.17 = (f32[8,128]{1,0:T(8,128)S(1)}, f32[8,128]{1,0:T(8,128)S(1)}, u32[]{:S(2)}, u32[]{:S(2)}) collective-permute-start(f32[8,128]{1,0:T(8,128)S(1)} %get-tuple-element.488), channel_id=1, source_target_pairs={{0,240},{16,32},{32,16},{48,64},{64,48},{80,96},{96,80},{112,128},... | collective-permute-start | bytes 12296 | tf_op jit(solution)/shard_map/ppermute | solution.py:363
  37.2 0.6 collective-permute-start.18
  37.7 2.7 %collective-permute-start.19 = (f32[8,128]{1,0:T(8,128)S(1)}, f32[8,128]{1,0:T(8,128)S(1)}, u32[]{:S(2)}, u32[]{:S(2)}) collective-permute-start(f32[8,128]{1,0:T(8,128)S(1)} %get-tuple-element.490), channel_id=1, source_target_pairs={{0,15},{1,0},{2,1},{3,2},{4,3},{5,4},{6,5},{7,6},{8,7},{9,8},{10,9... | collective-permute-start | bytes 12296 | tf_op jit(solution)/shard_map/ppermute | solution.py:365
  40.4 3.5 %shard_map.105.got = f32[3,32,512]{2,1,0:T(8,128)S(1)} custom-call(f32[3,32,128]{2,1,0:T(8,128)S(1)} %get-tuple-element.485.u.u1, s32[32,512]{1,0:T(8,128)S(1)} %get-tuple-element.468.nodes), custom_call_target="tpu_custom_call" | custom-call | flops 20000000 | bytes 1000000 | tf_op jit(solution)/shard_map/pallas_call | solution.py:27
  44.0 5.1 %shard_map.106 = (f32[96,512]{1,0:T(8,128)S(1)}, f32[12,128]{1,0:T(8,128)S(1)}, f32[12,128]{1,0:T(8,128)S(1)}, f32[8,128]{1,0:T(8,128)S(1)}, f32[8,128]{1,0:T(8,...) custom-call(s32[5]{0:T(128)S(1)} %stack.71.flags, f32[3,32,512]{2,1,0:T(8,128)S(1)} %shard_map.105.got, ...), custom_call_target="tpu_custom_call" | custom-call | flops 2000000 | bytes 1000000 | tf_op jit(solution)/shard_map/pallas_call | solution.py:27
  49.1 0.1 collective-permute-start.20
  49.2 1.6 %collective-permute-start.21 = (f32[8,128]{1,0:T(8,128)S(1)}, f32[8,128]{1,0:T(8,128)S(1)}, u32[]{:S(2)}, u32[]{:S(2)}) collective-permute-start(f32[8,128]{1,0:T(8,128)S(1)} %get-tuple-element.495), channel_id=1, source_target_pairs={{0,240},{16,32},{32,16},{48,64},{64,48},{80,96},{96,80},{112,128},... | collective-permute-start | bytes 12296 | tf_op jit(solution)/shard_map/ppermute | solution.py:363
  50.8 3.2 %collective-permute-start.23 = (f32[8,128]{1,0:T(8,128)S(1)}, f32[8,128]{1,0:T(8,128)S(1)}, u32[]{:S(2)}, u32[]{:S(2)}) collective-permute-start(f32[8,128]{1,0:T(8,128)S(1)} %get-tuple-element.497), channel_id=1, source_target_pairs={{0,15},{1,0},{2,1},{3,2},{4,3},{5,4},{6,5},{7,6},{8,7},{9,8},{10,9... | collective-permute-start | bytes 12296 | tf_op jit(solution)/shard_map/ppermute | solution.py:365
  54.1 3.8 %shard_map.107.part = f32[48,256]{1,0:T(8,128)S(1)} custom-call(f32[96,512]{1,0:T(8,128)S(1)} %get-tuple-element.491.r, s32[32,512]{1,0:T(8,128)S(1)} %get-tuple-element.468.nodes, s32[16,128]{1,0:T(8,128)S(1)} %get-tuple-element.476.sf, f32[12,128]{1,0:T(8,128)S(1)} %get-tuple-element.479.m_next.m.m1, f32[12,128]{1,0:T(8,128)S(1)} %get-tuple-element.492.facing), custom_call_target="tpu_custom_call" | custom-call | flops 20000000 | bytes 1000000 | tf_op jit(solution)/shard_map/pallas_call | solution.py:27
  57.9 1.3 %shard_map.108 = (f32[3,32,128]{2,1,0:T(8,128)S(1)}, f32[3,32,128]{2,1,0:T(8,128)S(1)}, f32[32,128]{1,0:T(8,128)S(1)}, f32[8,128]{1,0:T(8,128)S(1)}, f32[8,128]{...) custom-call(s32[5]{0:T(128)S(1)} %stack.71.flags, f32[48,256]{1,0:T(8,128)S(1)} %shard_map.107.part, ...), custom_call_target="tpu_custom_call" | custom-call | flops 2000000 | bytes 1000000 | tf_op jit(solution)/shard_map/pallas_call | solution.py:27
  59.2 0.1 collective-permute-start.24
  59.3 3.5 %collective-permute-start.25 = (f32[8,128]{1,0:T(8,128)S(1)}, f32[8,128]{1,0:T(8,128)S(1)}, u32[]{:S(2)}, u32[]{:S(2)}) collective-permute-start(f32[8,128]{1,0:T(8,128)S(1)} %get-tuple-element.501), channel_id=1, source_target_pairs={{0,240},{16,32},{32,16},{48,64},{64,48},{80,96},{96,80},{112,128},... | collective-permute-start | bytes 12296 | tf_op jit(solution)/shard_map/ppermute | solution.py:363
  62.8 3.2 %collective-permute-start.27 = (f32[8,128]{1,0:T(8,128)S(1)}, f32[8,128]{1,0:T(8,128)S(1)}, u32[]{:S(2)}, u32[]{:S(2)}) collective-permute-start(f32[8,128]{1,0:T(8,128)S(1)} %get-tuple-element.503), channel_id=1, source_target_pairs={{0,15},{1,0},{2,1},{3,2},{4,3},{5,4},{6,5},{7,6},{8,7},{9,8},{10,9... | collective-permute-start | bytes 12296 | tf_op jit(solution)/shard_map/ppermute | solution.py:365
  66.1 3.5 %shard_map.109.got = f32[3,32,512]{2,1,0:T(8,128)S(1)} custom-call(f32[3,32,128]{2,1,0:T(8,128)S(1)} %get-tuple-element.498.u.u2, s32[32,512]{1,0:T(8,128)S(1)} %get-tuple-element.468.nodes), custom_call_target="tpu_custom_call" | custom-call | flops 20000000 | bytes 1000000 | tf_op jit(solution)/shard_map/pallas_call | solution.py:27
  69.6 5.1 %shard_map.110 = (f32[96,512]{1,0:T(8,128)S(1)}, f32[12,128]{1,0:T(8,128)S(1)}, f32[12,128]{1,0:T(8,128)S(1)}, f32[8,128]{1,0:T(8,128)S(1)}, f32[8,128]{1,0:T(8,...) custom-call(s32[5]{0:T(128)S(1)} %stack.71.flags, f32[3,32,512]{2,1,0:T(8,128)S(1)} %shard_map.109.got, ...), custom_call_target="tpu_custom_call" | custom-call | flops 2000000 | bytes 1000000 | tf_op jit(solution)/shard_map/pallas_call | solution.py:27
  74.8 0.1 collective-permute-start.28
  74.9 1.6 %collective-permute-start.29 = (f32[8,128]{1,0:T(8,128)S(1)}, f32[8,128]{1,0:T(8,128)S(1)}, u32[]{:S(2)}, u32[]{:S(2)}) collective-permute-start(f32[8,128]{1,0:T(8,128)S(1)} %get-tuple-element.507), channel_id=1, source_target_pairs={{0,240},{16,32},{32,16},{48,64},{64,48},{80,96},{96,80},{112,128},... | collective-permute-start | bytes 12296 | tf_op jit(solution)/shard_map/ppermute | solution.py:363
  76.5 3.2 %collective-permute-start.31 = (f32[8,128]{1,0:T(8,128)S(1)}, f32[8,128]{1,0:T(8,128)S(1)}, u32[]{:S(2)}, u32[]{:S(2)}) collective-permute-start(f32[8,128]{1,0:T(8,128)S(1)} %get-tuple-element.509), channel_id=1, source_target_pairs={{0,15},{1,0},{2,1},{3,2},{4,3},{5,4},{6,5},{7,6},{8,7},{9,8},{10,9... | collective-permute-start | bytes 12296 | tf_op jit(solution)/shard_map/ppermute | solution.py:365
  79.7 3.8 %shard_map.111.part = f32[48,256]{1,0:T(8,128)S(1)} custom-call(f32[96,512]{1,0:T(8,128)S(1)} %get-tuple-element.504.r, s32[32,512]{1,0:T(8,128)S(1)} %get-tuple-element.468.nodes, s32[16,128]{1,0:T(8,128)S(1)} %get-tuple-element.476.sf, f32[12,128]{1,0:T(8,128)S(1)} %get-tuple-element.493.m_next.m.m2, f32[12,128]{1,0:T(8,128)S(1)} %get-tuple-element.505.facing), custom_call_target="tpu_custom_call" | custom-call | flops 20000000 | bytes 1000000 | tf_op jit(solution)/shard_map/pallas_call | solution.py:27
  83.5 1.7 %shard_map.112 = (f32[3,32,128]{2,1,0:T(8,128)}, f32[256,1,128]{2,1,0:T(1,128)}) custom-call(s32[5]{0:T(128)S(1)} %stack.71.flags, f32[48,256]{1,0:T(8,128)S(1)} %shard_map.111.part, s32[16,128]{1,0:T(8,128)S(1)} %get-tuple-element.476.sf, f32[8,128]{1,0:T(8,128)S(1)} %collective-permute-done.28.e, f32[8,128]{1,0:T(8,128)S(1)} %collective-permute-done.29.o, ...), custom_call_target="tpu_custom_call" | custom-call | flops 2000000 | bytes 1000000 | tf_op jit(solution)/shard_map/pallas_call | solution.py:27
  85.2 13.2 %all-to-all-start = ((f32[256,1,128]{2,1,0:T(1,128)}), f32[256,1,128]{2,1,0:T(1,128)S(1)}, u32[]{:S(2)}, u32[]{:S(2)}) async-start(f32[256,1,128]{2,1,0:T(1,128)} %get-tuple-element.514), calls=%async_computation | async-start | bytes 262144 | tf_op jit(solution)/shard_map/all_to_all | solution.py:513
  98.4 12.8 %all-to-all-done.sums = f32[256,1,128]{2,1,0:T(1,128)S(1)} async-done(((f32[256,1,128]{2,1,0:T(1,128)}), f32[256,1,128]{2,1,0:T(1,128)S(1)}, u32[]{:S(2)}, u32[]{:S(2)}) %all-to-all-start) | async-done | bytes 131104 | tf_op jit(solution)/shard_map/all_to_all | solution.py:513
  111.3 1.4 %shard_map.113 = (f32[3,4096]{1,0:T(4,128)S(1)}, f32[3,512]{1,0:T(4,128)S(1)}, s32[1,1]{1,0:T(1,128)}) custom-call(f32[256,1,128]{2,1,0:T(1,128)S(1)} %all-to-all-done.sums, f32[3,32,128]{2,1,0:T(8,128)S(1)} %get-tuple-element.467.u.u0, f32[3,32,128]{2,1,0:T(8,128)S(1)} %get-tuple-element.485.u.u1, f32[3,32,128]{2,1,0:T(8,128)S(1)} %get-tuple-element.498.u.u2, ...), custom_call_target="tpu_custom_call" | custom-call | flops 2000000 | bytes 1000000 | tf_op jit(solution)/shard_map/pallas_call | solution.py:27
  113.3 1.3 %conditional.1 = (f32[1,1,3,4096]{3,1,2,0:T(1,128)}, f32[1,1,3,512]{3,1,2,0:T(1,128)}) conditional(s32[]{:T(128)} %bitcast.40, (f32[3,32,128]{2,1,0:T(8,128)S(1)}, f32[12,128]{1,0:T(8,128)S(1)}, s32[5]{0:T(128)S(1)}, f32[9,32,128]{2,1,0:T(8,128)S(1)}, s32[16,128]{1,0:T(8,128)S(1)}, /*index=5*/s32[32,512]{1,0:T(8,128)S(1)}, f32[2,512]{1,0:T(2,128)S(1)}, ...), branch_computations={%region_0.22_spmd, %region_22.23_spmd} | conditional | flops 46371820 | bytes 7154757 | solution.py:519
  113.3 0.7 reshape_bitcast_fusion
  114.0 0.6 copy.23
  (38 shorter events, 0.1 us)
Async XLA Ops:
  0.6 1.6 %copy-start.3 = (f32[1,1,9,4096]{3,1,2,0:T(1,128)S(1)}, f32[1,1,9,4096]{3,1,2,0:T(1,128)}, u32[]{:S(2)}) copy-start(f32[1,1,9,4096]{3,1,2,0:T(1,128)} %param.29) | copy-start | bytes 442372
  2.4 0.7 copy-start.1
  2.4 0.7 copy-start
  3.1 10.2 %copy-start.5 = (s32[1,1,27,512]{3,1,2,0:T(1,128)S(1)}, s32[1,1,27,512]{3,1,2,0:T(1,128)}, u32[]{:S(2)}) copy-start(s32[1,1,27,512]{3,1,2,0:T(1,128)} %param.26) | copy-start | bytes 165892
  4.2 9.2 %copy-start.4 = (f32[2,81,81]{2,0,1:T(2,128)S(1)}, f32[2,81,81]{2,0,1:T(2,128)}, u32[]{:S(2)}) copy-start(f32[2,81,81]{2,0,1:T(2,128)} %param.28) | copy-start | bytes 157468
  4.2 13.4 %collective-permute-start.8 = (f32[32,128]{1,0:T(8,128)S(1)}, f32[32,128]{1,0:T(8,128)S(1)}, u32[]{:S(2)}, u32[]{:S(2)}) collective-permute-start(f32[32,128]{1,0:T(8,128)S(1)} %get-tuple-element.471), channel_id=1, source_target_pairs={{0,16},{16,0},{32,48},{48,32},{64,80},{80,64},{96,112},{112,96},{1... | collective-permute-start | bytes 49160 | tf_op jit(solution)/shard_map/ppermute | solution.py:362
  6.3 11.2 %collective-permute-start.9 = (f32[8,128]{1,0:T(8,128)S(1)}, f32[8,128]{1,0:T(8,128)S(1)}, u32[]{:S(2)}, u32[]{:S(2)}) collective-permute-start(f32[8,128]{1,0:T(8,128)S(1)} %get-tuple-element.472), channel_id=1, source_target_pairs={{0,240},{16,32},{32,16},{48,64},{64,48},{80,96},{96,80},{112,128},... | collective-permute-start | bytes 12296 | tf_op jit(solution)/shard_map/ppermute | solution.py:363
  10.6 7.0 %collective-permute-start.10 = (f32[8,128]{1,0:T(8,128)S(1)}, f32[8,128]{1,0:T(8,128)S(1)}, u32[]{:S(2)}, u32[]{:S(2)}) collective-permute-start(f32[8,128]{1,0:T(8,128)S(1)} %get-tuple-element.473), channel_id=1, source_target_pairs={{0,1},{1,2},{2,3},{3,4},{4,5},{5,6},{6,7},{7,8},{8,9},{9,10},{10,1... | collective-permute-start | bytes 12296 | tf_op jit(solution)/shard_map/ppermute | solution.py:364
  13.4 4.2 %collective-permute-start.11 = (f32[8,128]{1,0:T(8,128)S(1)}, f32[8,128]{1,0:T(8,128)S(1)}, u32[]{:S(2)}, u32[]{:S(2)}) collective-permute-start(f32[8,128]{1,0:T(8,128)S(1)} %get-tuple-element.474), channel_id=1, source_target_pairs={{0,15},{1,0},{2,1},{3,2},{4,3},{5,4},{6,5},{7,6},{8,7},{9,8},{10,9... | collective-permute-start | bytes 12296 | tf_op jit(solution)/shard_map/ppermute | solution.py:365
  17.5 0.7 copy-start.2
  23.4 8.6 %collective-permute-start.12 = (f32[8,128]{1,0:T(8,128)S(1)}, f32[8,128]{1,0:T(8,128)S(1)}, u32[]{:S(2)}, u32[]{:S(2)}) collective-permute-start(f32[8,128]{1,0:T(8,128)S(1)} %get-tuple-element.481), channel_id=1, source_target_pairs={{0,16},{16,0},{32,48},{48,32},{64,80},{80,64},{96,112},{112,96},{1... | collective-permute-start | bytes 12296 | tf_op jit(solution)/shard_map/ppermute | solution.py:362
  23.5 8.5 %collective-permute-start.13 = (f32[8,128]{1,0:T(8,128)S(1)}, f32[8,128]{1,0:T(8,128)S(1)}, u32[]{:S(2)}, u32[]{:S(2)}) collective-permute-start(f32[8,128]{1,0:T(8,128)S(1)} %get-tuple-element.482), channel_id=1, source_target_pairs={{0,240},{16,32},{32,16},{48,64},{64,48},{80,96},{96,80},{112,128},... | collective-permute-start | bytes 12296 | tf_op jit(solution)/shard_map/ppermute | solution.py:363
  24.1 7.9 %collective-permute-start.14 = (f32[8,128]{1,0:T(8,128)S(1)}, f32[8,128]{1,0:T(8,128)S(1)}, u32[]{:S(2)}, u32[]{:S(2)}) collective-permute-start(f32[8,128]{1,0:T(8,128)S(1)} %get-tuple-element.483), channel_id=1, source_target_pairs={{0,1},{1,2},{2,3},{3,4},{4,5},{5,6},{6,7},{7,8},{8,9},{9,10},{10,1... | collective-permute-start | bytes 12296 | tf_op jit(solution)/shard_map/ppermute | solution.py:364
  26.4 5.6 %collective-permute-start.15 = (f32[8,128]{1,0:T(8,128)S(1)}, f32[8,128]{1,0:T(8,128)S(1)}, u32[]{:S(2)}, u32[]{:S(2)}) collective-permute-start(f32[8,128]{1,0:T(8,128)S(1)} %get-tuple-element.484), channel_id=1, source_target_pairs={{0,15},{1,0},{2,1},{3,2},{4,3},{5,4},{6,5},{7,6},{8,7},{9,8},{10,9... | collective-permute-start | bytes 12296 | tf_op jit(solution)/shard_map/ppermute | solution.py:365
  33.3 10.6 %collective-permute-start.16 = (f32[32,128]{1,0:T(8,128)S(1)}, f32[32,128]{1,0:T(8,128)S(1)}, u32[]{:S(2)}, u32[]{:S(2)}) collective-permute-start(f32[32,128]{1,0:T(8,128)S(1)} %get-tuple-element.487), channel_id=1, source_target_pairs={{0,16},{16,0},{32,48},{48,32},{64,80},{80,64},{96,112},{112,96},{1... | collective-permute-start | bytes 49160 | tf_op jit(solution)/shard_map/ppermute | solution.py:362
  33.7 10.3 %collective-permute-start.17 = (f32[8,128]{1,0:T(8,128)S(1)}, f32[8,128]{1,0:T(8,128)S(1)}, u32[]{:S(2)}, u32[]{:S(2)}) collective-permute-start(f32[8,128]{1,0:T(8,128)S(1)} %get-tuple-element.488), channel_id=1, source_target_pairs={{0,240},{16,32},{32,16},{48,64},{64,48},{80,96},{96,80},{112,128},... | collective-permute-start | bytes 12296 | tf_op jit(solution)/shard_map/ppermute | solution.py:363
  37.2 6.8 %collective-permute-start.18 = (f32[8,128]{1,0:T(8,128)S(1)}, f32[8,128]{1,0:T(8,128)S(1)}, u32[]{:S(2)}, u32[]{:S(2)}) collective-permute-start(f32[8,128]{1,0:T(8,128)S(1)} %get-tuple-element.489), channel_id=1, source_target_pairs={{0,1},{1,2},{2,3},{3,4},{4,5},{5,6},{6,7},{7,8},{8,9},{9,10},{10,1... | collective-permute-start | bytes 12296 | tf_op jit(solution)/shard_map/ppermute | solution.py:364
  37.7 6.2 %collective-permute-start.19 = (f32[8,128]{1,0:T(8,128)S(1)}, f32[8,128]{1,0:T(8,128)S(1)}, u32[]{:S(2)}, u32[]{:S(2)}) collective-permute-start(f32[8,128]{1,0:T(8,128)S(1)} %get-tuple-element.490), channel_id=1, source_target_pairs={{0,15},{1,0},{2,1},{3,2},{4,3},{5,4},{6,5},{7,6},{8,7},{9,8},{10,9... | collective-permute-start | bytes 12296 | tf_op jit(solution)/shard_map/ppermute | solution.py:365
  49.1 8.7 %collective-permute-start.20 = (f32[8,128]{1,0:T(8,128)S(1)}, f32[8,128]{1,0:T(8,128)S(1)}, u32[]{:S(2)}, u32[]{:S(2)}) collective-permute-start(f32[8,128]{1,0:T(8,128)S(1)} %get-tuple-element.494), channel_id=1, source_target_pairs={{0,16},{16,0},{32,48},{48,32},{64,80},{80,64},{96,112},{112,96},{1... | collective-permute-start | bytes 12296 | tf_op jit(solution)/shard_map/ppermute | solution.py:362
  49.2 8.7 %collective-permute-start.21 = (f32[8,128]{1,0:T(8,128)S(1)}, f32[8,128]{1,0:T(8,128)S(1)}, u32[]{:S(2)}, u32[]{:S(2)}) collective-permute-start(f32[8,128]{1,0:T(8,128)S(1)} %get-tuple-element.495), channel_id=1, source_target_pairs={{0,240},{16,32},{32,16},{48,64},{64,48},{80,96},{96,80},{112,128},... | collective-permute-start | bytes 12296 | tf_op jit(solution)/shard_map/ppermute | solution.py:363
  50.8 7.0 %collective-permute-start.22 = (f32[8,128]{1,0:T(8,128)S(1)}, f32[8,128]{1,0:T(8,128)S(1)}, u32[]{:S(2)}, u32[]{:S(2)}) collective-permute-start(f32[8,128]{1,0:T(8,128)S(1)} %get-tuple-element.496), channel_id=1, source_target_pairs={{0,1},{1,2},{2,3},{3,4},{4,5},{5,6},{6,7},{7,8},{8,9},{9,10},{10,1... | collective-permute-start | bytes 12296 | tf_op jit(solution)/shard_map/ppermute | solution.py:364
  50.8 7.0 %collective-permute-start.23 = (f32[8,128]{1,0:T(8,128)S(1)}, f32[8,128]{1,0:T(8,128)S(1)}, u32[]{:S(2)}, u32[]{:S(2)}) collective-permute-start(f32[8,128]{1,0:T(8,128)S(1)} %get-tuple-element.497), channel_id=1, source_target_pairs={{0,15},{1,0},{2,1},{3,2},{4,3},{5,4},{6,5},{7,6},{8,7},{9,8},{10,9... | collective-permute-start | bytes 12296 | tf_op jit(solution)/shard_map/ppermute | solution.py:365
  59.2 10.4 %collective-permute-start.24 = (f32[32,128]{1,0:T(8,128)S(1)}, f32[32,128]{1,0:T(8,128)S(1)}, u32[]{:S(2)}, u32[]{:S(2)}) collective-permute-start(f32[32,128]{1,0:T(8,128)S(1)} %get-tuple-element.500), channel_id=1, source_target_pairs={{0,16},{16,0},{32,48},{48,32},{64,80},{80,64},{96,112},{112,96},{1... | collective-permute-start | bytes 49160 | tf_op jit(solution)/shard_map/ppermute | solution.py:362
  59.3 10.3 %collective-permute-start.25 = (f32[8,128]{1,0:T(8,128)S(1)}, f32[8,128]{1,0:T(8,128)S(1)}, u32[]{:S(2)}, u32[]{:S(2)}) collective-permute-start(f32[8,128]{1,0:T(8,128)S(1)} %get-tuple-element.501), channel_id=1, source_target_pairs={{0,240},{16,32},{32,16},{48,64},{64,48},{80,96},{96,80},{112,128},... | collective-permute-start | bytes 12296 | tf_op jit(solution)/shard_map/ppermute | solution.py:363
  62.8 6.8 %collective-permute-start.26 = (f32[8,128]{1,0:T(8,128)S(1)}, f32[8,128]{1,0:T(8,128)S(1)}, u32[]{:S(2)}, u32[]{:S(2)}) collective-permute-start(f32[8,128]{1,0:T(8,128)S(1)} %get-tuple-element.502), channel_id=1, source_target_pairs={{0,1},{1,2},{2,3},{3,4},{4,5},{5,6},{6,7},{7,8},{8,9},{9,10},{10,1... | collective-permute-start | bytes 12296 | tf_op jit(solution)/shard_map/ppermute | solution.py:364
  62.8 6.8 %collective-permute-start.27 = (f32[8,128]{1,0:T(8,128)S(1)}, f32[8,128]{1,0:T(8,128)S(1)}, u32[]{:S(2)}, u32[]{:S(2)}) collective-permute-start(f32[8,128]{1,0:T(8,128)S(1)} %get-tuple-element.503), channel_id=1, source_target_pairs={{0,15},{1,0},{2,1},{3,2},{4,3},{5,4},{6,5},{7,6},{8,7},{9,8},{10,9... | collective-permute-start | bytes 12296 | tf_op jit(solution)/shard_map/ppermute | solution.py:365
  74.8 8.7 %collective-permute-start.28 = (f32[8,128]{1,0:T(8,128)S(1)}, f32[8,128]{1,0:T(8,128)S(1)}, u32[]{:S(2)}, u32[]{:S(2)}) collective-permute-start(f32[8,128]{1,0:T(8,128)S(1)} %get-tuple-element.506), channel_id=1, source_target_pairs={{0,16},{16,0},{32,48},{48,32},{64,80},{80,64},{96,112},{112,96},{1... | collective-permute-start | bytes 12296 | tf_op jit(solution)/shard_map/ppermute | solution.py:362
  74.9 8.7 %collective-permute-start.29 = (f32[8,128]{1,0:T(8,128)S(1)}, f32[8,128]{1,0:T(8,128)S(1)}, u32[]{:S(2)}, u32[]{:S(2)}) collective-permute-start(f32[8,128]{1,0:T(8,128)S(1)} %get-tuple-element.507), channel_id=1, source_target_pairs={{0,240},{16,32},{32,16},{48,64},{64,48},{80,96},{96,80},{112,128},... | collective-permute-start | bytes 12296 | tf_op jit(solution)/shard_map/ppermute | solution.py:363
  76.5 7.0 %collective-permute-start.30 = (f32[8,128]{1,0:T(8,128)S(1)}, f32[8,128]{1,0:T(8,128)S(1)}, u32[]{:S(2)}, u32[]{:S(2)}) collective-permute-start(f32[8,128]{1,0:T(8,128)S(1)} %get-tuple-element.508), channel_id=1, source_target_pairs={{0,1},{1,2},{2,3},{3,4},{4,5},{5,6},{6,7},{7,8},{8,9},{9,10},{10,1... | collective-permute-start | bytes 12296 | tf_op jit(solution)/shard_map/ppermute | solution.py:364
  76.5 7.0 %collective-permute-start.31 = (f32[8,128]{1,0:T(8,128)S(1)}, f32[8,128]{1,0:T(8,128)S(1)}, u32[]{:S(2)}, u32[]{:S(2)}) collective-permute-start(f32[8,128]{1,0:T(8,128)S(1)} %get-tuple-element.509), channel_id=1, source_target_pairs={{0,15},{1,0},{2,1},{3,2},{4,3},{5,4},{6,5},{7,6},{8,7},{9,8},{10,9... | collective-permute-start | bytes 12296 | tf_op jit(solution)/shard_map/ppermute | solution.py:365
  85.2 26.0 %all-to-all-start = ((f32[256,1,128]{2,1,0:T(1,128)}), f32[256,1,128]{2,1,0:T(1,128)S(1)}, u32[]{:S(2)}, u32[]{:S(2)}) async-start(f32[256,1,128]{2,1,0:T(1,128)} %get-tuple-element.514), calls=%async_computation | async-start | bytes 262144 | tf_op jit(solution)/shard_map/all_to_all | solution.py:513

commit v2 on v1

v2 whole, which is shorter than its diff:
```python
import jax
import jax.numpy as jnp
from jax import lax
from jax.experimental import pallas as pl
from jax.experimental.pallas import tpu as pltpu
from jax.sharding import PartitionSpec as P

ITERS = 3
LANES = 128
ROWS = 32
PIVOT_MIN = 0.01
f32, bf16, i32, i16 = jnp.float32, jnp.bfloat16, jnp.int32, jnp.int16
highest = lax.Precision.HIGHEST

VMEM = pl.BlockSpec(memory_space=pltpu.VMEM)
SMEM = pl.BlockSpec(memory_space=pltpu.SMEM)


def shape(*dims):
    return jax.ShapeDtypeStruct(dims, f32)


def call(kernel, outs, args, scratch=(), smem_first=False, flops=2_000_000):
    specs = [VMEM] * len(args)
    if smem_first:
        specs[0] = SMEM
    return pl.pallas_call(
        kernel,
        out_shape=outs,
        in_specs=specs,
        out_specs=[VMEM] * len(outs),
        scratch_shapes=list(scratch),
        compiler_params=pltpu.CompilerParams(vmem_limit_bytes=32 * 1024 * 1024),
        cost_estimate=pl.CostEstimate(flops=flops, bytes_accessed=1_000_000, transcendentals=0),
    )(*args)


def take_lanes(row, lanes):
    return jnp.take_along_axis(
        jnp.broadcast_to(row, lanes.shape), lanes, axis=1, mode="promise_in_bounds"
    )


def gather_rows(table, first, count, high, low, start):
    acc = [list(per) for per in start]
    for r in range(count):
        rows = [table(c, r) for c in range(3)]
        for n in range(len(high)):
            here = high[n] == r + first
            for c in range(3):
                acc[n][c] = jnp.where(here, take_lanes(rows[c], low[n]), acc[n][c])
    return acc


def pair_rows(row):
    return jnp.broadcast_to(row, (16, row.shape[1]))


def one_hot_low(low_row):
    width = low_row.shape[1]
    low = pair_rows(low_row).astype(i16)
    rows = lax.broadcasted_iota(i16, (16, width), 0)
    one, zero = jnp.ones((16, width), bf16), jnp.zeros((16, width), bf16)
    return [jnp.where(rows + i16(16 * g) == low, one, zero) for g in range(16)]


def spread(high_row, values, with_ghost):
    width = high_row.shape[1]
    high = pair_rows(high_row).astype(i16)
    rows = lax.broadcasted_iota(i16, (16, width), 0)
    here = rows == high
    zero = jnp.zeros((16, width), bf16)
    wide = [pair_rows(value) for value in values]
    tops = [value.astype(bf16) for value in wide]
    lows = [(value - top.astype(f32)).astype(bf16) for value, top in zip(wide, tops)]
    parts = [jnp.where(here, value, zero) for value in tops + lows]
    if with_ghost:
        ghost = jnp.where(rows < 12, (rows & 3) + i16(16), i16(-1)) == high
        for v in (tops, lows):
            whole = jnp.where(rows < 4, v[0], jnp.where(rows < 8, v[1], v[2]))
            parts.append(jnp.where(ghost, whole, zero))
    return parts


def place_chunk(spreads, hots, chunk, index_row, values, with_ghost):
    lanes = slice(LANES * chunk, LANES * chunk + LANES)
    for g, part in enumerate(spread(index_row >> 8, values, with_ghost)):
        spreads[16 * g : 16 * g + 16, lanes] = part
    for g, part in enumerate(one_hot_low(index_row & 255)):
        hots[16 * g : 16 * g + 16, lanes] = part


def scatter_product(spreads, hots):
    return lax.dot_general(
        hots[...], spreads[...], (((1,), (1,)), ((), ())), preferred_element_type=f32
    ).T


def send_payloads(par, u_ref, m_rows, sf, pay_e, pay_o, pay_f, pay_b, uown):
    index = [sf[0:8, :], sf[8:16, :]]
    high = [x >> 7 for x in index]
    low = [x & 127 for x in index]
    zero = jnp.zeros((8, LANES), f32)
    got = gather_rows(
        lambda c, r: u_ref[c, r : r + 1, :], 0, ROWS, high, low, [[zero] * 3, [zero] * 3]
    )
    pad = jnp.zeros((2, LANES), f32)
    sides = [
        jnp.concatenate([got[0][c][2 * s : 2 * s + 2, :] for c in range(3)] + [pad], axis=0)
        for s in range(4)
    ]
    odd = par == 1
    pay_e[0:8, :] = jnp.where(odd, sides[0], sides[1])
    pay_o[...] = jnp.where(odd, sides[1], sides[0])
    pay_b[...] = sides[2]
    pay_f[...] = sides[3]
    for c in range(3):
        uown[4 * c : 4 * c + 4, :] = got[1][c][0:4, :]
        pay_e[8 + 4 * c : 12 + 4 * c, :] = got[1][c][4:8, :]
    pay_e[20:32, :] = m_rows


def apply_blocks(inv_ref, w_ref, u_ref):
    w = [w_ref[c] for c in range(3)]
    for i in range(3):
        u_ref[i] = inv_ref[3 * i] * w[0] + inv_ref[3 * i + 1] * w[1] + inv_ref[3 * i + 2] * w[2]


def from_sides(flags, e, o, f, b):
    odd = flags[0] == 1
    zero = jnp.zeros((8, LANES), f32)
    e, o = e[0:8, :], o[...]
    return [
        jnp.where(flags[1] == 1, jnp.where(odd, e, o), zero),
        jnp.where(flags[2] == 1, jnp.where(odd, o, e), zero),
        jnp.where(flags[3] == 1, f[...], zero),
        jnp.where(flags[4] == 1, b[...], zero),
    ]


def first_kernel(flags, w, slip, inv, send, fault, m, u, sf, pay_e, pay_o, pay_f, pay_b, uown):
    for c in range(3):
        m[4 * c : 4 * c + 4, :] = slip[c]
    for s in range(4):
        for h in range(2):
            sf[2 * s + h : 2 * s + h + 1, :] = send[s : s + 1, LANES * h : LANES * h + LANES]
    for k in range(2):
        for t in range(4):
            row = 8 + 4 * k + t
            sf[row : row + 1, :] = fault[k : k + 1, LANES * t : LANES * t + LANES]
    apply_blocks(inv, w, u)
    send_payloads(flags[0], u, m[...], sf, pay_e, pay_o, pay_f, pay_b, uown)


def prepare_kernel(nodes, stiff, nodes_out, stiff_out):
    for a in range(27):
        nodes_out[4 * a : 4 * a + 4, :] = nodes[a]
    nodes_out[108:112, :] = jnp.zeros((4, LANES), i32)
    rows = lax.broadcasted_iota(i32, (96, 81), 0)
    cols = lax.broadcasted_iota(i32, (96, 81), 1)
    a = rows & 31
    widen = jnp.where(((rows >> 5) * 27 + a == cols) & (a < 27), 1.0, 0.0)
    for k in range(2):
        part = jnp.dot(widen, stiff[:, k, :], precision=highest, preferred_element_type=f32)
        part = lax.dot_general(
            part, widen, (((1,), (1,)), ((), ())), precision=highest, preferred_element_type=f32
        )
        top = part.astype(bf16)
        low = (part - top.astype(f32)).astype(bf16)
        stiff_out[96 * k : 96 * k + 96, :] = jnp.concatenate([top, top, low], axis=1)


def local_kernel(u, nodes, got):
    zero = jnp.zeros((8, LANES), f32)
    for i in range(14):
        index = nodes[8 * i : 8 * i + 8, :]
        (acc,) = gather_rows(
            lambda c, r: u[c, r : r + 1, :], 0, ROWS, [index >> 7], [index & 127], [[zero] * 3]
        )
        for c in range(3):
            got[c, 8 * i : 8 * i + 8, :] = acc[c]


def element_kernel(flags, got, nodes, moduli, stiff, sf, m, uown, e, o, f, b,
                   part, m_next, pay_e, pay_o, pay_f, pay_b, ghost, full, wide, r, spreads, hots, out):
    sides = from_sides(flags, e, o, f, b)
    for k in range(4):
        for c in range(3):
            ghost[c, 2 * k : 2 * k + 2, :] = sides[k][2 * c : 2 * c + 2, :]
    m_next[...] = uown[...] - e[8:20, :]
    for i in range(14):
        rows = slice(8 * i, 8 * i + 8)
        index = nodes[rows, :]
        (acc,) = gather_rows(
            lambda c, r: ghost[c, r : r + 1, :], ROWS, 8, [index >> 7], [index & 127],
            [[got[c, rows, :] for c in range(3)]],
        )
        for c in range(3):
            full[c, rows, :] = acc[c]
    for c in range(3):
        wide[32 * c + 24 : 32 * c + 32, :] = jnp.zeros((8, 512), f32)
        for t in range(4):
            wide[32 * c : 32 * c + 27, LANES * t : LANES * t + LANES] = full[
                c, pl.ds(t, 27, stride=4), :
            ]
    local = wide[...]
    top = local.astype(bf16)
    low = (local - top.astype(f32)).astype(bf16)
    both = jnp.dot(
        stiff[...], jnp.concatenate([top, low, top], axis=0), preferred_element_type=f32
    )
    r[...] = both[0:96] * moduli[0:1, :] + both[96:192] * moduli[1:2, :]
    for a in range(27):
        for t in range(4):
            lanes = slice(LANES * t, LANES * t + LANES)
            row = 4 * a + t
            values = [r[32 * c + a : 32 * c + a + 1, lanes] for c in range(3)]
            place_chunk(spreads, hots, row, nodes[row : row + 1, :], values, True)
    for t in range(8):
        if t < 4:
            values = [m[4 * c + t : 4 * c + t + 1, :] for c in range(3)]
        else:
            values = [-e[16 + 4 * c + t : 17 + 4 * c + t, :] for c in range(3)]
        place_chunk(spreads, hots, 108 + t, sf[8 + t : 9 + t, :], values, True)
    total = scatter_product(spreads, hots)
    part[...] = total[0:48] + total[48:96]
    out[...] = total[96:112] + total[112:128]
    odd = flags[0] == 1
    for dst in (pay_e, pay_o, pay_f, pay_b):
        dst[6:8, :] = jnp.zeros((2, LANES), f32)
    for c in range(3):
        for h in range(2):
            lane = slice(LANES * h, LANES * h + LANES)
            blocks = [out[4 * c + k : 4 * c + k + 1, lane] for k in range(4)]
            row = slice(2 * c + h, 2 * c + h + 1)
            pay_e[row, :] = jnp.where(odd, blocks[0], blocks[1])
            pay_o[row, :] = jnp.where(odd, blocks[1], blocks[0])
            pay_b[row, :] = blocks[2]
            pay_f[row, :] = blocks[3]


def assemble(flags, part, sf, e, o, f, b, w, spreads, hots):
    sides = from_sides(flags, e, o, f, b)
    for s in range(4):
        for h in range(2):
            row = 2 * s + h
            values = [sides[s][2 * c + h : 2 * c + h + 1, :] for c in range(3)]
            place_chunk(spreads, hots, row, sf[row : row + 1, :], values, False)
    total = scatter_product(spreads, hots)
    total = part[...] + total[0:48] + total[48:96]
    for c in range(3):
        for h in range(2):
            w[c, pl.ds(h, 16, stride=2), :] = total[
                16 * c : 16 * c + 16, LANES * h : LANES * h + LANES
            ]


def next_kernel(flags, part, sf, m_next, inv, e, o, f, b, w, u, pay_e, pay_o, pay_f, pay_b, uown,
                spreads, hots):
    assemble(flags, part, sf, e, o, f, b, w, spreads, hots)
    apply_blocks(inv, w, u)
    send_payloads(flags[0], u, m_next[...], sf, pay_e, pay_o, pay_f, pay_b, uown)


def last_kernel(flags, part, sf, e, o, f, b, w0, w1, w2, m0, m1, m2, m3, sums, w3, spreads, hots):
    assemble(flags, part, sf, e, o, f, b, w3, spreads, hots)
    fields, mults = [w0, w1, w2, w3], [m0, m1, m2, m3]
    lane = lax.broadcasted_iota(i32, (1, LANES), 1)
    row = jnp.zeros((1, LANES), f32)
    place = 0
    for i in range(4):
        for j in range(i, 4):
            prod = fields[i][...] * fields[j][...]
            prod = jnp.sum(prod, axis=0)
            total = jnp.sum(prod, axis=0, keepdims=True) + jnp.sum(
                mults[i][...] * mults[j][...], axis=0, keepdims=True
            )
            row = jnp.where(lane == place, jnp.sum(total, axis=1, keepdims=True), row)
            place += 1
    sums[...] = row


def solve_kernel(sums, coeffs, good):
    whole = jnp.sum(sums[:, 0, :], axis=0, keepdims=True)
    gram = {}
    place = 0
    for i in range(4):
        for j in range(i, 4):
            gram[i, j] = whole[0:1, place : place + 1]
            place += 1
    scale = [lax.rsqrt(gram[i, i]) for i in range(4)]
    scale = [s * (1.5 - 0.5 * ((gram[i, i] * s) * s)) for i, s in enumerate(scale)]
    norm = {(i, j): (gram[i, j] * scale[i]) * scale[j] for i, j in gram}
    d1 = norm[1, 1]
    l21 = norm[1, 2] / d1
    l31 = norm[1, 3] / d1
    d2 = norm[2, 2] - l21 * norm[1, 2]
    t32 = norm[2, 3] - l21 * norm[1, 3]
    l32 = t32 / d2
    d3 = norm[3, 3] - l31 * norm[1, 3] - l32 * t32
    z1 = norm[0, 1]
    z2 = norm[0, 2] - l21 * z1
    z3 = norm[0, 3] - l31 * z1 - l32 * z2
    y3 = z3 / d3
    y2 = z2 / d2 - l32 * y3
    y1 = z1 / d1 - l21 * y2 - l31 * y3
    root = gram[0, 0] * scale[0]
    coef = [y1 * (root * scale[1]), y2 * (root * scale[2]), y3 * (root * scale[3])]
    ok = (d2 > PIVOT_MIN) & (d3 > PIVOT_MIN)
    for i in range(4):
        ok = ok & (gram[i, i] > 1e-25) & (gram[i, i] < 1e37)
    good[...] = jnp.where(ok, 1, 0)
    lane = lax.broadcasted_iota(i32, (8, LANES), 0)
    coeffs[...] = jnp.where(lane == 0, coef[0], jnp.where(lane == 1, coef[1], coef[2]))


def finish_kernel(coeffs, u0, u1, u2, m0, m1, m2, disp, mult):
    coef = [coeffs[j : j + 1, :] for j in range(ITERS)]
    for c in range(3):
        disp[c] = coef[0] * u0[c] + coef[1] * u1[c] + coef[2] * u2[c]
        rows = slice(4 * c, 4 * c + 4)
        mult[c] = coef[0] * m0[rows, :] + coef[1] * m1[rows, :] + coef[2] * m2[rows, :]


def exchange(pay_e, pay_o, pay_f, pay_b):
    count_x, count_y = lax.axis_size("px"), lax.axis_size("py")
    pairs = [(i, i ^ 1) for i in range(count_x)]
    others = [(i, (((i + 1) ^ 1) - 1) % count_x) for i in range(count_x)]
    forward = [(i, (i + 1) % count_y) for i in range(count_y)]
    backward = [(i, (i - 1) % count_y) for i in range(count_y)]
    return (
        lax.ppermute(pay_e, "px", pairs),
        lax.ppermute(pay_o, "px", others),
        lax.ppermute(pay_f, "py", forward),
        lax.ppermute(pay_b, "py", backward),
    )


def half_operator(flags, u, m, uown, pays, nodes, moduli, stiff, sf):
    came = exchange(*pays)
    (got,) = call(local_kernel, [shape(3, 112, LANES)], [u, nodes], flops=20_000_000)
    part, m_next, *pays = call(
        element_kernel,
        [shape(48, 256), shape(12, LANES)] + [shape(8, LANES)] * 4,
        [flags, got, nodes, moduli, stiff, sf, m, uown, *came],
        scratch=[
            pltpu.VMEM((3, 8, LANES), f32),
            pltpu.VMEM((3, 112, LANES), f32),
            pltpu.VMEM((96, 512), f32),
            pltpu.VMEM((96, 512), f32),
            pltpu.VMEM((128, 116 * LANES), bf16),
            pltpu.VMEM((256, 116 * LANES), bf16),
            pltpu.VMEM((16, 256), f32),
        ],
        smem_first=True,
    )
    return part, exchange(*pays), m_next


SMALL = [pltpu.VMEM((96, 8 * LANES), bf16), pltpu.VMEM((256, 8 * LANES), bf16)]
PAYLOADS = [shape(32, LANES), shape(8, LANES), shape(8, LANES), shape(8, LANES), shape(12, LANES)]


def least_squares(columns, beta):
    cosines, sines, upper = ([], [], [])
    target = [beta] + [jnp.zeros_like(beta) for later in columns]
    for position, column in enumerate(columns):
        column = list(column)
        for earlier in range(position):
            top = cosines[earlier] * column[earlier] + sines[earlier] * column[earlier + 1]
            below = -sines[earlier] * column[earlier] + cosines[earlier] * column[earlier + 1]
            column[earlier] = top
            column[earlier + 1] = below
        pivot = column[position]
        under = column[position + 1]
        radius = jnp.sqrt(pivot * pivot + under * under)
        cosine = pivot / radius
        sine = under / radius
        column[position] = radius
        cosines.append(cosine)
        sines.append(sine)
        target[position + 1] = -sine * target[position]
        target[position] = cosine * target[position]
        upper.append(column)
    count = len(columns)
    coeffs = [None] * count
    for row_index in reversed(range(count)):
        total = target[row_index]
        for later in range(row_index + 1, count):
            total = total - upper[later][row_index] * coeffs[later]
        coeffs[row_index] = total / upper[row_index][row_index]
    return coeffs


def inner(first, second):
    total = jnp.sum(first[0] * second[0]) + jnp.sum(first[1] * second[1])
    return lax.psum(total, ("px", "py"))


def apply_kernel(flags, w, m, inv, sf, u, pay_e, pay_o, pay_f, pay_b, uown):
    apply_blocks(inv, w, u)
    send_payloads(flags[0], u, m[...], sf, pay_e, pay_o, pay_f, pay_b, uown)


def step_by_step(flags, w0, m0, inv, nodes, moduli, stiff, sf):
    beta = jnp.sqrt(inner((w0, m0), (w0, m0)))
    basis_w = jnp.zeros((ITERS + 1,) + w0.shape, f32).at[0].set(w0 / beta)
    basis_m = jnp.zeros((ITERS + 1,) + m0.shape, f32).at[0].set(m0 / beta)
    solves = jnp.zeros((ITERS,) + w0.shape, f32)
    entries = jnp.zeros((ITERS, ITERS + 1), f32)

    def step(j, state):
        basis_w, basis_m, solves, entries = state
        m = basis_m[j]
        u, *pays, uown = call(
            apply_kernel, [shape(3, ROWS, LANES)] + PAYLOADS,
            [flags, basis_w[j], m, inv, sf], smem_first=True,
        )
        part, back, m_next = half_operator(flags, u, m, uown, pays, nodes, moduli, stiff, sf)
        w = call(
            next_kernel, [shape(3, ROWS, LANES)] * 2 + PAYLOADS,
            [flags, part, sf, m_next, inv, *back], scratch=SMALL, smem_first=True,
        )[0]
        column = []
        for i in range(ITERS):
            entry = jnp.where(i <= j, inner((w, m_next), (basis_w[i], basis_m[i])), 0.0)
            w, m_next = w - entry * basis_w[i], m_next - entry * basis_m[i]
            column.append(entry)
        norm = jnp.sqrt(inner((w, m_next), (w, m_next)))
        column = jnp.stack(column + [jnp.zeros_like(norm)])
        column = jnp.where(jnp.arange(ITERS + 1) == j + 1, norm, column)
        return (
            basis_w.at[j + 1].set(w / norm),
            basis_m.at[j + 1].set(m_next / norm),
            solves.at[j].set(u),
            entries.at[j].set(column),
        )

    basis_w, basis_m, solves, entries = lax.fori_loop(
        0, ITERS, step, (basis_w, basis_m, solves, entries)
    )
    columns = [[entries[j, i] for i in range(j + 2)] for j in range(ITERS)]
    coeffs = least_squares(columns, beta)
    disp = sum(coeffs[j] * solves[j] for j in range(ITERS))
    mult = sum(coeffs[j] * basis_m[j] for j in range(ITERS))
    return disp, mult.reshape(3, 4, LANES)


def body(body_force, fault_slip, elem_nodes, moduli, stiff_ref, block_inv, send_nodes, fault_nodes):
    lame = moduli[0, 0]
    at_x, at_y = lax.axis_index("px"), lax.axis_index("py")
    count_x, count_y = lax.axis_size("px"), lax.axis_size("py")
    flags = jnp.stack(
        [at_x % 2, at_x > 0, at_x < count_x - 1, at_y > 0, at_y < count_y - 1]
    ).astype(i32)
    w0 = body_force.reshape(3, ROWS, LANES)
    inv = block_inv.reshape(9, ROWS, LANES)
    m0, u, sf, *pays, uown = call(
        first_kernel,
        [shape(12, LANES), shape(3, ROWS, LANES), jax.ShapeDtypeStruct((16, LANES), i32)] + PAYLOADS,
        [flags, w0, fault_slip.reshape(3, 4, LANES), inv, send_nodes[0, 0], fault_nodes[0, 0]],
        smem_first=True,
    )
    nodes, stiff = call(
        prepare_kernel,
        [jax.ShapeDtypeStruct((112, LANES), i32), jax.ShapeDtypeStruct((192, 288), bf16)],
        [elem_nodes.reshape(27, 4, LANES), stiff_ref.transpose(1, 0, 2)],
    )
    fields, mults, solves = [w0], [m0], []
    for j in range(ITERS):
        solves.append(u)
        part, back, m = half_operator(flags, u, mults[-1], uown, pays, nodes, lame, stiff, sf)
        mults.append(m)
        if j < ITERS - 1:
            w, u, *pays, uown = call(
                next_kernel, [shape(3, ROWS, LANES)] * 2 + PAYLOADS,
                [flags, part, sf, m, inv, *back], scratch=SMALL, smem_first=True,
            )
            fields.append(w)
    count = count_x * count_y
    (sums,) = call(
        last_kernel, [shape(1, LANES)], [flags, part, sf, *back, *fields, *mults],
        scratch=[pltpu.VMEM((3, ROWS, LANES), f32)] + SMALL, smem_first=True,
    )
    sums = lax.all_to_all(
        jnp.broadcast_to(sums[None], (count, 1, LANES)), ("px", "py"), 0, 0
    )
    coeffs, good = call(
        solve_kernel, [shape(8, LANES), jax.ShapeDtypeStruct((1, 1), i32)], [sums]
    )
    disp, mult = lax.cond(
        good[0, 0] == 1,
        lambda: tuple(
            call(
                finish_kernel,
                [shape(3, ROWS, LANES), shape(3, 4, LANES)],
                [coeffs, *solves, *mults[:ITERS]],
            )
        ),
        lambda: step_by_step(flags, w0, m0, inv, nodes, lame, stiff, sf),
    )
    return (disp.reshape(body_force.shape), mult.reshape(fault_slip.shape))


def solution(mesh):
    split = P("px", "py", None, None)
    in_specs = (split, split, split, split, P(), split, split, split)
    return jax.shard_map(
        body, mesh=mesh, in_specs=in_specs, out_specs=(split, split), check_vma=False
    )
```

time: 115 us -> 113 us (0.983)
  Pallas kernels: 44.6 us -> 26.3 us
  starting transfers between devices: 51 us -> 62.3 us
  waiting for transfers between devices: 12.9 us -> 20 us
  local copies, waits for them, and re-layouts: 4.37 us -> 2.21 us
    pallas_call x15 -> x13, Pallas kernels: 44.6 us -> 26.3 us  [call(): pl.pallas_call(kernel, out_shape=outs, in_specs=specs, out_specs=[VMEM] *...]
    ppermute x6, starting transfers between devices: 15.2 us -> 28.6 us  [exchange(): lax.ppermute(pay_o, 'px', others)]
    ppermute x6, starting transfers between devices: 14.1 us -> 6.05 us  [exchange(): lax.ppermute(pay_b, 'py', backward)]
    ppermute x6, starting transfers between devices: 5.63 us -> 12.3 us  [exchange(): lax.ppermute(pay_f, 'py', forward)]
    ppermute x6, waiting for transfers between devices: 0.02 us -> 3.94 us  [exchange(): lax.ppermute(pay_b, 'py', backward)]
    ppermute x6, waiting for transfers between devices: 0.02 us -> 2.4 us  [exchange(): lax.ppermute(pay_o, 'px', others)]
    unnamed x17 -> x16, local copies, waits for them, and re-layouts: 3.03 us -> 1.4 us
    cond x2 -> x0, local copies, waits for them, and re-layouts: 1.25 us -> none  [body(): lax.cond(good[0, 0] == 1, lambda: (disp, mult), lambda: step_by_step(flag...]
  transfers between devices with their start and end apart: 25 -> 25, of which waited for: 1 -> 11; matrix products, arithmetic and copies ran while one was open for 0% -> 0% of each run, Pallas kernels for 20% -> 5%
where the time goes in v2:
time: 113 us
  starting transfers between devices  62.3 us (55%)
  Pallas kernels  26.3 us (23%)
  waiting for transfers between devices  20 us (18%)
  local copies, waits for them, and re-layouts  2.21 us (2%)
  between operations  1.73 us (2%)
    ppermute x6, starting transfers between devices, exchange(): lax.ppermute(pay_o, 'px', others)  28.6 us
    pallas_call x13, Pallas kernels, call(): pl.pallas_call(kernel, out_shape=outs, in_specs=specs, out_specs=[VMEM] *...  26.3 us
    all_to_all x1, waiting for transfers between devices, body(): lax.all_to_all(jnp.broadcast_to(sums[None], (count, 1, LANES)), ('px', 'p...  12.9 us
    all_to_all x1, starting transfers between devices, body(): lax.all_to_all(jnp.broadcast_to(sums[None], (count, 1, LANES)), ('px', 'p...  12.7 us
    ppermute x6, starting transfers between devices, exchange(): lax.ppermute(pay_f, 'py', forward)  12.3 us
    ppermute x6, starting transfers between devices, exchange(): lax.ppermute(pay_b, 'py', backward)  6.05 us
    ppermute x6, waiting for transfers between devices, exchange(): lax.ppermute(pay_b, 'py', backward)  3.94 us
    ppermute x6, starting transfers between devices, exchange(): lax.ppermute(pay_e, 'px', pairs)  2.59 us
  transfers between devices with their start and end apart: 25, of which 11 were waited for; matrix products, arithmetic and copies ran while one was open for 0% of the time, Pallas kernels for 5%

profile of v2, /device:TPU:1, one launch (start us, length us, event | category | flops | bytes accessed | tf_op | source)
XLA Modules:
  0.0 112.6 jit_solution(18354884132040495430)
XLA Ops:
  0.8 0.7 copy-done.6
  1.5 1.4 %shard_map.99 = (f32[12,128]{1,0:T(8,128)S(1)}, f32[3,32,128]{2,1,0:T(8,128)S(1)}, s32[16,128]{1,0:T(8,128)S(1)}, f32[32,128]{1,0:T(8,128)S(1)}, f32[8,128]{1,0:...) custom-call(s32[5]{0:T(128)S(1)} %stack.71.flags, f32[3,32,128]{2,1,0:T(8,128)S(1)} %bitcast.158, ...), custom_call_target="tpu_custom_call" | custom-call | flops 2000000 | bytes 1000000 | tf_op jit(solution)/shard_map/pallas_call | solution.py:27
  2.9 2.1 %collective-permute-start.8 = (f32[32,128]{1,0:T(8,128)S(1)}, f32[32,128]{1,0:T(8,128)S(1)}, u32[]{:S(2)}, u32[]{:S(2)}) collective-permute-start(f32[32,128]{1,0:T(8,128)S(1)} %get-tuple-element.482), channel_id=1, source_target_pairs={{0,16},{16,0},{32,48},{48,32},{64,80},{80,64},{96,112},{112,96},{1... | collective-permute-start | bytes 49160 | tf_op jit(solution)/shard_map/ppermute | solution.py:332
  5.0 4.3 %collective-permute-start.9 = (f32[8,128]{1,0:T(8,128)S(1)}, f32[8,128]{1,0:T(8,128)S(1)}, u32[]{:S(2)}, u32[]{:S(2)}) collective-permute-start(f32[8,128]{1,0:T(8,128)S(1)} %get-tuple-element.483), channel_id=1, source_target_pairs={{0,240},{16,32},{32,16},{48,64},{64,48},{80,96},{96,80},{112,128},... | collective-permute-start | bytes 12296 | tf_op jit(solution)/shard_map/ppermute | solution.py:333
  9.3 2.8 %collective-permute-start.10 = (f32[8,128]{1,0:T(8,128)S(1)}, f32[8,128]{1,0:T(8,128)S(1)}, u32[]{:S(2)}, u32[]{:S(2)}) collective-permute-start(f32[8,128]{1,0:T(8,128)S(1)} %get-tuple-element.484), channel_id=1, source_target_pairs={{0,1},{1,2},{2,3},{3,4},{4,5},{5,6},{6,7},{7,8},{8,9},{9,10},{10,1... | collective-permute-start | bytes 12296 | tf_op jit(solution)/shard_map/ppermute | solution.py:334
  12.1 0.6 shard_map.100
  12.7 1.5 %shard_map.101.got = f32[3,112,128]{2,1,0:T(8,128)S(1)} custom-call(f32[3,32,128]{2,1,0:T(8,128)S(1)} %get-tuple-element.476.u, s32[112,128]{1,0:T(8,128)S(1)} %get-tuple-element.477.nodes), custom_call_target="tpu_custom_call" | custom-call | flops 20000000 | bytes 1000000 | tf_op jit(solution)/shard_map/pallas_call | solution.py:27
  14.3 0.8 collective-permute-done.11.b
  15.1 0.7 copy-done.7
  15.8 4.6 %shard_map.102 = (f32[48,256]{1,0:T(8,128)S(1)}, f32[12,128]{1,0:T(8,128)S(1)}, f32[8,128]{1,0:T(8,128)S(1)}, f32[8,128]{1,0:T(8,128)S(1)}, f32[8,128]{1,0:T(8,128)S(1)}, /*index=5*/f32[8,128]{1,0:T(8,128)S(1)}) custom-call(s32[5]{0:T(128)S(1)} %stack.71.flags, f32[3,112,128]{2,1,0:T(8,128)S(1)} %shard_map.101.got, s32[112,128]{1,0:T(8,128)S(1)} %get-tuple-element.477.nodes, ...), custom_call_target="tpu_custom_call" | custom-call | flops 2000000 | bytes 1000000 | tf_op jit(solution)/shard_map/pallas_call | solution.py:27
  20.5 0.9 collective-permute-start.13
  21.4 3.1 %collective-permute-start.14 = (f32[8,128]{1,0:T(8,128)S(1)}, f32[8,128]{1,0:T(8,128)S(1)}, u32[]{:S(2)}, u32[]{:S(2)}) collective-permute-start(f32[8,128]{1,0:T(8,128)S(1)} %get-tuple-element.490), channel_id=1, source_target_pairs={{0,1},{1,2},{2,3},{3,4},{4,5},{5,6},{6,7},{7,8},{8,9},{9,10},{10,1... | collective-permute-start | bytes 12296 | tf_op jit(solution)/shard_map/ppermute | solution.py:334
  24.5 1.9 %collective-permute-done.13.o = f32[8,128]{1,0:T(8,128)S(1)} collective-permute-done((f32[8,128]{1,0:T(8,128)S(1)}, f32[8,128]{1,0:T(8,128)S(1)}, u32[]{:S(2)}, u32[]{:S(2)}) %collective-permute-start.13) | collective-permute-done | bytes 4128 | tf_op jit(solution)/shard_map/ppermute | solution.py:333
  26.3 1.5 %collective-permute-done.15.b = f32[8,128]{1,0:T(8,128)S(1)} collective-permute-done((f32[8,128]{1,0:T(8,128)S(1)}, f32[8,128]{1,0:T(8,128)S(1)}, u32[]{:S(2)}, u32[]{:S(2)}) %collective-permute-start.15) | collective-permute-done | bytes 4128 | tf_op jit(solution)/shard_map/ppermute | solution.py:335
  27.8 1.4 %shard_map.103 = (f32[3,32,128]{2,1,0:T(8,128)S(1)}, f32[3,32,128]{2,1,0:T(8,128)S(1)}, f32[32,128]{1,0:T(8,128)S(1)}, f32[8,128]{1,0:T(8,128)S(1)}, f32[8,128]{...) custom-call(s32[5]{0:T(128)S(1)} %stack.71.flags, f32[48,256]{1,0:T(8,128)S(1)} %get-tuple-element.486.part, ...), custom_call_target="tpu_custom_call" | custom-call | flops 2000000 | bytes 1000000 | tf_op jit(solution)/shard_map/pallas_call | solution.py:27
  29.3 2.5 %collective-permute-start.17 = (f32[8,128]{1,0:T(8,128)S(1)}, f32[8,128]{1,0:T(8,128)S(1)}, u32[]{:S(2)}, u32[]{:S(2)}) collective-permute-start(f32[8,128]{1,0:T(8,128)S(1)} %get-tuple-element.495), channel_id=1, source_target_pairs={{0,240},{16,32},{32,16},{48,64},{64,48},{80,96},{96,80},{112,128},... | collective-permute-start | bytes 12296 | tf_op jit(solution)/shard_map/ppermute | solution.py:333
  31.8 1.5 %collective-permute-start.18 = (f32[8,128]{1,0:T(8,128)S(1)}, f32[8,128]{1,0:T(8,128)S(1)}, u32[]{:S(2)}, u32[]{:S(2)}) collective-permute-start(f32[8,128]{1,0:T(8,128)S(1)} %get-tuple-element.496), channel_id=1, source_target_pairs={{0,1},{1,2},{2,3},{3,4},{4,5},{5,6},{6,7},{7,8},{8,9},{9,10},{10,1... | collective-permute-start | bytes 12296 | tf_op jit(solution)/shard_map/ppermute | solution.py:334
  33.3 1.2 %collective-permute-start.19 = (f32[8,128]{1,0:T(8,128)S(1)}, f32[8,128]{1,0:T(8,128)S(1)}, u32[]{:S(2)}, u32[]{:S(2)}) collective-permute-start(f32[8,128]{1,0:T(8,128)S(1)} %get-tuple-element.497), channel_id=1, source_target_pairs={{0,15},{1,0},{2,1},{3,2},{4,3},{5,4},{6,5},{7,6},{8,7},{9,8},{10,9... | collective-permute-start | bytes 12296 | tf_op jit(solution)/shard_map/ppermute | solution.py:335
  34.5 1.5 %shard_map.104.got = f32[3,112,128]{2,1,0:T(8,128)S(1)} custom-call(f32[3,32,128]{2,1,0:T(8,128)S(1)} %get-tuple-element.492.u, s32[112,128]{1,0:T(8,128)S(1)} %get-tuple-element.477.nodes), custom_call_target="tpu_custom_call" | custom-call | flops 20000000 | bytes 1000000 | tf_op jit(solution)/shard_map/pallas_call | solution.py:27
  36.1 0.2 collective-permute-done.19.b
  36.3 4.6 %shard_map.105 = (f32[48,256]{1,0:T(8,128)S(1)}, f32[12,128]{1,0:T(8,128)S(1)}, f32[8,128]{1,0:T(8,128)S(1)}, f32[8,128]{1,0:T(8,128)S(1)}, f32[8,128]{1,0:T(8,128)S(1)}, /*index=5*/f32[8,128]{1,0:T(8,128)S(1)}) custom-call(s32[5]{0:T(128)S(1)} %stack.71.flags, f32[3,112,128]{2,1,0:T(8,128)S(1)} %shard_map.104.got, s32[112,128]{1,0:T(8,128)S(1)} %get-tuple-element.477.nodes, ...), custom_call_target="tpu_custom_call" | custom-call | flops 2000000 | bytes 1000000 | tf_op jit(solution)/shard_map/pallas_call | solution.py:27
  40.9 0.1 collective-permute-start.20
  41.0 2.3 %collective-permute-start.21 = (f32[8,128]{1,0:T(8,128)S(1)}, f32[8,128]{1,0:T(8,128)S(1)}, u32[]{:S(2)}, u32[]{:S(2)}) collective-permute-start(f32[8,128]{1,0:T(8,128)S(1)} %get-tuple-element.501), channel_id=1, source_target_pairs={{0,240},{16,32},{32,16},{48,64},{64,48},{80,96},{96,80},{112,128},... | collective-permute-start | bytes 12296 | tf_op jit(solution)/shard_map/ppermute | solution.py:333
  43.2 1.7 %collective-permute-start.22 = (f32[8,128]{1,0:T(8,128)S(1)}, f32[8,128]{1,0:T(8,128)S(1)}, u32[]{:S(2)}, u32[]{:S(2)}) collective-permute-start(f32[8,128]{1,0:T(8,128)S(1)} %get-tuple-element.502), channel_id=1, source_target_pairs={{0,1},{1,2},{2,3},{3,4},{4,5},{5,6},{6,7},{7,8},{8,9},{9,10},{10,1... | collective-permute-start | bytes 12296 | tf_op jit(solution)/shard_map/ppermute | solution.py:334
  45.0 1.5 %collective-permute-start.23 = (f32[8,128]{1,0:T(8,128)S(1)}, f32[8,128]{1,0:T(8,128)S(1)}, u32[]{:S(2)}, u32[]{:S(2)}) collective-permute-start(f32[8,128]{1,0:T(8,128)S(1)} %get-tuple-element.503), channel_id=1, source_target_pairs={{0,15},{1,0},{2,1},{3,2},{4,3},{5,4},{6,5},{7,6},{8,7},{9,8},{10,9... | collective-permute-start | bytes 12296 | tf_op jit(solution)/shard_map/ppermute | solution.py:335
  46.5 0.4 collective-permute-done.21.o
  46.9 0.3 collective-permute-done.22.f
  47.1 0.9 collective-permute-done.23.b
  48.0 1.4 %shard_map.106 = (f32[3,32,128]{2,1,0:T(8,128)S(1)}, f32[3,32,128]{2,1,0:T(8,128)S(1)}, f32[32,128]{1,0:T(8,128)S(1)}, f32[8,128]{1,0:T(8,128)S(1)}, f32[8,128]{...) custom-call(s32[5]{0:T(128)S(1)} %stack.71.flags, f32[48,256]{1,0:T(8,128)S(1)} %get-tuple-element.498.part, ...), custom_call_target="tpu_custom_call" | custom-call | flops 2000000 | bytes 1000000 | tf_op jit(solution)/shard_map/pallas_call | solution.py:27
  49.4 0.1 collective-permute-start.24
  49.5 16.3 %collective-permute-start.25 = (f32[8,128]{1,0:T(8,128)S(1)}, f32[8,128]{1,0:T(8,128)S(1)}, u32[]{:S(2)}, u32[]{:S(2)}) collective-permute-start(f32[8,128]{1,0:T(8,128)S(1)} %get-tuple-element.507), channel_id=1, source_target_pairs={{0,240},{16,32},{32,16},{48,64},{64,48},{80,96},{96,80},{112,128},... | collective-permute-start | bytes 12296 | tf_op jit(solution)/shard_map/ppermute | solution.py:333
  65.8 1.8 %collective-permute-start.26 = (f32[8,128]{1,0:T(8,128)S(1)}, f32[8,128]{1,0:T(8,128)S(1)}, u32[]{:S(2)}, u32[]{:S(2)}) collective-permute-start(f32[8,128]{1,0:T(8,128)S(1)} %get-tuple-element.508), channel_id=1, source_target_pairs={{0,1},{1,2},{2,3},{3,4},{4,5},{5,6},{6,7},{7,8},{8,9},{9,10},{10,1... | collective-permute-start | bytes 12296 | tf_op jit(solution)/shard_map/ppermute | solution.py:334
  67.6 1.5 %collective-permute-start.27 = (f32[8,128]{1,0:T(8,128)S(1)}, f32[8,128]{1,0:T(8,128)S(1)}, u32[]{:S(2)}, u32[]{:S(2)}) collective-permute-start(f32[8,128]{1,0:T(8,128)S(1)} %get-tuple-element.509), channel_id=1, source_target_pairs={{0,15},{1,0},{2,1},{3,2},{4,3},{5,4},{6,5},{7,6},{8,7},{9,8},{10,9... | collective-permute-start | bytes 12296 | tf_op jit(solution)/shard_map/ppermute | solution.py:335
  69.1 1.5 %shard_map.107.got = f32[3,112,128]{2,1,0:T(8,128)S(1)} custom-call(f32[3,32,128]{2,1,0:T(8,128)S(1)} %get-tuple-element.504.u, s32[112,128]{1,0:T(8,128)S(1)} %get-tuple-element.477.nodes), custom_call_target="tpu_custom_call" | custom-call | flops 20000000 | bytes 1000000 | tf_op jit(solution)/shard_map/pallas_call | solution.py:27
  70.7 4.6 %shard_map.108 = (f32[48,256]{1,0:T(8,128)S(1)}, f32[12,128]{1,0:T(8,128)S(1)}, f32[8,128]{1,0:T(8,128)S(1)}, f32[8,128]{1,0:T(8,128)S(1)}, f32[8,128]{1,0:T(8,128)S(1)}, /*index=5*/f32[8,128]{1,0:T(8,128)S(1)}) custom-call(s32[5]{0:T(128)S(1)} %stack.71.flags, f32[3,112,128]{2,1,0:T(8,128)S(1)} %shard_map.107.got, s32[112,128]{1,0:T(8,128)S(1)} %get-tuple-element.477.nodes, ...), custom_call_target="tpu_custom_call" | custom-call | flops 2000000 | bytes 1000000 | tf_op jit(solution)/shard_map/pallas_call | solution.py:27
  75.4 2.5 %collective-permute-start.29 = (f32[8,128]{1,0:T(8,128)S(1)}, f32[8,128]{1,0:T(8,128)S(1)}, u32[]{:S(2)}, u32[]{:S(2)}) collective-permute-start(f32[8,128]{1,0:T(8,128)S(1)} %get-tuple-element.512), channel_id=1, source_target_pairs={{0,240},{16,32},{32,16},{48,64},{64,48},{80,96},{96,80},{112,128},... | collective-permute-start | bytes 12296 | tf_op jit(solution)/shard_map/ppermute | solution.py:333
  77.9 1.4 %collective-permute-start.30 = (f32[8,128]{1,0:T(8,128)S(1)}, f32[8,128]{1,0:T(8,128)S(1)}, u32[]{:S(2)}, u32[]{:S(2)}) collective-permute-start(f32[8,128]{1,0:T(8,128)S(1)} %get-tuple-element.513), channel_id=1, source_target_pairs={{0,1},{1,2},{2,3},{3,4},{4,5},{5,6},{6,7},{7,8},{8,9},{9,10},{10,1... | collective-permute-start | bytes 12296 | tf_op jit(solution)/shard_map/ppermute | solution.py:334
  79.3 1.8 %collective-permute-start.31 = (f32[8,128]{1,0:T(8,128)S(1)}, f32[8,128]{1,0:T(8,128)S(1)}, u32[]{:S(2)}, u32[]{:S(2)}) collective-permute-start(f32[8,128]{1,0:T(8,128)S(1)} %get-tuple-element.514), channel_id=1, source_target_pairs={{0,15},{1,0},{2,1},{3,2},{4,3},{5,4},{6,5},{7,6},{8,7},{9,8},{10,9... | collective-permute-start | bytes 12296 | tf_op jit(solution)/shard_map/ppermute | solution.py:335
  81.1 0.2 collective-permute-done.29.o
  81.3 0.5 collective-permute-done.30.f
  81.8 0.6 collective-permute-done.31.b
  82.4 1.0 shard_map.109
  83.4 0.7 broadcast_in_dim.26
  84.1 12.7 %all-to-all-start = ((f32[256,1,128]{2,1,0:T(1,128)}), f32[256,1,128]{2,1,0:T(1,128)S(1)}, u32[]{:S(2)}, u32[]{:S(2)}) async-start(f32[256,1,128]{2,1,0:T(1,128)} %broadcast_in_dim.26), calls=%async_computation | async-start | bytes 262144 | tf_op jit(solution)/shard_map/all_to_all | solution.py:485
  96.8 12.9 %all-to-all-done.sums = f32[256,1,128]{2,1,0:T(1,128)S(1)} async-done(((f32[256,1,128]{2,1,0:T(1,128)}), f32[256,1,128]{2,1,0:T(1,128)S(1)}, u32[]{:S(2)}, u32[]{:S(2)}) %all-to-all-start) | async-done | bytes 131104 | tf_op jit(solution)/shard_map/all_to_all | solution.py:485
  109.7 1.4 %shard_map.110 = (f32[8,128]{1,0:T(8,128)S(1)}, s32[1,1]{1,0:T(1,128)}) custom-call(f32[256,1,128]{2,1,0:T(1,128)S(1)} %all-to-all-done.sums), custom_call_target="tpu_custom_call" | custom-call | flops 2000000 | bytes 1000000 | tf_op jit(solution)/shard_map/pallas_call | solution.py:27
  111.7 0.7 conditional.1
  111.7 0.6 branch_1_fun.1
  (34 shorter events, 0.5 us)
Async XLA Ops:
  0.6 0.8 copy-start.6
  0.7 0.8 copy-start.4
  0.7 0.8 copy-start.2
  0.8 0.7 copy-start.3
  1.5 10.6 %copy-start = (f32[2,81,81]{2,0,1:T(2,128)S(1)}, f32[2,81,81]{2,0,1:T(2,128)}, u32[]{:S(2)}) copy-start(f32[2,81,81]{2,0,1:T(2,128)} %param.28) | copy-start | bytes 157468
  1.5 10.6 %copy-start.1 = (s32[1,1,27,512]{3,1,2,0:T(1,128)S(1)}, s32[1,1,27,512]{3,1,2,0:T(1,128)}, u32[]{:S(2)}) copy-start(s32[1,1,27,512]{3,1,2,0:T(1,128)} %param.26) | copy-start | bytes 165892
  2.9 12.2 %collective-permute-start.8 = (f32[32,128]{1,0:T(8,128)S(1)}, f32[32,128]{1,0:T(8,128)S(1)}, u32[]{:S(2)}, u32[]{:S(2)}) collective-permute-start(f32[32,128]{1,0:T(8,128)S(1)} %get-tuple-element.482), channel_id=1, source_target_pairs={{0,16},{16,0},{32,48},{48,32},{64,80},{80,64},{96,112},{112,96},{1... | collective-permute-start | bytes 49160 | tf_op jit(solution)/shard_map/ppermute | solution.py:332
  5.0 9.2 %collective-permute-start.9 = (f32[8,128]{1,0:T(8,128)S(1)}, f32[8,128]{1,0:T(8,128)S(1)}, u32[]{:S(2)}, u32[]{:S(2)}) collective-permute-start(f32[8,128]{1,0:T(8,128)S(1)} %get-tuple-element.483), channel_id=1, source_target_pairs={{0,240},{16,32},{32,16},{48,64},{64,48},{80,96},{96,80},{112,128},... | collective-permute-start | bytes 12296 | tf_op jit(solution)/shard_map/ppermute | solution.py:333
  9.3 5.0 %collective-permute-start.10 = (f32[8,128]{1,0:T(8,128)S(1)}, f32[8,128]{1,0:T(8,128)S(1)}, u32[]{:S(2)}, u32[]{:S(2)}) collective-permute-start(f32[8,128]{1,0:T(8,128)S(1)} %get-tuple-element.484), channel_id=1, source_target_pairs={{0,1},{1,2},{2,3},{3,4},{4,5},{5,6},{6,7},{7,8},{8,9},{9,10},{10,1... | collective-permute-start | bytes 12296 | tf_op jit(solution)/shard_map/ppermute | solution.py:334
  12.1 3.0 %collective-permute-start.11 = (f32[8,128]{1,0:T(8,128)S(1)}, f32[8,128]{1,0:T(8,128)S(1)}, u32[]{:S(2)}, u32[]{:S(2)}) collective-permute-start(f32[8,128]{1,0:T(8,128)S(1)} %get-tuple-element.485), channel_id=1, source_target_pairs={{0,15},{1,0},{2,1},{3,2},{4,3},{5,4},{6,5},{7,6},{8,7},{9,8},{10,9... | collective-permute-start | bytes 12296 | tf_op jit(solution)/shard_map/ppermute | solution.py:335
  15.1 0.7 copy-start.7
  15.8 12.0 %copy-start.5 = (f32[1,1,9,4096]{3,1,2,0:T(1,128)S(1)}, f32[1,1,9,4096]{3,1,2,0:T(1,128)}, u32[]{:S(2)}) copy-start(f32[1,1,9,4096]{3,1,2,0:T(1,128)} %param.29) | copy-start | bytes 442372
  20.4 4.1 %collective-permute-start.12 = (f32[8,128]{1,0:T(8,128)S(1)}, f32[8,128]{1,0:T(8,128)S(1)}, u32[]{:S(2)}, u32[]{:S(2)}) collective-permute-start(f32[8,128]{1,0:T(8,128)S(1)} %get-tuple-element.488), channel_id=1, source_target_pairs={{0,16},{16,0},{32,48},{48,32},{64,80},{80,64},{96,112},{112,96},{1... | collective-permute-start | bytes 12296 | tf_op jit(solution)/shard_map/ppermute | solution.py:332
  20.5 5.9 %collective-permute-start.13 = (f32[8,128]{1,0:T(8,128)S(1)}, f32[8,128]{1,0:T(8,128)S(1)}, u32[]{:S(2)}, u32[]{:S(2)}) collective-permute-start(f32[8,128]{1,0:T(8,128)S(1)} %get-tuple-element.489), channel_id=1, source_target_pairs={{0,240},{16,32},{32,16},{48,64},{64,48},{80,96},{96,80},{112,128},... | collective-permute-start | bytes 12296 | tf_op jit(solution)/shard_map/ppermute | solution.py:333
  21.4 5.0 %collective-permute-start.14 = (f32[8,128]{1,0:T(8,128)S(1)}, f32[8,128]{1,0:T(8,128)S(1)}, u32[]{:S(2)}, u32[]{:S(2)}) collective-permute-start(f32[8,128]{1,0:T(8,128)S(1)} %get-tuple-element.490), channel_id=1, source_target_pairs={{0,1},{1,2},{2,3},{3,4},{4,5},{5,6},{6,7},{7,8},{8,9},{9,10},{10,1... | collective-permute-start | bytes 12296 | tf_op jit(solution)/shard_map/ppermute | solution.py:334
  24.5 3.3 %collective-permute-start.15 = (f32[8,128]{1,0:T(8,128)S(1)}, f32[8,128]{1,0:T(8,128)S(1)}, u32[]{:S(2)}, u32[]{:S(2)}) collective-permute-start(f32[8,128]{1,0:T(8,128)S(1)} %get-tuple-element.491), channel_id=1, source_target_pairs={{0,15},{1,0},{2,1},{3,2},{4,3},{5,4},{6,5},{7,6},{8,7},{9,8},{10,9... | collective-permute-start | bytes 12296 | tf_op jit(solution)/shard_map/ppermute | solution.py:335
  29.2 7.1 %collective-permute-start.16 = (f32[32,128]{1,0:T(8,128)S(1)}, f32[32,128]{1,0:T(8,128)S(1)}, u32[]{:S(2)}, u32[]{:S(2)}) collective-permute-start(f32[32,128]{1,0:T(8,128)S(1)} %get-tuple-element.494), channel_id=1, source_target_pairs={{0,16},{16,0},{32,48},{48,32},{64,80},{80,64},{96,112},{112,96},{1... | collective-permute-start | bytes 49160 | tf_op jit(solution)/shard_map/ppermute | solution.py:332
  29.3 6.7 %collective-permute-start.17 = (f32[8,128]{1,0:T(8,128)S(1)}, f32[8,128]{1,0:T(8,128)S(1)}, u32[]{:S(2)}, u32[]{:S(2)}) collective-permute-start(f32[8,128]{1,0:T(8,128)S(1)} %get-tuple-element.495), channel_id=1, source_target_pairs={{0,240},{16,32},{32,16},{48,64},{64,48},{80,96},{96,80},{112,128},... | collective-permute-start | bytes 12296 | tf_op jit(solution)/shard_map/ppermute | solution.py:333
  31.8 4.3 %collective-permute-start.18 = (f32[8,128]{1,0:T(8,128)S(1)}, f32[8,128]{1,0:T(8,128)S(1)}, u32[]{:S(2)}, u32[]{:S(2)}) collective-permute-start(f32[8,128]{1,0:T(8,128)S(1)} %get-tuple-element.496), channel_id=1, source_target_pairs={{0,1},{1,2},{2,3},{3,4},{4,5},{5,6},{6,7},{7,8},{8,9},{9,10},{10,1... | collective-permute-start | bytes 12296 | tf_op jit(solution)/shard_map/ppermute | solution.py:334
  33.3 3.0 %collective-permute-start.19 = (f32[8,128]{1,0:T(8,128)S(1)}, f32[8,128]{1,0:T(8,128)S(1)}, u32[]{:S(2)}, u32[]{:S(2)}) collective-permute-start(f32[8,128]{1,0:T(8,128)S(1)} %get-tuple-element.497), channel_id=1, source_target_pairs={{0,15},{1,0},{2,1},{3,2},{4,3},{5,4},{6,5},{7,6},{8,7},{9,8},{10,9... | collective-permute-start | bytes 12296 | tf_op jit(solution)/shard_map/ppermute | solution.py:335
  40.9 5.6 %collective-permute-start.20 = (f32[8,128]{1,0:T(8,128)S(1)}, f32[8,128]{1,0:T(8,128)S(1)}, u32[]{:S(2)}, u32[]{:S(2)}) collective-permute-start(f32[8,128]{1,0:T(8,128)S(1)} %get-tuple-element.500), channel_id=1, source_target_pairs={{0,16},{16,0},{32,48},{48,32},{64,80},{80,64},{96,112},{112,96},{1... | collective-permute-start | bytes 12296 | tf_op jit(solution)/shard_map/ppermute | solution.py:332
  41.0 5.9 %collective-permute-start.21 = (f32[8,128]{1,0:T(8,128)S(1)}, f32[8,128]{1,0:T(8,128)S(1)}, u32[]{:S(2)}, u32[]{:S(2)}) collective-permute-start(f32[8,128]{1,0:T(8,128)S(1)} %get-tuple-element.501), channel_id=1, source_target_pairs={{0,240},{16,32},{32,16},{48,64},{64,48},{80,96},{96,80},{112,128},... | collective-permute-start | bytes 12296 | tf_op jit(solution)/shard_map/ppermute | solution.py:333
  43.2 3.9 %collective-permute-start.22 = (f32[8,128]{1,0:T(8,128)S(1)}, f32[8,128]{1,0:T(8,128)S(1)}, u32[]{:S(2)}, u32[]{:S(2)}) collective-permute-start(f32[8,128]{1,0:T(8,128)S(1)} %get-tuple-element.502), channel_id=1, source_target_pairs={{0,1},{1,2},{2,3},{3,4},{4,5},{5,6},{6,7},{7,8},{8,9},{9,10},{10,1... | collective-permute-start | bytes 12296 | tf_op jit(solution)/shard_map/ppermute | solution.py:334
  45.0 3.0 %collective-permute-start.23 = (f32[8,128]{1,0:T(8,128)S(1)}, f32[8,128]{1,0:T(8,128)S(1)}, u32[]{:S(2)}, u32[]{:S(2)}) collective-permute-start(f32[8,128]{1,0:T(8,128)S(1)} %get-tuple-element.503), channel_id=1, source_target_pairs={{0,15},{1,0},{2,1},{3,2},{4,3},{5,4},{6,5},{7,6},{8,7},{9,8},{10,9... | collective-permute-start | bytes 12296 | tf_op jit(solution)/shard_map/ppermute | solution.py:335
  49.4 21.3 %collective-permute-start.24 = (f32[32,128]{1,0:T(8,128)S(1)}, f32[32,128]{1,0:T(8,128)S(1)}, u32[]{:S(2)}, u32[]{:S(2)}) collective-permute-start(f32[32,128]{1,0:T(8,128)S(1)} %get-tuple-element.506), channel_id=1, source_target_pairs={{0,16},{16,0},{32,48},{48,32},{64,80},{80,64},{96,112},{112,96},{1... | collective-permute-start | bytes 49160 | tf_op jit(solution)/shard_map/ppermute | solution.py:332
  49.5 21.1 %collective-permute-start.25 = (f32[8,128]{1,0:T(8,128)S(1)}, f32[8,128]{1,0:T(8,128)S(1)}, u32[]{:S(2)}, u32[]{:S(2)}) collective-permute-start(f32[8,128]{1,0:T(8,128)S(1)} %get-tuple-element.507), channel_id=1, source_target_pairs={{0,240},{16,32},{32,16},{48,64},{64,48},{80,96},{96,80},{112,128},... | collective-permute-start | bytes 12296 | tf_op jit(solution)/shard_map/ppermute | solution.py:333
  65.8 4.9 %collective-permute-start.26 = (f32[8,128]{1,0:T(8,128)S(1)}, f32[8,128]{1,0:T(8,128)S(1)}, u32[]{:S(2)}, u32[]{:S(2)}) collective-permute-start(f32[8,128]{1,0:T(8,128)S(1)} %get-tuple-element.508), channel_id=1, source_target_pairs={{0,1},{1,2},{2,3},{3,4},{4,5},{5,6},{6,7},{7,8},{8,9},{9,10},{10,1... | collective-permute-start | bytes 12296 | tf_op jit(solution)/shard_map/ppermute | solution.py:334
  67.6 3.1 %collective-permute-start.27 = (f32[8,128]{1,0:T(8,128)S(1)}, f32[8,128]{1,0:T(8,128)S(1)}, u32[]{:S(2)}, u32[]{:S(2)}) collective-permute-start(f32[8,128]{1,0:T(8,128)S(1)} %get-tuple-element.509), channel_id=1, source_target_pairs={{0,15},{1,0},{2,1},{3,2},{4,3},{5,4},{6,5},{7,6},{8,7},{9,8},{10,9... | collective-permute-start | bytes 12296 | tf_op jit(solution)/shard_map/ppermute | solution.py:335
  75.3 5.8 %collective-permute-start.28 = (f32[8,128]{1,0:T(8,128)S(1)}, f32[8,128]{1,0:T(8,128)S(1)}, u32[]{:S(2)}, u32[]{:S(2)}) collective-permute-start(f32[8,128]{1,0:T(8,128)S(1)} %get-tuple-element.511), channel_id=1, source_target_pairs={{0,16},{16,0},{32,48},{48,32},{64,80},{80,64},{96,112},{112,96},{1... | collective-permute-start | bytes 12296 | tf_op jit(solution)/shard_map/ppermute | solution.py:332
  75.4 5.9 %collective-permute-start.29 = (f32[8,128]{1,0:T(8,128)S(1)}, f32[8,128]{1,0:T(8,128)S(1)}, u32[]{:S(2)}, u32[]{:S(2)}) collective-permute-start(f32[8,128]{1,0:T(8,128)S(1)} %get-tuple-element.512), channel_id=1, source_target_pairs={{0,240},{16,32},{32,16},{48,64},{64,48},{80,96},{96,80},{112,128},... | collective-permute-start | bytes 12296 | tf_op jit(solution)/shard_map/ppermute | solution.py:333
  77.9 3.9 %collective-permute-start.30 = (f32[8,128]{1,0:T(8,128)S(1)}, f32[8,128]{1,0:T(8,128)S(1)}, u32[]{:S(2)}, u32[]{:S(2)}) collective-permute-start(f32[8,128]{1,0:T(8,128)S(1)} %get-tuple-element.513), channel_id=1, source_target_pairs={{0,1},{1,2},{2,3},{3,4},{4,5},{5,6},{6,7},{7,8},{8,9},{9,10},{10,1... | collective-permute-start | bytes 12296 | tf_op jit(solution)/shard_map/ppermute | solution.py:334
  79.3 3.0 %collective-permute-start.31 = (f32[8,128]{1,0:T(8,128)S(1)}, f32[8,128]{1,0:T(8,128)S(1)}, u32[]{:S(2)}, u32[]{:S(2)}) collective-permute-start(f32[8,128]{1,0:T(8,128)S(1)} %get-tuple-element.514), channel_id=1, source_target_pairs={{0,15},{1,0},{2,1},{3,2},{4,3},{5,4},{6,5},{7,6},{8,7},{9,8},{10,9... | collective-permute-start | bytes 12296 | tf_op jit(solution)/shard_map/ppermute | solution.py:335
  84.1 25.6 %all-to-all-start = ((f32[256,1,128]{2,1,0:T(1,128)}), f32[256,1,128]{2,1,0:T(1,128)S(1)}, u32[]{:S(2)}, u32[]{:S(2)}) async-start(f32[256,1,128]{2,1,0:T(1,128)} %broadcast_in_dim.26), calls=%async_computation | async-start | bytes 262144 | tf_op jit(solution)/shard_map/all_to_all | solution.py:485

commit v3 on v2

--- a/solution.py
+++ b/solution.py
@@ -9,6 +9,7 @@
 LANES = 128
 ROWS = 32
 PIVOT_MIN = 0.01
+LARGE = 54
 f32, bf16, i32, i16 = jnp.float32, jnp.bfloat16, jnp.int32, jnp.int16
 highest = lax.Precision.HIGHEST
 
@@ -20,7 +21,7 @@
     return jax.ShapeDtypeStruct(dims, f32)
 
 
-def call(kernel, outs, args, scratch=(), smem_first=False, flops=2_000_000):
+def call(kernel, outs, args, scratch=(), smem_first=False, flops=2_000_000, grant=24):
     specs = [VMEM] * len(args)
     if smem_first:
         specs[0] = SMEM
@@ -30,7 +31,7 @@
         in_specs=specs,
         out_specs=[VMEM] * len(outs),
         scratch_shapes=list(scratch),
-        compiler_params=pltpu.CompilerParams(vmem_limit_bytes=32 * 1024 * 1024),
+        compiler_params=pltpu.CompilerParams(vmem_limit_bytes=grant * 1024 * 1024),
         cost_estimate=pl.CostEstimate(flops=flops, bytes_accessed=1_000_000, transcendentals=0),
     )(*args)
 
@@ -86,6 +87,8 @@
     lanes = slice(LANES * chunk, LANES * chunk + LANES)
     for g, part in enumerate(spread(index_row >> 8, values, with_ghost)):
         spreads[16 * g : 16 * g + 16, lanes] = part
+    if hots is None:
+        return
     for g, part in enumerate(one_hot_low(index_row & 255)):
         hots[16 * g : 16 * g + 16, lanes] = part
 
@@ -152,7 +155,8 @@
     send_payloads(flags[0], u, m[...], sf, pay_e, pay_o, pay_f, pay_b, uown)
 
 
-def prepare_kernel(nodes, stiff, nodes_out, stiff_out):
+def prepare_kernel(nodes, stiff, moduli, nodes_out, stiff_out, moduli_out):
+    moduli_out[...] = moduli[...]
     for a in range(27):
         nodes_out[4 * a : 4 * a + 4, :] = nodes[a]
     nodes_out[108:112, :] = jnp.zeros((4, LANES), i32)
@@ -181,8 +185,30 @@
             got[c, 8 * i : 8 * i + 8, :] = acc[c]
 
 
+def columns_kernel(nodes, sf, after, hots, send_hots):
+    low = jnp.concatenate(
+        [nodes[0:108, :], sf[8:16, :], sf[0:8, :], jnp.zeros((4, LANES), i32)], axis=0
+    )
+    low = (low & 255).astype(f32).T
+    lanes = lax.broadcasted_iota(i32, (LANES, 256), 1).astype(f32)
+    for chunk in range(124):
+        column = jnp.broadcast_to(low[:, chunk : chunk + 1], (LANES, 256))
+        made = jnp.where(lanes == column, 1.0, 0.0).astype(bf16)
+        dst, place = (hots, chunk) if chunk < 116 else (send_hots, chunk - 116)
+        dst[LANES * place : LANES * place + LANES, :] = made
+
+
+def late_element_kernel(flags, got, nodes, moduli, stiff, sf, m, uown, e, o, f, b, columns,
+                        part, m_next, pay_e, pay_o, pay_f, pay_b, ghost, full, wide, r, spreads, out):
+    element_kernel(
+        flags, got, nodes, moduli, stiff, sf, m, uown, e, o, f, b,
+        part, m_next, pay_e, pay_o, pay_f, pay_b, ghost, full, wide, r, spreads, None, out, columns,
+    )
+
+
 def element_kernel(flags, got, nodes, moduli, stiff, sf, m, uown, e, o, f, b,
-                   part, m_next, pay_e, pay_o, pay_f, pay_b, ghost, full, wide, r, spreads, hots, out):
+                   part, m_next, pay_e, pay_o, pay_f, pay_b, ghost, full, wide, r, spreads, hots, out,
+                   columns=None):
     sides = from_sides(flags, e, o, f, b)
     for k in range(4):
         for c in range(3):
@@ -222,7 +248,10 @@
         else:
             values = [-e[16 + 4 * c + t : 17 + 4 * c + t, :] for c in range(3)]
         place_chunk(spreads, hots, 108 + t, sf[8 + t : 9 + t, :], values, True)
-    total = scatter_product(spreads, hots)
+    if columns is None:
+        total = scatter_product(spreads, hots)
+    else:
+        total = jnp.dot(spreads[...], columns[...], preferred_element_type=f32)
     part[...] = total[0:48] + total[48:96]
     out[...] = total[96:112] + total[112:128]
     odd = flags[0] == 1
@@ -239,14 +268,17 @@
             pay_f[row, :] = blocks[3]
 
 
-def assemble(flags, part, sf, e, o, f, b, w, spreads, hots):
+def assemble(flags, part, sf, e, o, f, b, w, spreads, hots, send_columns):
     sides = from_sides(flags, e, o, f, b)
     for s in range(4):
         for h in range(2):
             row = 2 * s + h
             values = [sides[s][2 * c + h : 2 * c + h + 1, :] for c in range(3)]
             place_chunk(spreads, hots, row, sf[row : row + 1, :], values, False)
-    total = scatter_product(spreads, hots)
+    if send_columns is None:
+        total = scatter_product(spreads, hots)
+    else:
+        total = jnp.dot(spreads[...], send_columns[...], preferred_element_type=f32)
     total = part[...] + total[0:48] + total[48:96]
     for c in range(3):
         for h in range(2):
@@ -255,15 +287,20 @@
             ]
 
 
-def next_kernel(flags, part, sf, m_next, inv, e, o, f, b, w, u, pay_e, pay_o, pay_f, pay_b, uown,
-                spreads, hots):
-    assemble(flags, part, sf, e, o, f, b, w, spreads, hots)
+def alone_kernel(flags, part, sf, e, o, f, b, w, spreads, hots):
+    assemble(flags, part, sf, e, o, f, b, w, spreads, hots, None)
+
+
+def next_kernel(flags, part, sf, m_next, inv, e, o, f, b, send_columns,
+                w, u, pay_e, pay_o, pay_f, pay_b, uown, spreads):
+    assemble(flags, part, sf, e, o, f, b, w, spreads, None, send_columns)
     apply_blocks(inv, w, u)
     send_payloads(flags[0], u, m_next[...], sf, pay_e, pay_o, pay_f, pay_b, uown)
 
 
-def last_kernel(flags, part, sf, e, o, f, b, w0, w1, w2, m0, m1, m2, m3, sums, w3, spreads, hots):
-    assemble(flags, part, sf, e, o, f, b, w3, spreads, hots)
+def last_kernel(flags, part, sf, e, o, f, b, send_columns, w0, w1, w2, m0, m1, m2, m3,
+                sums, w3, spreads):
+    assemble(flags, part, sf, e, o, f, b, w3, spreads, None, send_columns)
     fields, mults = [w0, w1, w2, w3], [m0, m1, m2, m3]
     lane = lax.broadcasted_iota(i32, (1, LANES), 1)
     row = jnp.zeros((1, LANES), f32)
@@ -280,8 +317,8 @@
     sums[...] = row
 
 
-def solve_kernel(sums, coeffs, good):
-    whole = jnp.sum(sums[:, 0, :], axis=0, keepdims=True)
+def finish_kernel(sums, u0, u1, u2, m0, m1, m2, disp, mult, good):
+    whole = jnp.sum(jnp.sum(sums[...], axis=0), axis=0, keepdims=True)
     gram = {}
     place = 0
     for i in range(4):
@@ -310,12 +347,6 @@
     for i in range(4):
         ok = ok & (gram[i, i] > 1e-25) & (gram[i, i] < 1e37)
     good[...] = jnp.where(ok, 1, 0)
-    lane = lax.broadcasted_iota(i32, (8, LANES), 0)
-    coeffs[...] = jnp.where(lane == 0, coef[0], jnp.where(lane == 1, coef[1], coef[2]))
-
-
-def finish_kernel(coeffs, u0, u1, u2, m0, m1, m2, disp, mult):
-    coef = [coeffs[j : j + 1, :] for j in range(ITERS)]
     for c in range(3):
         disp[c] = coef[0] * u0[c] + coef[1] * u1[c] + coef[2] * u2[c]
         rows = slice(4 * c, 4 * c + 4)
@@ -336,20 +367,21 @@
     )
 
 
-def half_operator(flags, u, m, uown, pays, nodes, moduli, stiff, sf):
+def half_operator(flags, u, m, uown, pays, nodes, moduli, stiff, sf, columns=None):
     came = exchange(*pays)
     (got,) = call(local_kernel, [shape(3, 112, LANES)], [u, nodes], flops=20_000_000)
+    hots = [pltpu.VMEM((256, 116 * LANES), bf16)] if columns is None else []
     part, m_next, *pays = call(
-        element_kernel,
+        element_kernel if columns is None else late_element_kernel,
         [shape(48, 256), shape(12, LANES)] + [shape(8, LANES)] * 4,
-        [flags, got, nodes, moduli, stiff, sf, m, uown, *came],
+        [flags, got, nodes, moduli, stiff, sf, m, uown, *came] + ([] if columns is None else [columns]),
         scratch=[
             pltpu.VMEM((3, 8, LANES), f32),
             pltpu.VMEM((3, 112, LANES), f32),
             pltpu.VMEM((96, 512), f32),
             pltpu.VMEM((96, 512), f32),
             pltpu.VMEM((128, 116 * LANES), bf16),
-            pltpu.VMEM((256, 116 * LANES), bf16),
+            *hots,
             pltpu.VMEM((16, 256), f32),
         ],
         smem_first=True,
@@ -403,51 +435,53 @@
 
 
 def step_by_step(flags, w0, m0, inv, nodes, moduli, stiff, sf):
-    beta = jnp.sqrt(inner((w0, m0), (w0, m0)))
-    basis_w = jnp.zeros((ITERS + 1,) + w0.shape, f32).at[0].set(w0 / beta)
-    basis_m = jnp.zeros((ITERS + 1,) + m0.shape, f32).at[0].set(m0 / beta)
-    solves = jnp.zeros((ITERS,) + w0.shape, f32)
-    entries = jnp.zeros((ITERS, ITERS + 1), f32)
+    def operate(w, m):
+        u, *pays, uown = call(
+            apply_kernel, [shape(3, ROWS, LANES)] + PAYLOADS, [flags, w, m, inv, sf], smem_first=True
+        )
+        part, back, m_next = half_operator(flags, u, m, uown, pays, nodes, moduli, stiff, sf)
+        (w,) = call(
+            alone_kernel, [shape(3, ROWS, LANES)], [flags, part, sf, *back],
+            scratch=SMALL, smem_first=True,
+        )
+        return w, m_next, u
 
     def step(j, state):
         basis_w, basis_m, solves, entries = state
-        m = basis_m[j]
-        u, *pays, uown = call(
-            apply_kernel, [shape(3, ROWS, LANES)] + PAYLOADS,
-            [flags, basis_w[j], m, inv, sf], smem_first=True,
-        )
-        part, back, m_next = half_operator(flags, u, m, uown, pays, nodes, moduli, stiff, sf)
-        w = call(
-            next_kernel, [shape(3, ROWS, LANES)] * 2 + PAYLOADS,
-            [flags, part, sf, m_next, inv, *back], scratch=SMALL, smem_first=True,
-        )[0]
-        column = []
-        for i in range(ITERS):
-            entry = jnp.where(i <= j, inner((w, m_next), (basis_w[i], basis_m[i])), 0.0)
-            w, m_next = w - entry * basis_w[i], m_next - entry * basis_m[i]
-            column.append(entry)
-        norm = jnp.sqrt(inner((w, m_next), (w, m_next)))
-        column = jnp.stack(column + [jnp.zeros_like(norm)])
-        column = jnp.where(jnp.arange(ITERS + 1) == j + 1, norm, column)
+        last = jnp.maximum(j - 1, 0)
+        w, m, u = operate(basis_w[last], basis_m[last])
+        w, m = jnp.where(j == 0, w0, w), jnp.where(j == 0, m0, m)
+
+        def remove(i, inside):
+            w, m, column = inside
+            itself = i == j
+            other_w = jnp.where(itself, w, basis_w[i])
+            other_m = jnp.where(itself, m, basis_m[i])
+            entry = inner((w, m), (other_w, other_m))
+            norm = jnp.sqrt(entry)
+            w = jnp.where(itself, w / norm, w - entry * other_w)
+            m = jnp.where(itself, m / norm, m - entry * other_m)
+            return w, m, column.at[i].set(jnp.where(itself, norm, entry))
+
+        w, m, column = lax.fori_loop(0, j + 1, remove, (w, m, jnp.zeros((ITERS + 1,), f32)))
         return (
-            basis_w.at[j + 1].set(w / norm),
-            basis_m.at[j + 1].set(m_next / norm),
-            solves.at[j].set(u),
-            entries.at[j].set(column),
-        )
-
-    basis_w, basis_m, solves, entries = lax.fori_loop(
-        0, ITERS, step, (basis_w, basis_m, solves, entries)
-    )
-    columns = [[entries[j, i] for i in range(j + 2)] for j in range(ITERS)]
-    coeffs = least_squares(columns, beta)
+            basis_w.at[j].set(w), basis_m.at[j].set(m),
+            solves.at[last].set(u), entries.at[j].set(column),
+        )
+
+    start = (
+        jnp.zeros((ITERS + 1,) + w0.shape, f32), jnp.zeros((ITERS + 1,) + m0.shape, f32),
+        jnp.zeros((ITERS,) + w0.shape, f32), jnp.zeros((ITERS + 1, ITERS + 1), f32),
+    )
+    basis_w, basis_m, solves, entries = lax.fori_loop(0, ITERS + 1, step, start)
+    columns = [[entries[j, i] for i in range(j + 1)] for j in range(1, ITERS + 1)]
+    coeffs = least_squares(columns, entries[0, 0])
     disp = sum(coeffs[j] * solves[j] for j in range(ITERS))
     mult = sum(coeffs[j] * basis_m[j] for j in range(ITERS))
     return disp, mult.reshape(3, 4, LANES)
 
 
 def body(body_force, fault_slip, elem_nodes, moduli, stiff_ref, block_inv, send_nodes, fault_nodes):
-    lame = moduli[0, 0]
     at_x, at_y = lax.axis_index("px"), lax.axis_index("py")
     count_x, count_y = lax.axis_size("px"), lax.axis_size("py")
     flags = jnp.stack(
@@ -460,44 +494,56 @@
         [shape(12, LANES), shape(3, ROWS, LANES), jax.ShapeDtypeStruct((16, LANES), i32)] + PAYLOADS,
         [flags, w0, fault_slip.reshape(3, 4, LANES), inv, send_nodes[0, 0], fault_nodes[0, 0]],
         smem_first=True,
-    )
-    nodes, stiff = call(
+        grant=LARGE,
+    )
+    nodes, stiff, lame = call(
         prepare_kernel,
-        [jax.ShapeDtypeStruct((112, LANES), i32), jax.ShapeDtypeStruct((192, 288), bf16)],
-        [elem_nodes.reshape(27, 4, LANES), stiff_ref.transpose(1, 0, 2)],
-    )
+        [jax.ShapeDtypeStruct((112, LANES), i32), jax.ShapeDtypeStruct((192, 288), bf16), shape(2, 512)],
+        [elem_nodes.reshape(27, 4, LANES), stiff_ref.transpose(1, 0, 2), moduli[0, 0]],
+        grant=LARGE,
+    )
+    columns = None
     fields, mults, solves = [w0], [m0], []
     for j in range(ITERS):
         solves.append(u)
-        part, back, m = half_operator(flags, u, mults[-1], uown, pays, nodes, lame, stiff, sf)
+        part, back, m = half_operator(
+            flags, u, mults[-1], uown, pays, nodes, lame, stiff, sf, columns
+        )
         mults.append(m)
+        if columns is None:
+            columns, send_columns = call(
+                columns_kernel,
+                [
+                    jax.ShapeDtypeStruct((116 * LANES, 256), bf16),
+                    jax.ShapeDtypeStruct((8 * LANES, 256), bf16),
+                ],
+                [nodes, sf, part], flops=20_000_000,
+            )
         if j < ITERS - 1:
             w, u, *pays, uown = call(
                 next_kernel, [shape(3, ROWS, LANES)] * 2 + PAYLOADS,
-                [flags, part, sf, m, inv, *back], scratch=SMALL, smem_first=True,
+                [flags, part, sf, m, inv, *back, send_columns], scratch=SMALL[:1], smem_first=True,
             )
             fields.append(w)
     count = count_x * count_y
     (sums,) = call(
-        last_kernel, [shape(1, LANES)], [flags, part, sf, *back, *fields, *mults],
-        scratch=[pltpu.VMEM((3, ROWS, LANES), f32)] + SMALL, smem_first=True,
+        last_kernel, [shape(1, LANES)], [flags, part, sf, *back, send_columns, *fields, *mults],
+        scratch=[pltpu.VMEM((3, ROWS, LANES), f32)] + SMALL[:1], smem_first=True,
     )
     sums = lax.all_to_all(
         jnp.broadcast_to(sums[None], (count, 1, LANES)), ("px", "py"), 0, 0
     )
-    coeffs, good = call(
-        solve_kernel, [shape(8, LANES), jax.ShapeDtypeStruct((1, 1), i32)], [sums]
-    )
-    disp, mult = lax.cond(
-        good[0, 0] == 1,
-        lambda: tuple(
-            call(
-                finish_kernel,
-                [shape(3, ROWS, LANES), shape(3, 4, LANES)],
-                [coeffs, *solves, *mults[:ITERS]],
-            )
+    disp, mult, good = call(
+        finish_kernel,
+        [shape(3, ROWS, LANES), shape(3, 4, LANES), jax.ShapeDtypeStruct((1, 1), i32)],
+        [sums.reshape(count // 8, 8, LANES), *solves, *mults[:ITERS]],
+    )
+    disp, mult, good = lax.while_loop(
+        lambda state: state[2][0, 0] == 0,
+        lambda state: (
+            *step_by_step(flags, w0, m0, inv, nodes, lame, stiff, sf), jnp.ones((1, 1), i32)
         ),
-        lambda: step_by_step(flags, w0, m0, inv, nodes, lame, stiff, sf),
+        (disp, mult, good),
     )
     return (disp.reshape(body_force.shape), mult.reshape(fault_slip.shape))
 

time: 113 us -> 97.6 us (0.86)
  blocking collectives: 0 us -> 25.8 us
  starting transfers between devices: 62.3 us -> 39 us
  waiting for transfers between devices: 20 us -> 1.69 us
    all_to_all x0 -> x1, blocking collectives: none -> 25.8 us  [body(): lax.all_to_all(jnp.broadcast_to(sums[None], (count, 1, LANES)), ('px', 'p...]
    ppermute x6, starting transfers between devices: 28.6 us -> 15.2 us  [exchange(): lax.ppermute(pay_o, 'px', others)]
    all_to_all x1 -> x0, waiting for transfers between devices: 12.9 us -> none  [body(): lax.all_to_all(jnp.broadcast_to(sums[None], (count, 1, LANES)), ('px', 'p...]
    all_to_all x1 -> x0, starting transfers between devices: 12.7 us -> none  [body(): lax.all_to_all(jnp.broadcast_to(sums[None], (count, 1, LANES)), ('px', 'p...]
    ppermute x6, starting transfers between devices: 6.05 us -> 12.9 us  [exchange(): lax.ppermute(pay_b, 'py', backward)]
    ppermute x6, starting transfers between devices: 12.3 us -> 8.1 us  [exchange(): lax.ppermute(pay_f, 'py', forward)]
    ppermute x6, waiting for transfers between devices: 3.94 us -> 0.35 us  [exchange(): lax.ppermute(pay_b, 'py', backward)]
    ppermute x6, waiting for transfers between devices: 2.4 us -> 0.58 us  [exchange(): lax.ppermute(pay_o, 'px', others)]
  transfers between devices with their start and end apart: 25 -> 24, of which waited for: 11 -> 6; matrix products, arithmetic and copies ran while one was open for 0% -> 0% of each run, Pallas kernels for 5% -> 9%
where the time goes in v3:
time: 97.6 us; the launch traced here: 97.3 us
  starting transfers between devices  39 us (40%)
  Pallas kernels  27.4 us (28%)
  blocking collectives  25.8 us (26%)
  waiting for transfers between devices  1.69 us (2%)
  local copies, waits for them, and re-layouts  1.66 us (2%)
  between operations  1.13 us (1%)
    pallas_call x13, Pallas kernels, call(): pl.pallas_call(kernel, out_shape=outs, in_specs=specs, out_specs=[VMEM] *...  27.4 us
    all_to_all x1, blocking collectives, body(): lax.all_to_all(jnp.broadcast_to(sums[None], (count, 1, LANES)), ('px', 'p...  25.8 us
    ppermute x6, starting transfers between devices, exchange(): lax.ppermute(pay_o, 'px', others)  15.2 us
    ppermute x6, starting transfers between devices, exchange(): lax.ppermute(pay_b, 'py', backward)  12.9 us
    ppermute x6, starting transfers between devices, exchange(): lax.ppermute(pay_f, 'py', forward)  8.1 us
    ppermute x6, starting transfers between devices, exchange(): lax.ppermute(pay_e, 'px', pairs)  2.77 us
  transfers between devices with their start and end apart: 24, of which 6 were waited for; matrix products, arithmetic and copies ran while one was open for 0% of the time, Pallas kernels for 9%

profile of v3, /device:TPU:1, one launch (start us, length us, event | category | flops | bytes accessed | tf_op | source)
XLA Modules:
  0.0 97.3 jit_solution(10088401658012397247)
XLA Ops:
  0.7 0.1 stack.39.flags
  0.7 2.1 %shard_map.95 = (f32[12,128]{1,0:T(8,128)S(1)}, f32[3,32,128]{2,1,0:T(8,128)}, s32[16,128]{1,0:T(8,128)S(1)}, f32[32,128]{1,0:T(8,128)}, f32[8,128]{1,0:T(8,128)...) custom-call(s32[5]{0:T(128)S(1)} %stack.39.flags, f32[3,32,128]{2,1,0:T(8,128)} %bitcast.98, ...), custom_call_target="tpu_custom_call" | custom-call | flops 2000000 | bytes 1000000 | tf_op jit(solution)/shard_map/pallas_call | solution.py:28
  2.8 2.0 %collective-permute-start.8 = (f32[32,128]{1,0:T(8,128)}, f32[32,128]{1,0:T(8,128)S(1)}, u32[]{:S(2)}, u32[]{:S(2)}) collective-permute-start(f32[32,128]{1,0:T(8,128)} %get-tuple-element.567), channel_id=1, source_target_pairs={{0,16},{16,0},{32,48},{48,32},{64,80},{80,64},{96,112},{112,96},{1... | collective-permute-start | bytes 49160 | tf_op jit(solution)/shard_map/ppermute | solution.py:363
  4.9 4.3 %collective-permute-start.9 = (f32[8,128]{1,0:T(8,128)}, f32[8,128]{1,0:T(8,128)S(1)}, u32[]{:S(2)}, u32[]{:S(2)}) collective-permute-start(f32[8,128]{1,0:T(8,128)} %get-tuple-element.568), channel_id=1, source_target_pairs={{0,240},{16,32},{32,16},{48,64},{64,48},{80,96},{96,80},{112,128},... | collective-permute-start | bytes 12296 | tf_op jit(solution)/shard_map/ppermute | solution.py:364
  9.1 2.8 %collective-permute-start.10 = (f32[8,128]{1,0:T(8,128)}, f32[8,128]{1,0:T(8,128)S(1)}, u32[]{:S(2)}, u32[]{:S(2)}) collective-permute-start(f32[8,128]{1,0:T(8,128)} %get-tuple-element.569), channel_id=1, source_target_pairs={{0,1},{1,2},{2,3},{3,4},{4,5},{5,6},{6,7},{7,8},{8,9},{9,10},{10,1... | collective-permute-start | bytes 12296 | tf_op jit(solution)/shard_map/ppermute | solution.py:365
  11.9 1.5 %shard_map.96 = (s32[112,128]{1,0:T(8,128)S(1)}, bf16[192,288]{1,0:T(8,128)(2,1)S(1)}, f32[2,512]{1,0:T(2,128)S(1)}) custom-call(s32[27,4,128]{2,1,0:T(4,128)} %bitcast.102, f32[81,2,81]{2,1,0:T(2,128)} %bitcast.101, f32[2,512]{1,0:T(2,128)} %bitcast.106), custom_call_target="tpu_custom_call" | custom-call | flops 2000000 | bytes 1000000 | tf_op jit(solution)/shard_map/pallas_call | solution.py:28
  13.4 0.8 copy-done
  14.2 1.5 %shard_map.97.got = f32[3,112,128]{2,1,0:T(8,128)S(1)} custom-call(f32[3,32,128]{2,1,0:T(8,128)S(1)} %copy-done, s32[112,128]{1,0:T(8,128)S(1)} %get-tuple-element.991.nodes), custom_call_target="tpu_custom_call" | custom-call | flops 20000000 | bytes 1000000 | tf_op jit(solution)/shard_map/pallas_call | solution.py:28
  15.8 0.7 copy-done.2
  16.5 4.6 %shard_map.98 = (f32[48,256]{1,0:T(8,128)S(1)}, f32[12,128]{1,0:T(8,128)S(1)}, f32[8,128]{1,0:T(8,128)S(1)}, f32[8,128]{1,0:T(8,128)S(1)}, f32[8,128]{1,0:T(8,128)S(1)}, /*index=5*/f32[8,128]{1,0:T(8,128)S(1)}) custom-call(s32[5]{0:T(128)S(1)} %stack.39.flags, f32[3,112,128]{2,1,0:T(8,128)S(1)} %shard_map.97.got, s32[112,128]{1,0:T(8,128)S(1)} %get-tuple-element.991.nodes, ...), custom_call_target="tpu_custom_call" | custom-call | flops 2000000 | bytes 1000000 | tf_op jit(solution)/shard_map/pallas_call | solution.py:28
  21.1 0.1 collective-permute-start.12
  21.2 0.6 collective-permute-start.13
  21.8 2.7 %collective-permute-start.14 = (f32[8,128]{1,0:T(8,128)S(1)}, f32[8,128]{1,0:T(8,128)S(1)}, u32[]{:S(2)}, u32[]{:S(2)}) collective-permute-start(f32[8,128]{1,0:T(8,128)S(1)} %get-tuple-element.575), channel_id=1, source_target_pairs={{0,1},{1,2},{2,3},{3,4},{4,5},{5,6},{6,7},{7,8},{8,9},{9,10},{10,1... | collective-permute-start | bytes 12296 | tf_op jit(solution)/shard_map/ppermute | solution.py:365
  24.5 1.4 %collective-permute-start.15 = (f32[8,128]{1,0:T(8,128)S(1)}, f32[8,128]{1,0:T(8,128)S(1)}, u32[]{:S(2)}, u32[]{:S(2)}) collective-permute-start(f32[8,128]{1,0:T(8,128)S(1)} %get-tuple-element.576), channel_id=1, source_target_pairs={{0,15},{1,0},{2,1},{3,2},{4,3},{5,4},{6,5},{7,6},{8,7},{9,8},{10,9... | collective-permute-start | bytes 12296 | tf_op jit(solution)/shard_map/ppermute | solution.py:366
  25.9 2.5 %shard_map.99 = (bf16[14848,256]{1,0:T(8,128)(2,1)S(1)}, bf16[1024,256]{1,0:T(8,128)(2,1)S(1)}) custom-call(s32[112,128]{1,0:T(8,128)S(1)} %get-tuple-element.991.nodes, s32[16,128]{1,0:T(8,128)S(1)} %get-tuple-element.990.sf, f32[48,256]{1,0:T(8,128)S(1)} %get-tuple-element.571.after.part), custom_call_target="tpu_custom_call" | custom-call | flops 20000000 | bytes 1000000 | tf_op jit(solution)/shard_map/pallas_call | solution.py:28
  28.4 1.6 %shard_map.100 = (f32[3,32,128]{2,1,0:T(8,128)S(1)}, f32[3,32,128]{2,1,0:T(8,128)S(1)}, f32[32,128]{1,0:T(8,128)S(1)}, f32[8,128]{1,0:T(8,128)S(1)}, f32[8,128]{...) custom-call(s32[5]{0:T(128)S(1)} %stack.39.flags, f32[48,256]{1,0:T(8,128)S(1)} %get-tuple-element.571.after.part, ...), custom_call_target="tpu_custom_call" | custom-call | flops 2000000 | bytes 1000000 | tf_op jit(solution)/shard_map/pallas_call | solution.py:28
  30.0 0.4 collective-permute-start.16
  30.4 3.7 %collective-permute-start.17 = (f32[8,128]{1,0:T(8,128)S(1)}, f32[8,128]{1,0:T(8,128)S(1)}, u32[]{:S(2)}, u32[]{:S(2)}) collective-permute-start(f32[8,128]{1,0:T(8,128)S(1)} %get-tuple-element.581), channel_id=1, source_target_pairs={{0,240},{16,32},{32,16},{48,64},{64,48},{80,96},{96,80},{112,128},... | collective-permute-start | bytes 12296 | tf_op jit(solution)/shard_map/ppermute | solution.py:364
  34.1 0.6 collective-permute-start.18
  34.6 2.7 %collective-permute-start.19 = (f32[8,128]{1,0:T(8,128)S(1)}, f32[8,128]{1,0:T(8,128)S(1)}, u32[]{:S(2)}, u32[]{:S(2)}) collective-permute-start(f32[8,128]{1,0:T(8,128)S(1)} %get-tuple-element.583), channel_id=1, source_target_pairs={{0,15},{1,0},{2,1},{3,2},{4,3},{5,4},{6,5},{7,6},{8,7},{9,8},{10,9... | collective-permute-start | bytes 12296 | tf_op jit(solution)/shard_map/ppermute | solution.py:366
  37.3 1.5 %shard_map.101.got = f32[3,112,128]{2,1,0:T(8,128)S(1)} custom-call(f32[3,32,128]{2,1,0:T(8,128)S(1)} %get-tuple-element.578.u.u1, s32[112,128]{1,0:T(8,128)S(1)} %get-tuple-element.991.nodes), custom_call_target="tpu_custom_call" | custom-call | flops 20000000 | bytes 1000000 | tf_op jit(solution)/shard_map/pallas_call | solution.py:28
  38.9 3.5 %shard_map.102 = (f32[48,256]{1,0:T(8,128)S(1)}, f32[12,128]{1,0:T(8,128)S(1)}, f32[8,128]{1,0:T(8,128)S(1)}, f32[8,128]{1,0:T(8,128)S(1)}, f32[8,128]{1,0:T(8,128)S(1)}, /*index=5*/f32[8,128]{1,0:T(8,128)S(1)}) custom-call(s32[5]{0:T(128)S(1)} %stack.39.flags, f32[3,112,128]{2,1,0:T(8,128)S(1)} %shard_map.101.got, s32[112,128]{1,0:T(8,128)S(1)} %get-tuple-element.991.nodes, ...), custom_call_target="tpu_custom_call" | custom-call | flops 2000000 | bytes 1000000 | tf_op jit(solution)/shard_map/pallas_call | solution.py:28
  42.4 0.1 collective-permute-start.20
  42.5 1.4 %collective-permute-start.21 = (f32[8,128]{1,0:T(8,128)S(1)}, f32[8,128]{1,0:T(8,128)S(1)}, u32[]{:S(2)}, u32[]{:S(2)}) collective-permute-start(f32[8,128]{1,0:T(8,128)S(1)} %get-tuple-element.588), channel_id=1, source_target_pairs={{0,240},{16,32},{32,16},{48,64},{64,48},{80,96},{96,80},{112,128},... | collective-permute-start | bytes 12296 | tf_op jit(solution)/shard_map/ppermute | solution.py:364
  44.0 1.3 %collective-permute-start.22 = (f32[8,128]{1,0:T(8,128)S(1)}, f32[8,128]{1,0:T(8,128)S(1)}, u32[]{:S(2)}, u32[]{:S(2)}) collective-permute-start(f32[8,128]{1,0:T(8,128)S(1)} %get-tuple-element.589), channel_id=1, source_target_pairs={{0,1},{1,2},{2,3},{3,4},{4,5},{5,6},{6,7},{7,8},{8,9},{9,10},{10,1... | collective-permute-start | bytes 12296 | tf_op jit(solution)/shard_map/ppermute | solution.py:365
  45.3 2.7 %collective-permute-start.23 = (f32[8,128]{1,0:T(8,128)S(1)}, f32[8,128]{1,0:T(8,128)S(1)}, u32[]{:S(2)}, u32[]{:S(2)}) collective-permute-start(f32[8,128]{1,0:T(8,128)S(1)} %get-tuple-element.590), channel_id=1, source_target_pairs={{0,15},{1,0},{2,1},{3,2},{4,3},{5,4},{6,5},{7,6},{8,7},{9,8},{10,9... | collective-permute-start | bytes 12296 | tf_op jit(solution)/shard_map/ppermute | solution.py:366
  48.0 0.4 collective-permute-done.21.o
  48.4 0.2 collective-permute-done.22.f
  48.6 0.2 collective-permute-done.23.b
  48.8 1.2 %shard_map.103 = (f32[3,32,128]{2,1,0:T(8,128)S(1)}, f32[3,32,128]{2,1,0:T(8,128)S(1)}, f32[32,128]{1,0:T(8,128)S(1)}, f32[8,128]{1,0:T(8,128)S(1)}, f32[8,128]{...) custom-call(s32[5]{0:T(128)S(1)} %stack.39.flags, f32[48,256]{1,0:T(8,128)S(1)} %get-tuple-element.585.part, ...), custom_call_target="tpu_custom_call" | custom-call | flops 2000000 | bytes 1000000 | tf_op jit(solution)/shard_map/pallas_call | solution.py:28
  50.0 0.1 collective-permute-start.24
  50.1 2.7 %collective-permute-start.25 = (f32[8,128]{1,0:T(8,128)S(1)}, f32[8,128]{1,0:T(8,128)S(1)}, u32[]{:S(2)}, u32[]{:S(2)}) collective-permute-start(f32[8,128]{1,0:T(8,128)S(1)} %get-tuple-element.594), channel_id=1, source_target_pairs={{0,240},{16,32},{32,16},{48,64},{64,48},{80,96},{96,80},{112,128},... | collective-permute-start | bytes 12296 | tf_op jit(solution)/shard_map/ppermute | solution.py:364
  52.9 0.8 collective-permute-start.26
  53.7 3.0 %collective-permute-start.27 = (f32[8,128]{1,0:T(8,128)S(1)}, f32[8,128]{1,0:T(8,128)S(1)}, u32[]{:S(2)}, u32[]{:S(2)}) collective-permute-start(f32[8,128]{1,0:T(8,128)S(1)} %get-tuple-element.596), channel_id=1, source_target_pairs={{0,15},{1,0},{2,1},{3,2},{4,3},{5,4},{6,5},{7,6},{8,7},{9,8},{10,9... | collective-permute-start | bytes 12296 | tf_op jit(solution)/shard_map/ppermute | solution.py:366
  56.6 1.5 %shard_map.104.got = f32[3,112,128]{2,1,0:T(8,128)S(1)} custom-call(f32[3,32,128]{2,1,0:T(8,128)S(1)} %get-tuple-element.591.u.u2, s32[112,128]{1,0:T(8,128)S(1)} %get-tuple-element.991.nodes), custom_call_target="tpu_custom_call" | custom-call | flops 20000000 | bytes 1000000 | tf_op jit(solution)/shard_map/pallas_call | solution.py:28
  58.2 3.5 %shard_map.105 = (f32[48,256]{1,0:T(8,128)S(1)}, f32[12,128]{1,0:T(8,128)S(1)}, f32[8,128]{1,0:T(8,128)S(1)}, f32[8,128]{1,0:T(8,128)S(1)}, f32[8,128]{1,0:T(8,128)S(1)}, /*index=5*/f32[8,128]{1,0:T(8,128)S(1)}) custom-call(s32[5]{0:T(128)S(1)} %stack.39.flags, f32[3,112,128]{2,1,0:T(8,128)S(1)} %shard_map.104.got, s32[112,128]{1,0:T(8,128)S(1)} %get-tuple-element.991.nodes, ...), custom_call_target="tpu_custom_call" | custom-call | flops 2000000 | bytes 1000000 | tf_op jit(solution)/shard_map/pallas_call | solution.py:28
  61.7 0.1 collective-permute-start.28
  61.8 2.5 %collective-permute-start.29 = (f32[8,128]{1,0:T(8,128)S(1)}, f32[8,128]{1,0:T(8,128)S(1)}, u32[]{:S(2)}, u32[]{:S(2)}) collective-permute-start(f32[8,128]{1,0:T(8,128)S(1)} %get-tuple-element.599), channel_id=1, source_target_pairs={{0,240},{16,32},{32,16},{48,64},{64,48},{80,96},{96,80},{112,128},... | collective-permute-start | bytes 12296 | tf_op jit(solution)/shard_map/ppermute | solution.py:364
  64.3 0.0 collective-permute-start.30
  64.3 3.2 %collective-permute-start.31 = (f32[8,128]{1,0:T(8,128)S(1)}, f32[8,128]{1,0:T(8,128)S(1)}, u32[]{:S(2)}, u32[]{:S(2)}) collective-permute-start(f32[8,128]{1,0:T(8,128)S(1)} %get-tuple-element.601), channel_id=1, source_target_pairs={{0,15},{1,0},{2,1},{3,2},{4,3},{5,4},{6,5},{7,6},{8,7},{9,8},{10,9... | collective-permute-start | bytes 12296 | tf_op jit(solution)/shard_map/ppermute | solution.py:366
  67.5 0.2 collective-permute-done.29.o
  67.7 0.5 collective-permute-done.30.f
  68.2 0.2 collective-permute-done.31.b
  68.3 0.9 shard_map.106
  69.2 0.1 broadcast_in_dim.18
  69.3 25.8 %all_to_all.5 = f32[256,1,128]{2,1,0:T(1,128)S(1)} all-to-all(f32[256,1,128]{2,1,0:T(1,128)S(1)} %broadcast_in_dim.18), channel_id=1, replica_groups=mesh['px'=16,'py'=16] {'px','py'}, dimensions={0} | all-to-all | bytes 262144 | tf_op jit(solution)/shard_map/all_to_all | solution.py:533
  95.1 1.4 %shard_map.107 = (f32[3,32,128]{2,1,0:T(8,128)}, f32[3,4,128]{2,1,0:T(4,128)}, s32[1,1]{1,0:T(1,128)}) custom-call(f32[32,8,128]{2,1,0:T(8,128)S(1)} %bitcast.92, f32[3,32,128]{2,1,0:T(8,128)S(1)} %copy-done.1, f32[3,32,128]{2,1,0:T(8,128)S(1)} %get-tuple-element.578.u.u1, f32[3,32,128]{2,1,0:T(8,128)S(1)} %get-tuple-element.591.u.u2, ...), custom_call_target="tpu_custom_call" | custom-call | flops 2000000 | bytes 1000000 | tf_op jit(solution)/shard_map/pallas_call | solution.py:28
  96.5 0.6 while.84
  (27 shorter events, 0.1 us)
Async XLA Ops:
  0.6 48.2 %copy-start.3 = (f32[1,1,9,4096]{3,1,2,0:T(1,128)S(1)}, f32[1,1,9,4096]{3,1,2,0:T(1,128)}, u32[]{:S(2)}) copy-start(f32[1,1,9,4096]{3,1,2,0:T(1,128)} %param.29) | copy-start | bytes 442372
  2.8 13.0 %collective-permute-start.8 = (f32[32,128]{1,0:T(8,128)}, f32[32,128]{1,0:T(8,128)S(1)}, u32[]{:S(2)}, u32[]{:S(2)}) collective-permute-start(f32[32,128]{1,0:T(8,128)} %get-tuple-element.567), channel_id=1, source_target_pairs={{0,16},{16,0},{32,48},{48,32},{64,80},{80,64},{96,112},{112,96},{1... | collective-permute-start | bytes 49160 | tf_op jit(solution)/shard_map/ppermute | solution.py:363
  4.9 10.9 %collective-permute-start.9 = (f32[8,128]{1,0:T(8,128)}, f32[8,128]{1,0:T(8,128)S(1)}, u32[]{:S(2)}, u32[]{:S(2)}) collective-permute-start(f32[8,128]{1,0:T(8,128)} %get-tuple-element.568), channel_id=1, source_target_pairs={{0,240},{16,32},{32,16},{48,64},{64,48},{80,96},{96,80},{112,128},... | collective-permute-start | bytes 12296 | tf_op jit(solution)/shard_map/ppermute | solution.py:364
  9.1 6.6 %collective-permute-start.10 = (f32[8,128]{1,0:T(8,128)}, f32[8,128]{1,0:T(8,128)S(1)}, u32[]{:S(2)}, u32[]{:S(2)}) collective-permute-start(f32[8,128]{1,0:T(8,128)} %get-tuple-element.569), channel_id=1, source_target_pairs={{0,1},{1,2},{2,3},{3,4},{4,5},{5,6},{6,7},{7,8},{8,9},{9,10},{10,1... | collective-permute-start | bytes 12296 | tf_op jit(solution)/shard_map/ppermute | solution.py:365
  11.9 3.9 %collective-permute-start.11 = (f32[8,128]{1,0:T(8,128)}, f32[8,128]{1,0:T(8,128)S(1)}, u32[]{:S(2)}, u32[]{:S(2)}) collective-permute-start(f32[8,128]{1,0:T(8,128)} %get-tuple-element.570), channel_id=1, source_target_pairs={{0,15},{1,0},{2,1},{3,2},{4,3},{5,4},{6,5},{7,6},{8,7},{9,8},{10,9... | collective-permute-start | bytes 12296 | tf_op jit(solution)/shard_map/ppermute | solution.py:366
  13.4 0.8 copy-start
  15.8 0.7 copy-start.2
  21.1 7.3 %collective-permute-start.12 = (f32[8,128]{1,0:T(8,128)S(1)}, f32[8,128]{1,0:T(8,128)S(1)}, u32[]{:S(2)}, u32[]{:S(2)}) collective-permute-start(f32[8,128]{1,0:T(8,128)S(1)} %get-tuple-element.573), channel_id=1, source_target_pairs={{0,16},{16,0},{32,48},{48,32},{64,80},{80,64},{96,112},{112,96},{1... | collective-permute-start | bytes 12296 | tf_op jit(solution)/shard_map/ppermute | solution.py:363
  21.2 7.2 %collective-permute-start.13 = (f32[8,128]{1,0:T(8,128)S(1)}, f32[8,128]{1,0:T(8,128)S(1)}, u32[]{:S(2)}, u32[]{:S(2)}) collective-permute-start(f32[8,128]{1,0:T(8,128)S(1)} %get-tuple-element.574), channel_id=1, source_target_pairs={{0,240},{16,32},{32,16},{48,64},{64,48},{80,96},{96,80},{112,128},... | collective-permute-start | bytes 12296 | tf_op jit(solution)/shard_map/ppermute | solution.py:364
  21.8 6.6 %collective-permute-start.14 = (f32[8,128]{1,0:T(8,128)S(1)}, f32[8,128]{1,0:T(8,128)S(1)}, u32[]{:S(2)}, u32[]{:S(2)}) collective-permute-start(f32[8,128]{1,0:T(8,128)S(1)} %get-tuple-element.575), channel_id=1, source_target_pairs={{0,1},{1,2},{2,3},{3,4},{4,5},{5,6},{6,7},{7,8},{8,9},{9,10},{10,1... | collective-permute-start | bytes 12296 | tf_op jit(solution)/shard_map/ppermute | solution.py:365
  24.5 3.9 %collective-permute-start.15 = (f32[8,128]{1,0:T(8,128)S(1)}, f32[8,128]{1,0:T(8,128)S(1)}, u32[]{:S(2)}, u32[]{:S(2)}) collective-permute-start(f32[8,128]{1,0:T(8,128)S(1)} %get-tuple-element.576), channel_id=1, source_target_pairs={{0,15},{1,0},{2,1},{3,2},{4,3},{5,4},{6,5},{7,6},{8,7},{9,8},{10,9... | collective-permute-start | bytes 12296 | tf_op jit(solution)/shard_map/ppermute | solution.py:366
  30.0 8.9 %collective-permute-start.16 = (f32[32,128]{1,0:T(8,128)S(1)}, f32[32,128]{1,0:T(8,128)S(1)}, u32[]{:S(2)}, u32[]{:S(2)}) collective-permute-start(f32[32,128]{1,0:T(8,128)S(1)} %get-tuple-element.580), channel_id=1, source_target_pairs={{0,16},{16,0},{32,48},{48,32},{64,80},{80,64},{96,112},{112,96},{1... | collective-permute-start | bytes 49160 | tf_op jit(solution)/shard_map/ppermute | solution.py:363
  30.4 8.5 %collective-permute-start.17 = (f32[8,128]{1,0:T(8,128)S(1)}, f32[8,128]{1,0:T(8,128)S(1)}, u32[]{:S(2)}, u32[]{:S(2)}) collective-permute-start(f32[8,128]{1,0:T(8,128)S(1)} %get-tuple-element.581), channel_id=1, source_target_pairs={{0,240},{16,32},{32,16},{48,64},{64,48},{80,96},{96,80},{112,128},... | collective-permute-start | bytes 12296 | tf_op jit(solution)/shard_map/ppermute | solution.py:364
  34.1 4.8 %collective-permute-start.18 = (f32[8,128]{1,0:T(8,128)S(1)}, f32[8,128]{1,0:T(8,128)S(1)}, u32[]{:S(2)}, u32[]{:S(2)}) collective-permute-start(f32[8,128]{1,0:T(8,128)S(1)} %get-tuple-element.582), channel_id=1, source_target_pairs={{0,1},{1,2},{2,3},{3,4},{4,5},{5,6},{6,7},{7,8},{8,9},{9,10},{10,1... | collective-permute-start | bytes 12296 | tf_op jit(solution)/shard_map/ppermute | solution.py:365
  34.6 4.2 %collective-permute-start.19 = (f32[8,128]{1,0:T(8,128)S(1)}, f32[8,128]{1,0:T(8,128)S(1)}, u32[]{:S(2)}, u32[]{:S(2)}) collective-permute-start(f32[8,128]{1,0:T(8,128)S(1)} %get-tuple-element.583), channel_id=1, source_target_pairs={{0,15},{1,0},{2,1},{3,2},{4,3},{5,4},{6,5},{7,6},{8,7},{9,8},{10,9... | collective-permute-start | bytes 12296 | tf_op jit(solution)/shard_map/ppermute | solution.py:366
  38.9 29.4 %copy-start.4 = (f32[1,1,3,4096]{3,1,2,0:T(1,128)S(1)}, f32[1,1,3,4096]{3,1,2,0:T(1,128)}, u32[]{:S(2)}) copy-start(f32[1,1,3,4096]{3,1,2,0:T(1,128)} %param.24) | copy-start | bytes 147460
  38.9 56.2 %copy-start.1 = (f32[3,32,128]{2,1,0:T(8,128)S(1)}, f32[3,32,128]{2,1,0:T(8,128)}, u32[]{:S(2)}) copy-start(f32[3,32,128]{2,1,0:T(8,128)} %get-tuple-element.560.u.u0) | copy-start | bytes 147460
  42.4 5.6 %collective-permute-start.20 = (f32[8,128]{1,0:T(8,128)S(1)}, f32[8,128]{1,0:T(8,128)S(1)}, u32[]{:S(2)}, u32[]{:S(2)}) collective-permute-start(f32[8,128]{1,0:T(8,128)S(1)} %get-tuple-element.587), channel_id=1, source_target_pairs={{0,16},{16,0},{32,48},{48,32},{64,80},{80,64},{96,112},{112,96},{1... | collective-permute-start | bytes 12296 | tf_op jit(solution)/shard_map/ppermute | solution.py:363
  42.5 5.9 %collective-permute-start.21 = (f32[8,128]{1,0:T(8,128)S(1)}, f32[8,128]{1,0:T(8,128)S(1)}, u32[]{:S(2)}, u32[]{:S(2)}) collective-permute-start(f32[8,128]{1,0:T(8,128)S(1)} %get-tuple-element.588), channel_id=1, source_target_pairs={{0,240},{16,32},{32,16},{48,64},{64,48},{80,96},{96,80},{112,128},... | collective-permute-start | bytes 12296 | tf_op jit(solution)/shard_map/ppermute | solution.py:364
  44.0 4.7 %collective-permute-start.22 = (f32[8,128]{1,0:T(8,128)S(1)}, f32[8,128]{1,0:T(8,128)S(1)}, u32[]{:S(2)}, u32[]{:S(2)}) collective-permute-start(f32[8,128]{1,0:T(8,128)S(1)} %get-tuple-element.589), channel_id=1, source_target_pairs={{0,1},{1,2},{2,3},{3,4},{4,5},{5,6},{6,7},{7,8},{8,9},{9,10},{10,1... | collective-permute-start | bytes 12296 | tf_op jit(solution)/shard_map/ppermute | solution.py:365
  45.3 3.5 %collective-permute-start.23 = (f32[8,128]{1,0:T(8,128)S(1)}, f32[8,128]{1,0:T(8,128)S(1)}, u32[]{:S(2)}, u32[]{:S(2)}) collective-permute-start(f32[8,128]{1,0:T(8,128)S(1)} %get-tuple-element.590), channel_id=1, source_target_pairs={{0,15},{1,0},{2,1},{3,2},{4,3},{5,4},{6,5},{7,6},{8,7},{9,8},{10,9... | collective-permute-start | bytes 12296 | tf_op jit(solution)/shard_map/ppermute | solution.py:366
  50.0 8.2 %collective-permute-start.24 = (f32[32,128]{1,0:T(8,128)S(1)}, f32[32,128]{1,0:T(8,128)S(1)}, u32[]{:S(2)}, u32[]{:S(2)}) collective-permute-start(f32[32,128]{1,0:T(8,128)S(1)} %get-tuple-element.593), channel_id=1, source_target_pairs={{0,16},{16,0},{32,48},{48,32},{64,80},{80,64},{96,112},{112,96},{1... | collective-permute-start | bytes 49160 | tf_op jit(solution)/shard_map/ppermute | solution.py:363
  50.1 8.0 %collective-permute-start.25 = (f32[8,128]{1,0:T(8,128)S(1)}, f32[8,128]{1,0:T(8,128)S(1)}, u32[]{:S(2)}, u32[]{:S(2)}) collective-permute-start(f32[8,128]{1,0:T(8,128)S(1)} %get-tuple-element.594), channel_id=1, source_target_pairs={{0,240},{16,32},{32,16},{48,64},{64,48},{80,96},{96,80},{112,128},... | collective-permute-start | bytes 12296 | tf_op jit(solution)/shard_map/ppermute | solution.py:364
  52.9 5.3 %collective-permute-start.26 = (f32[8,128]{1,0:T(8,128)S(1)}, f32[8,128]{1,0:T(8,128)S(1)}, u32[]{:S(2)}, u32[]{:S(2)}) collective-permute-start(f32[8,128]{1,0:T(8,128)S(1)} %get-tuple-element.595), channel_id=1, source_target_pairs={{0,1},{1,2},{2,3},{3,4},{4,5},{5,6},{6,7},{7,8},{8,9},{9,10},{10,1... | collective-permute-start | bytes 12296 | tf_op jit(solution)/shard_map/ppermute | solution.py:365
  53.7 4.5 %collective-permute-start.27 = (f32[8,128]{1,0:T(8,128)S(1)}, f32[8,128]{1,0:T(8,128)S(1)}, u32[]{:S(2)}, u32[]{:S(2)}) collective-permute-start(f32[8,128]{1,0:T(8,128)S(1)} %get-tuple-element.596), channel_id=1, source_target_pairs={{0,15},{1,0},{2,1},{3,2},{4,3},{5,4},{6,5},{7,6},{8,7},{9,8},{10,9... | collective-permute-start | bytes 12296 | tf_op jit(solution)/shard_map/ppermute | solution.py:366
  61.7 5.8 %collective-permute-start.28 = (f32[8,128]{1,0:T(8,128)S(1)}, f32[8,128]{1,0:T(8,128)S(1)}, u32[]{:S(2)}, u32[]{:S(2)}) collective-permute-start(f32[8,128]{1,0:T(8,128)S(1)} %get-tuple-element.598), channel_id=1, source_target_pairs={{0,16},{16,0},{32,48},{48,32},{64,80},{80,64},{96,112},{112,96},{1... | collective-permute-start | bytes 12296 | tf_op jit(solution)/shard_map/ppermute | solution.py:363
  61.8 5.9 %collective-permute-start.29 = (f32[8,128]{1,0:T(8,128)S(1)}, f32[8,128]{1,0:T(8,128)S(1)}, u32[]{:S(2)}, u32[]{:S(2)}) collective-permute-start(f32[8,128]{1,0:T(8,128)S(1)} %get-tuple-element.599), channel_id=1, source_target_pairs={{0,240},{16,32},{32,16},{48,64},{64,48},{80,96},{96,80},{112,128},... | collective-permute-start | bytes 12296 | tf_op jit(solution)/shard_map/ppermute | solution.py:364
  64.3 3.9 %collective-permute-start.30 = (f32[8,128]{1,0:T(8,128)S(1)}, f32[8,128]{1,0:T(8,128)S(1)}, u32[]{:S(2)}, u32[]{:S(2)}) collective-permute-start(f32[8,128]{1,0:T(8,128)S(1)} %get-tuple-element.600), channel_id=1, source_target_pairs={{0,1},{1,2},{2,3},{3,4},{4,5},{5,6},{6,7},{7,8},{8,9},{9,10},{10,1... | collective-permute-start | bytes 12296 | tf_op jit(solution)/shard_map/ppermute | solution.py:365
  64.3 4.1 %collective-permute-start.31 = (f32[8,128]{1,0:T(8,128)S(1)}, f32[8,128]{1,0:T(8,128)S(1)}, u32[]{:S(2)}, u32[]{:S(2)}) collective-permute-start(f32[8,128]{1,0:T(8,128)S(1)} %get-tuple-element.601), channel_id=1, source_target_pairs={{0,15},{1,0},{2,1},{3,2},{4,3},{5,4},{6,5},{7,6},{8,7},{9,8},{10,9... | collective-permute-start | bytes 12296 | tf_op jit(solution)/shard_map/ppermute | solution.py:366
